TPU v7x, 512 devices: a whole 4x4x16 slice. The times are simulated.
512 devices in a mesh: tm: 8 (over x, z_hi), space: 64 (over z_lo, y, core).
Axes of the slice: x: 4, y: 4, z: 16 (z_hi: 2, z_lo: 8; z = z_hi * 8 + z_lo), core: 2. Of those that a mesh axis runs over, the one named last changes fastest.
Arguments:
- initial: float32 [5, 64, 8192], P(None, None, 'space'), may hold values from -6 to 6
- neighbours: int32 [6, 8192], P(None, 'space'), may hold values from 0 to 8191, as said below
- volume_op: float32 [64, 64], replicated, may hold values from -0.75 to 0.75
- lift_op: float32 [64, 96], replicated, may hold values from -0.625 to 0.625
- coarse_volume: float32 [8, 8], replicated, may hold values from -2 to 2
- coarse_lift: float32 [8, 24], replicated, may hold values from -2.25 to 2.25
- mixing: float32 [5, 5], replicated, may hold values from -2.5 to 2.5
- restrict_op: float32 [8, 64], replicated, may hold values from -0.75 to 0.75
- prolong_op: float32 [64, 8], replicated, may hold values from -2 to 2
Outputs:
- slice_ends: float32 [8, 5, 64, 8192], P('tm', None, None, 'space')
Inputs may be any that keep to these rules, and one draw needn't show every extreme that they name: Elements are numbered layer by layer, 64 to a layer; a layer is a periodic 8 x 8 grid in shuffled order; entries 0..3 name the neighbours along x and y in the same layer, entries 4 and 5 the element at the same grid place in the layer below and above, periodic over all layers.
All inputs are finite; a program needn't handle non-finite values.
Results may differ from a plain program's by a relative error of at most 0.0001.
Values sent between devices are 32-bit elements; how exact they have to be, the bound alone decides.
No kernel may reach another device: no remote copies, remote signals or barrier semaphores. Data moves between devices by JAX's collectives and lax.ppermute only.
A program may use at most 64 MiB of HBM per device.

v0:
```python
import jax
import jax.numpy as jnp
from jax import lax
from jax.sharding import PartitionSpec as P

ITERS = 2
LAYER = 64


exact_mode = lax.Precision.HIGHEST
time_step = 0.125


def extended(array, sides, width):
    for axis, dim in sides:
        peers, length = (lax.axis_size(axis), array.shape[dim])
        up = [(i, (i + 1) % peers) for i in range(peers)]
        down = [(j, i) for i, j in up]
        last = lax.slice_in_dim(array, length - width, length, axis=dim)
        leading = lax.slice_in_dim(array, 0, width, axis=dim)
        before = lax.ppermute(last, axis, up)
        after = lax.ppermute(leading, axis, down)
        array = jnp.concatenate([before, array, after], axis=dim)
    return array


def passed_along(block, axis, distance):
    devices = range(lax.axis_size(axis))
    route = [((i - distance) % len(devices), i) for i in devices]
    return lax.ppermute(block, axis, route)


def from_behind(value, axis, steps):
    count = lax.axis_size(axis)
    leading, last = (max(0, -steps), min(count, count - steps))
    return lax.ppermute(value, axis, [(source, source + steps) for source in range(leading, last)])


def traces(state, per_edge):
    leading = state.shape[:-2]
    elements = state.shape[-1]
    cubed = state.reshape(leading + (per_edge, per_edge, per_edge, elements))
    surfaces = [
        cubed[..., per_edge - 1, :, :, :],
        cubed[..., 0, :, :, :],
        cubed[..., :, per_edge - 1, :, :],
        cubed[..., :, 0, :, :],
        cubed[..., :, :, per_edge - 1, :],
        cubed[..., :, :, 0, :],
    ]
    return [surface.reshape(leading + (per_edge * per_edge, elements)) for surface in surfaces]


def apply_nodes(matrix, state):
    return jnp.einsum("ij,...je->...ie", matrix, state, precision=exact_mode)


def assemble(
    state,
    surfaces,
    upper_side,
    upper_base,
    lower_side,
    lower_base,
    index_ext,
    width,
    volume_op,
    lift_op,
    mixing,
):
    pieces = [jnp.take(surfaces[which], index_ext[which] - width, axis=-1) for which in range(4)]
    pieces.append(jnp.take(upper_side, index_ext[4] - upper_base, axis=-1))
    pieces.append(jnp.take(lower_side, index_ext[5] - lower_base, axis=-1))
    stacked = jnp.concatenate(pieces, axis=-2)
    inner = apply_nodes(volume_op, state) + apply_nodes(lift_op, stacked)
    return jnp.einsum("cd,...die->...cie", mixing, inner, precision=exact_mode)


def fine_rate(state, index_ext, width, volume_op, lift_op, mixing):
    surfaces = traces(state, 4)
    paired = jnp.stack([surfaces[4], surfaces[5]])
    grown = extended(paired, (("space", 3),), width)
    upper_side, lower_side = (grown[0], grown[1])
    lower_base = 0
    return assemble(
        state,
        surfaces,
        upper_side,
        0,
        lower_side,
        lower_base,
        index_ext,
        width,
        volume_op,
        lift_op,
        mixing,
    )


def coarse_rate(state, index_ext, width, volume_op, lift_op, mixing):
    surfaces = traces(state, 2)
    below = passed_along(surfaces[4][..., -width:], "space", 1)
    above = passed_along(surfaces[5][..., :width], "space", -1)
    upper_side = jnp.concatenate([below, surfaces[4]], axis=-1)
    lower_side = jnp.concatenate([surfaces[5], above], axis=-1)
    return assemble(
        state,
        surfaces,
        upper_side,
        0,
        lower_side,
        width,
        index_ext,
        width,
        volume_op,
        lift_op,
        mixing,
    )


def coarse_sweep(begin, begin_rate, prev_head, prev_tail, defect):
    return (
        begin
        + time_step * (begin_rate - prev_head)
        + time_step * (prev_head + prev_tail) / 2
        + defect
    )


def on_device(
    initial,
    neighbours,
    volume_op,
    lift_op,
    coarse_volume,
    coarse_lift,
    mixing,
    restrict_op,
    prolong_op,
):
    elements = initial.shape[-1]
    total = elements * lax.axis_size("space")
    place = lax.axis_index("space")
    index_ext = (neighbours - place * elements + LAYER) % total
    first_slice = lax.axis_index("tm") == 0

    def fine(state):
        return fine_rate(state, index_ext, LAYER, volume_op, lift_op, mixing)

    def coarse(state):
        return coarse_rate(state, index_ext, LAYER, coarse_volume, coarse_lift, mixing)

    start_rate = fine(initial)
    head_state = initial
    mid_state = initial
    end_state = initial
    head_rate = start_rate
    mid_rate = start_rate
    end_rate = start_rate
    for step in range(ITERS):
        if step > 0:
            paired = jnp.stack([end_state, end_rate])
            arrived = from_behind(paired, "tm", 1)
            head_state = jnp.where(first_slice, initial, arrived[0])
            head_rate = jnp.where(first_slice, start_rate, arrived[1])
        old_head = apply_nodes(restrict_op, head_state)
        old_tail = apply_nodes(restrict_op, end_state)
        old_head_rate = coarse(old_head)
        old_tail_rate = coarse(old_tail)
        integral = time_step * (head_rate + 4.0 * mid_rate + end_rate) / 6.0
        defect = (
            apply_nodes(restrict_op, integral) - time_step * (old_head_rate + old_tail_rate) / 2
        )

        def relay(turn, begin):
            head = coarse(begin)
            first_tail = coarse_sweep(begin, head, old_head_rate, old_tail_rate, defect)
            first_rate = coarse(first_tail)
            second_tail = coarse_sweep(begin, head, head, first_rate, defect)
            arrived_tail = from_behind(second_tail, "tm", 1)
            return jnp.where(first_slice, old_head, arrived_tail)

        new_head = lax.fori_loop(0, lax.axis_size("tm") - 1, relay, old_head)
        new_head_rate = coarse(new_head)
        first_tail = coarse_sweep(new_head, new_head_rate, old_head_rate, old_tail_rate, defect)
        first_rate = coarse(first_tail)
        new_tail = coarse_sweep(new_head, new_head_rate, new_head_rate, first_rate, defect)
        new_tail_rate = coarse(new_tail)
        delta_head = new_head - old_head
        delta_tail = new_tail - old_tail
        head_state = head_state + apply_nodes(prolong_op, delta_head)
        mid_state = mid_state + apply_nodes(prolong_op, (delta_head + delta_tail) / 2)
        end_state = end_state + apply_nodes(prolong_op, delta_tail)
        rate_head = new_head_rate - old_head_rate
        rate_tail = new_tail_rate - old_tail_rate
        head_rate = head_rate + apply_nodes(prolong_op, rate_head)
        mid_rate = mid_rate + apply_nodes(prolong_op, (rate_head + rate_tail) / 2)
        end_rate = end_rate + apply_nodes(prolong_op, rate_tail)
        fresh_head = fine(head_state)
        fresh_mid = (
            head_state
            + time_step / 2 * (fresh_head - head_rate)
            + time_step * (5.0 * head_rate + 8.0 * mid_rate - end_rate) / 24.0
        )
        fresh_mid_rate = fine(fresh_mid)
        fresh_end = (
            fresh_mid
            + time_step / 2 * (fresh_mid_rate - mid_rate)
            + time_step * (-head_rate + 8.0 * mid_rate + 5.0 * end_rate) / 24.0
        )
        if step + 1 < ITERS:
            end_rate_next = fine(fresh_end)
        else:
            end_rate_next = end_rate
        head_rate, mid_rate, end_rate = (fresh_head, fresh_mid_rate, end_rate_next)
        mid_state, end_state = (fresh_mid, fresh_end)
    return end_state[None]


def solution(mesh):
    return jax.shard_map(
        on_device,
        mesh=mesh,
        in_specs=(P(None, None, "space"), P(None, "space"), P(), P(), P(), P(), P(), P(), P()),
        out_specs=P("tm", None, None, "space"),
        check_vma=False,
    )
```

profile of v0, /device:TPU:2, one launch (start us, length us, event | category | flops | bytes accessed | tf_op | source)
XLA Modules:
  0.0 1181.1 jit_solution(12672524706753834486)
XLA Ops:
  3.1 15.0 %collective-permute-start.13 = (f32[2,5,16,64]{3,2,1,0:T(8,128)S(1)}, f32[2,5,16,64]{3,2,1,0:T(8,128)S(1)}, u32[]{:S(2)}, u32[]{:S(2)}) collective-permute-start(f32[2,5,16,64]{3,2,1,0:T(8,128)S(1)} %get-tuple-element.706), channel_id=1, source_target_pairs={{1,0},{2,1},{3,2},{4,3},{5,4},{6,5},{7,6},{8,7},{9,8},{10,9},{11,1... | collective-permute-start | bytes 122888 | tf_op jit(solution)/shard_map/ppermute | solution.py:22
  20.4 12.4 %collective-permute-start.11 = (f32[5,4,64]{2,1,0:T(4,128)S(1)}, f32[5,4,64]{2,1,0:T(4,128)S(1)}, u32[]{:S(2)}, u32[]{:S(2)}) collective-permute-start(f32[5,4,64]{2,1,0:T(4,128)S(1)} %bitcast.1231), channel_id=1, source_target_pairs={{1,0},{2,1},{3,2},{4,3},{5,4},{6,5},{7,6},{8,7},{9,8},{10,9},{11,1... | collective-permute-start | bytes 15368 | tf_op jit(solution)/shard_map/ppermute | solution.py:30
  52.3 415.0 %while.27 = (s32[]{:T(128)}, f32[5,8,128]{2,0,1:T(8,128)S(1)}, pred[]{:T(512)}, f32[8,8]{1,0:T(8,128)S(1)}, s32[6,128]{1,0:T(8,128)S(1)}, /*index=5*/f32[8,24]{1...) while((s32[]{:T(128)}, f32[5,8,128]{2,0,1:T(8,128)S(1)}, ...), condition=%wide.region_1.0_spmd, body=%wide.region_0.5_spmd.sunk | while | flops 4685954 | bytes 2543366 | solution.py:183
  54.8 12.4 %collective-permute-start.1 = (f32[5,4,64]{2,1,0:T(4,128)S(1)}, f32[5,4,64]{2,1,0:T(4,128)S(1)}, u32[]{:S(2)}, u32[]{:S(2)}) collective-permute-start(f32[5,4,64]{2,1,0:T(4,128)S(1)} %bitcast.1098), channel_id=1, source_target_pairs={{1,0},{2,1},{3,2},{4,3},{5,4},{6,5},{7,6},{8,7},{9,8},{10,9},{11,1... | collective-permute-start | bytes 15368 | tf_op jit(solution)/shard_map/while/body/eval_jaxpr/ppermute | solution.py:30
  77.0 12.4 %collective-permute-start.2 = (f32[5,4,64]{2,1,0:T(4,128)S(1)}, f32[5,4,64]{2,1,0:T(4,128)S(1)}, u32[]{:S(2)}, u32[]{:S(2)}) collective-permute-start(f32[5,4,64]{2,1,0:T(4,128)S(1)} %bitcast.1102), channel_id=1, source_target_pairs={{1,0},{2,1},{3,2},{4,3},{5,4},{6,5},{7,6},{8,7},{9,8},{10,9},{11,1... | collective-permute-start | bytes 15368 | tf_op jit(solution)/shard_map/while/body/eval_jaxpr/ppermute | solution.py:30
  96.6 13.0 %collective-permute-start.4 = (f32[5,8,128]{2,0,1:T(8,128)S(1)}, f32[5,8,128]{2,0,1:T(8,128)S(1)}, u32[]{:S(2)}, u32[]{:S(2)}) collective-permute-start(f32[5,8,128]{2,0,1:T(8,128)S(1)} %fusion.357), channel_id=1, source_target_pairs={{0,64},{64,128},{128,192},{192,256},{256,320},{320,384},{384,448},... | collective-permute-start | bytes 61448 | tf_op jit(solution)/shard_map/while/body/eval_jaxpr/ppermute | solution.py:36
  114.0 12.4 %collective-permute-start.1 = (f32[5,4,64]{2,1,0:T(4,128)S(1)}, f32[5,4,64]{2,1,0:T(4,128)S(1)}, u32[]{:S(2)}, u32[]{:S(2)}) collective-permute-start(f32[5,4,64]{2,1,0:T(4,128)S(1)} %bitcast.1098), channel_id=1, source_target_pairs={{1,0},{2,1},{3,2},{4,3},{5,4},{6,5},{7,6},{8,7},{9,8},{10,9},{11,1... | collective-permute-start | bytes 15368 | tf_op jit(solution)/shard_map/while/body/eval_jaxpr/ppermute | solution.py:30
  136.2 12.4 %collective-permute-start.2 = (f32[5,4,64]{2,1,0:T(4,128)S(1)}, f32[5,4,64]{2,1,0:T(4,128)S(1)}, u32[]{:S(2)}, u32[]{:S(2)}) collective-permute-start(f32[5,4,64]{2,1,0:T(4,128)S(1)} %bitcast.1102), channel_id=1, source_target_pairs={{1,0},{2,1},{3,2},{4,3},{5,4},{6,5},{7,6},{8,7},{9,8},{10,9},{11,1... | collective-permute-start | bytes 15368 | tf_op jit(solution)/shard_map/while/body/eval_jaxpr/ppermute | solution.py:30
  173.2 12.4 %collective-permute-start.1 = (f32[5,4,64]{2,1,0:T(4,128)S(1)}, f32[5,4,64]{2,1,0:T(4,128)S(1)}, u32[]{:S(2)}, u32[]{:S(2)}) collective-permute-start(f32[5,4,64]{2,1,0:T(4,128)S(1)} %bitcast.1098), channel_id=1, source_target_pairs={{1,0},{2,1},{3,2},{4,3},{5,4},{6,5},{7,6},{8,7},{9,8},{10,9},{11,1... | collective-permute-start | bytes 15368 | tf_op jit(solution)/shard_map/while/body/eval_jaxpr/ppermute | solution.py:30
  195.4 12.4 %collective-permute-start.2 = (f32[5,4,64]{2,1,0:T(4,128)S(1)}, f32[5,4,64]{2,1,0:T(4,128)S(1)}, u32[]{:S(2)}, u32[]{:S(2)}) collective-permute-start(f32[5,4,64]{2,1,0:T(4,128)S(1)} %bitcast.1102), channel_id=1, source_target_pairs={{1,0},{2,1},{3,2},{4,3},{5,4},{6,5},{7,6},{8,7},{9,8},{10,9},{11,1... | collective-permute-start | bytes 15368 | tf_op jit(solution)/shard_map/while/body/eval_jaxpr/ppermute | solution.py:30
  232.4 12.4 %collective-permute-start.1 = (f32[5,4,64]{2,1,0:T(4,128)S(1)}, f32[5,4,64]{2,1,0:T(4,128)S(1)}, u32[]{:S(2)}, u32[]{:S(2)}) collective-permute-start(f32[5,4,64]{2,1,0:T(4,128)S(1)} %bitcast.1098), channel_id=1, source_target_pairs={{1,0},{2,1},{3,2},{4,3},{5,4},{6,5},{7,6},{8,7},{9,8},{10,9},{11,1... | collective-permute-start | bytes 15368 | tf_op jit(solution)/shard_map/while/body/eval_jaxpr/ppermute | solution.py:30
  254.6 12.4 %collective-permute-start.2 = (f32[5,4,64]{2,1,0:T(4,128)S(1)}, f32[5,4,64]{2,1,0:T(4,128)S(1)}, u32[]{:S(2)}, u32[]{:S(2)}) collective-permute-start(f32[5,4,64]{2,1,0:T(4,128)S(1)} %bitcast.1102), channel_id=1, source_target_pairs={{1,0},{2,1},{3,2},{4,3},{5,4},{6,5},{7,6},{8,7},{9,8},{10,9},{11,1... | collective-permute-start | bytes 15368 | tf_op jit(solution)/shard_map/while/body/eval_jaxpr/ppermute | solution.py:30
  291.7 12.4 %collective-permute-start.1 = (f32[5,4,64]{2,1,0:T(4,128)S(1)}, f32[5,4,64]{2,1,0:T(4,128)S(1)}, u32[]{:S(2)}, u32[]{:S(2)}) collective-permute-start(f32[5,4,64]{2,1,0:T(4,128)S(1)} %bitcast.1098), channel_id=1, source_target_pairs={{1,0},{2,1},{3,2},{4,3},{5,4},{6,5},{7,6},{8,7},{9,8},{10,9},{11,1... | collective-permute-start | bytes 15368 | tf_op jit(solution)/shard_map/while/body/eval_jaxpr/ppermute | solution.py:30
  313.8 12.4 %collective-permute-start.2 = (f32[5,4,64]{2,1,0:T(4,128)S(1)}, f32[5,4,64]{2,1,0:T(4,128)S(1)}, u32[]{:S(2)}, u32[]{:S(2)}) collective-permute-start(f32[5,4,64]{2,1,0:T(4,128)S(1)} %bitcast.1102), channel_id=1, source_target_pairs={{1,0},{2,1},{3,2},{4,3},{5,4},{6,5},{7,6},{8,7},{9,8},{10,9},{11,1... | collective-permute-start | bytes 15368 | tf_op jit(solution)/shard_map/while/body/eval_jaxpr/ppermute | solution.py:30
  350.9 12.4 %collective-permute-start.1 = (f32[5,4,64]{2,1,0:T(4,128)S(1)}, f32[5,4,64]{2,1,0:T(4,128)S(1)}, u32[]{:S(2)}, u32[]{:S(2)}) collective-permute-start(f32[5,4,64]{2,1,0:T(4,128)S(1)} %bitcast.1098), channel_id=1, source_target_pairs={{1,0},{2,1},{3,2},{4,3},{5,4},{6,5},{7,6},{8,7},{9,8},{10,9},{11,1... | collective-permute-start | bytes 15368 | tf_op jit(solution)/shard_map/while/body/eval_jaxpr/ppermute | solution.py:30
  373.0 12.4 %collective-permute-start.2 = (f32[5,4,64]{2,1,0:T(4,128)S(1)}, f32[5,4,64]{2,1,0:T(4,128)S(1)}, u32[]{:S(2)}, u32[]{:S(2)}) collective-permute-start(f32[5,4,64]{2,1,0:T(4,128)S(1)} %bitcast.1102), channel_id=1, source_target_pairs={{1,0},{2,1},{3,2},{4,3},{5,4},{6,5},{7,6},{8,7},{9,8},{10,9},{11,1... | collective-permute-start | bytes 15368 | tf_op jit(solution)/shard_map/while/body/eval_jaxpr/ppermute | solution.py:30
  410.1 12.4 %collective-permute-start.1 = (f32[5,4,64]{2,1,0:T(4,128)S(1)}, f32[5,4,64]{2,1,0:T(4,128)S(1)}, u32[]{:S(2)}, u32[]{:S(2)}) collective-permute-start(f32[5,4,64]{2,1,0:T(4,128)S(1)} %bitcast.1098), channel_id=1, source_target_pairs={{1,0},{2,1},{3,2},{4,3},{5,4},{6,5},{7,6},{8,7},{9,8},{10,9},{11,1... | collective-permute-start | bytes 15368 | tf_op jit(solution)/shard_map/while/body/eval_jaxpr/ppermute | solution.py:30
  432.2 12.4 %collective-permute-start.2 = (f32[5,4,64]{2,1,0:T(4,128)S(1)}, f32[5,4,64]{2,1,0:T(4,128)S(1)}, u32[]{:S(2)}, u32[]{:S(2)}) collective-permute-start(f32[5,4,64]{2,1,0:T(4,128)S(1)} %bitcast.1102), channel_id=1, source_target_pairs={{1,0},{2,1},{3,2},{4,3},{5,4},{6,5},{7,6},{8,7},{9,8},{10,9},{11,1... | collective-permute-start | bytes 15368 | tf_op jit(solution)/shard_map/while/body/eval_jaxpr/ppermute | solution.py:30
  484.0 12.4 %collective-permute-start.15 = (f32[2,5,16,64]{3,2,1,0:T(8,128)S(1)}, f32[2,5,16,64]{3,2,1,0:T(8,128)S(1)}, u32[]{:S(2)}, u32[]{:S(2)}) collective-permute-start(f32[2,5,16,64]{3,2,1,0:T(8,128)S(1)} %get-tuple-element.704), channel_id=1, source_target_pairs={{1,0},{2,1},{3,2},{4,3},{5,4},{6,5},{7,6},{8,7},{9,8},{10,9},{11,1... | collective-permute-start | bytes 122888 | tf_op jit(solution)/shard_map/ppermute | solution.py:22
  514.7 14.5 %collective-permute-done.18 = f32[5,4,64]{2,1,0:T(4,128)S(1)} collective-permute-done((f32[5,4,64]{2,1,0:T(4,128)S(1)}, f32[5,4,64]{2,1,0:T(4,128)S(1)}, u32[]{:S(2)}, u32[]{:S(2)}) %collective-permute-start.18) | collective-permute-done | bytes 5152 | tf_op jit(solution)/shard_map/ppermute | solution.py:30
  556.8 12.6 %collective-permute-start.23 = (f32[2,5,16,64]{3,2,1,0:T(8,128)S(1)}, f32[2,5,16,64]{3,2,1,0:T(8,128)S(1)}, u32[]{:S(2)}, u32[]{:S(2)}) collective-permute-start(f32[2,5,16,64]{3,2,1,0:T(8,128)S(1)} %get-tuple-element.702), channel_id=1, source_target_pairs={{1,0},{2,1},{3,2},{4,3},{5,4},{6,5},{7,6},{8,7},{9,8},{10,9},{11,1... | collective-permute-start | bytes 122888 | tf_op jit(solution)/shard_map/ppermute | solution.py:22
  584.8 12.4 %collective-permute-start.25 = (f32[2,5,16,64]{3,2,1,0:T(8,128)S(1)}, f32[2,5,16,64]{3,2,1,0:T(8,128)S(1)}, u32[]{:S(2)}, u32[]{:S(2)}) collective-permute-start(f32[2,5,16,64]{3,2,1,0:T(8,128)S(1)} %get-tuple-element.700), channel_id=1, source_target_pairs={{1,0},{2,1},{3,2},{4,3},{5,4},{6,5},{7,6},{8,7},{9,8},{10,9},{11,1... | collective-permute-start | bytes 122888 | tf_op jit(solution)/shard_map/ppermute | solution.py:22
  653.7 414.5 %while.28 = (s32[]{:T(128)}, f32[5,8,128]{2,0,1:T(8,128)S(1)}, pred[]{:T(512)}, f32[8,8]{1,0:T(8,128)S(1)}, s32[6,128]{1,0:T(8,128)S(1)}, /*index=5*/f32[8,24]{1...) while((s32[]{:T(128)}, f32[5,8,128]{2,0,1:T(8,128)S(1)}, ...), condition=%wide.region_3.8_spmd, body=%wide.region_2.7_spmd.sunk | while | flops 4685954 | bytes 2543366 | solution.py:183
  655.7 12.4 %collective-permute-start.6 = (f32[5,4,64]{2,1,0:T(4,128)S(1)}, f32[5,4,64]{2,1,0:T(4,128)S(1)}, u32[]{:S(2)}, u32[]{:S(2)}) collective-permute-start(f32[5,4,64]{2,1,0:T(4,128)S(1)} %bitcast.1100), channel_id=1, source_target_pairs={{1,0},{2,1},{3,2},{4,3},{5,4},{6,5},{7,6},{8,7},{9,8},{10,9},{11,1... | collective-permute-start | bytes 15368 | tf_op jit(solution)/shard_map/while/body/eval_jaxpr/ppermute | solution.py:30
  677.9 12.4 %collective-permute-start.7 = (f32[5,4,64]{2,1,0:T(4,128)S(1)}, f32[5,4,64]{2,1,0:T(4,128)S(1)}, u32[]{:S(2)}, u32[]{:S(2)}) collective-permute-start(f32[5,4,64]{2,1,0:T(4,128)S(1)} %bitcast.1104), channel_id=1, source_target_pairs={{1,0},{2,1},{3,2},{4,3},{5,4},{6,5},{7,6},{8,7},{9,8},{10,9},{11,1... | collective-permute-start | bytes 15368 | tf_op jit(solution)/shard_map/while/body/eval_jaxpr/ppermute | solution.py:30
  715.0 12.4 %collective-permute-start.6 = (f32[5,4,64]{2,1,0:T(4,128)S(1)}, f32[5,4,64]{2,1,0:T(4,128)S(1)}, u32[]{:S(2)}, u32[]{:S(2)}) collective-permute-start(f32[5,4,64]{2,1,0:T(4,128)S(1)} %bitcast.1100), channel_id=1, source_target_pairs={{1,0},{2,1},{3,2},{4,3},{5,4},{6,5},{7,6},{8,7},{9,8},{10,9},{11,1... | collective-permute-start | bytes 15368 | tf_op jit(solution)/shard_map/while/body/eval_jaxpr/ppermute | solution.py:30
  855.5 12.4 %collective-permute-start.7 = (f32[5,4,64]{2,1,0:T(4,128)S(1)}, f32[5,4,64]{2,1,0:T(4,128)S(1)}, u32[]{:S(2)}, u32[]{:S(2)}) collective-permute-start(f32[5,4,64]{2,1,0:T(4,128)S(1)} %bitcast.1104), channel_id=1, source_target_pairs={{1,0},{2,1},{3,2},{4,3},{5,4},{6,5},{7,6},{8,7},{9,8},{10,9},{11,1... | collective-permute-start | bytes 15368 | tf_op jit(solution)/shard_map/while/body/eval_jaxpr/ppermute | solution.py:30
  914.7 12.4 %collective-permute-start.7 = (f32[5,4,64]{2,1,0:T(4,128)S(1)}, f32[5,4,64]{2,1,0:T(4,128)S(1)}, u32[]{:S(2)}, u32[]{:S(2)}) collective-permute-start(f32[5,4,64]{2,1,0:T(4,128)S(1)} %bitcast.1104), channel_id=1, source_target_pairs={{1,0},{2,1},{3,2},{4,3},{5,4},{6,5},{7,6},{8,7},{9,8},{10,9},{11,1... | collective-permute-start | bytes 15368 | tf_op jit(solution)/shard_map/while/body/eval_jaxpr/ppermute | solution.py:30
  951.8 12.4 %collective-permute-start.6 = (f32[5,4,64]{2,1,0:T(4,128)S(1)}, f32[5,4,64]{2,1,0:T(4,128)S(1)}, u32[]{:S(2)}, u32[]{:S(2)}) collective-permute-start(f32[5,4,64]{2,1,0:T(4,128)S(1)} %bitcast.1100), channel_id=1, source_target_pairs={{1,0},{2,1},{3,2},{4,3},{5,4},{6,5},{7,6},{8,7},{9,8},{10,9},{11,1... | collective-permute-start | bytes 15368 | tf_op jit(solution)/shard_map/while/body/eval_jaxpr/ppermute | solution.py:30
  1085.4 12.5 %collective-permute-start.32 = (f32[2,5,16,64]{3,2,1,0:T(8,128)}, f32[2,5,16,64]{3,2,1,0:T(8,128)}, u32[]{:S(2)}, u32[]{:S(2)}) collective-permute-start(f32[2,5,16,64]{3,2,1,0:T(8,128)} %get-tuple-element.698), channel_id=1, source_target_pairs={{1,0},{2,1},{3,2},{4,3},{5,4},{6,5},{7,6},{8,7},{9,8},{10,9},{11,1... | collective-permute-start | bytes 122888 | tf_op jit(solution)/shard_map/ppermute | solution.py:22
  1126.3 12.6 %collective-permute-start.38 = (f32[5,4,64]{2,1,0:T(4,128)S(1)}, f32[5,4,64]{2,1,0:T(4,128)S(1)}, u32[]{:S(2)}, u32[]{:S(2)}) collective-permute-start(f32[5,4,64]{2,1,0:T(4,128)S(1)} %bitcast.1241), channel_id=1, source_target_pairs={{1,0},{2,1},{3,2},{4,3},{5,4},{6,5},{7,6},{8,7},{9,8},{10,9},{11,1... | collective-permute-start | bytes 15368 | tf_op jit(solution)/shard_map/ppermute | solution.py:30
  1157.1 12.4 %collective-permute-start.40 = (f32[2,5,16,64]{3,2,1,0:T(8,128)S(1)}, f32[2,5,16,64]{3,2,1,0:T(8,128)S(1)}, u32[]{:S(2)}, u32[]{:S(2)}) collective-permute-start(f32[2,5,16,64]{3,2,1,0:T(8,128)S(1)} %get-tuple-element.696), channel_id=1, source_target_pairs={{1,0},{2,1},{3,2},{4,3},{5,4},{6,5},{7,6},{8,7},{9,8},{10,9},{11,1... | collective-permute-start | bytes 122888 | tf_op jit(solution)/shard_map/ppermute | solution.py:22
  (1879 shorter events, 792.9 us)
Async XLA Ops:
  1.2 45.9 %collective-permute-start.12 = (f32[2,5,16,64]{3,2,1,0:T(8,128)S(1)}, f32[2,5,16,64]{3,2,1,0:T(8,128)S(1)}, u32[]{:S(2)}, u32[]{:S(2)}) collective-permute-start(f32[2,5,16,64]{3,2,1,0:T(8,128)S(1)} %get-tuple-element.705), channel_id=1, source_target_pairs={{0,1},{1,2},{2,3},{3,4},{4,5},{5,6},{6,7},{7,8},{8,9},{9,10},{10,1... | collective-permute-start | bytes 122888 | tf_op jit(solution)/shard_map/ppermute | solution.py:21
  3.1 44.0 %collective-permute-start.13 = (f32[2,5,16,64]{3,2,1,0:T(8,128)S(1)}, f32[2,5,16,64]{3,2,1,0:T(8,128)S(1)}, u32[]{:S(2)}, u32[]{:S(2)}) collective-permute-start(f32[2,5,16,64]{3,2,1,0:T(8,128)S(1)} %get-tuple-element.706), channel_id=1, source_target_pairs={{1,0},{2,1},{3,2},{4,3},{5,4},{6,5},{7,6},{8,7},{9,8},{10,9},{11,1... | collective-permute-start | bytes 122888 | tf_op jit(solution)/shard_map/ppermute | solution.py:22
  18.5 25.3 %collective-permute-start.10 = (f32[5,4,64]{2,1,0:T(4,128)S(1)}, f32[5,4,64]{2,1,0:T(4,128)S(1)}, u32[]{:S(2)}, u32[]{:S(2)}) collective-permute-start(f32[5,4,64]{2,1,0:T(4,128)S(1)} %slice.1265), channel_id=1, source_target_pairs={{63,0},{0,1},{1,2},{2,3},{3,4},{4,5},{5,6},{6,7},{7,8},{8,9},{9,10... | collective-permute-start | bytes 15368 | tf_op jit(solution)/shard_map/ppermute | solution.py:30
  20.4 24.6 %collective-permute-start.11 = (f32[5,4,64]{2,1,0:T(4,128)S(1)}, f32[5,4,64]{2,1,0:T(4,128)S(1)}, u32[]{:S(2)}, u32[]{:S(2)}) collective-permute-start(f32[5,4,64]{2,1,0:T(4,128)S(1)} %bitcast.1231), channel_id=1, source_target_pairs={{1,0},{2,1},{3,2},{4,3},{5,4},{6,5},{7,6},{8,7},{9,8},{10,9},{11,1... | collective-permute-start | bytes 15368 | tf_op jit(solution)/shard_map/ppermute | solution.py:30
  52.9 19.1 %collective-permute-start = (f32[5,4,64]{2,1,0:T(4,128)S(1)}, f32[5,4,64]{2,1,0:T(4,128)S(1)}, u32[]{:S(2)}, u32[]{:S(2)}) collective-permute-start(f32[5,4,64]{2,1,0:T(4,128)S(1)} %slice.1655), channel_id=1, source_target_pairs={{63,0},{0,1},{1,2},{2,3},{3,4},{4,5},{5,6},{6,7},{7,8},{8,9},{9,10... | collective-permute-start | bytes 15368 | tf_op jit(solution)/shard_map/while/body/eval_jaxpr/ppermute | solution.py:30
  112.1 19.1 %collective-permute-start = (f32[5,4,64]{2,1,0:T(4,128)S(1)}, f32[5,4,64]{2,1,0:T(4,128)S(1)}, u32[]{:S(2)}, u32[]{:S(2)}) collective-permute-start(f32[5,4,64]{2,1,0:T(4,128)S(1)} %slice.1655), channel_id=1, source_target_pairs={{63,0},{0,1},{1,2},{2,3},{3,4},{4,5},{5,6},{6,7},{7,8},{8,9},{9,10... | collective-permute-start | bytes 15368 | tf_op jit(solution)/shard_map/while/body/eval_jaxpr/ppermute | solution.py:30
  171.3 19.1 %collective-permute-start = (f32[5,4,64]{2,1,0:T(4,128)S(1)}, f32[5,4,64]{2,1,0:T(4,128)S(1)}, u32[]{:S(2)}, u32[]{:S(2)}) collective-permute-start(f32[5,4,64]{2,1,0:T(4,128)S(1)} %slice.1655), channel_id=1, source_target_pairs={{63,0},{0,1},{1,2},{2,3},{3,4},{4,5},{5,6},{6,7},{7,8},{8,9},{9,10... | collective-permute-start | bytes 15368 | tf_op jit(solution)/shard_map/while/body/eval_jaxpr/ppermute | solution.py:30
  230.5 19.1 %collective-permute-start = (f32[5,4,64]{2,1,0:T(4,128)S(1)}, f32[5,4,64]{2,1,0:T(4,128)S(1)}, u32[]{:S(2)}, u32[]{:S(2)}) collective-permute-start(f32[5,4,64]{2,1,0:T(4,128)S(1)} %slice.1655), channel_id=1, source_target_pairs={{63,0},{0,1},{1,2},{2,3},{3,4},{4,5},{5,6},{6,7},{7,8},{8,9},{9,10... | collective-permute-start | bytes 15368 | tf_op jit(solution)/shard_map/while/body/eval_jaxpr/ppermute | solution.py:30
  289.7 19.1 %collective-permute-start = (f32[5,4,64]{2,1,0:T(4,128)S(1)}, f32[5,4,64]{2,1,0:T(4,128)S(1)}, u32[]{:S(2)}, u32[]{:S(2)}) collective-permute-start(f32[5,4,64]{2,1,0:T(4,128)S(1)} %slice.1655), channel_id=1, source_target_pairs={{63,0},{0,1},{1,2},{2,3},{3,4},{4,5},{5,6},{6,7},{7,8},{8,9},{9,10... | collective-permute-start | bytes 15368 | tf_op jit(solution)/shard_map/while/body/eval_jaxpr/ppermute | solution.py:30
  348.9 19.1 %collective-permute-start = (f32[5,4,64]{2,1,0:T(4,128)S(1)}, f32[5,4,64]{2,1,0:T(4,128)S(1)}, u32[]{:S(2)}, u32[]{:S(2)}) collective-permute-start(f32[5,4,64]{2,1,0:T(4,128)S(1)} %slice.1655), channel_id=1, source_target_pairs={{63,0},{0,1},{1,2},{2,3},{3,4},{4,5},{5,6},{6,7},{7,8},{8,9},{9,10... | collective-permute-start | bytes 15368 | tf_op jit(solution)/shard_map/while/body/eval_jaxpr/ppermute | solution.py:30
  408.1 19.1 %collective-permute-start = (f32[5,4,64]{2,1,0:T(4,128)S(1)}, f32[5,4,64]{2,1,0:T(4,128)S(1)}, u32[]{:S(2)}, u32[]{:S(2)}) collective-permute-start(f32[5,4,64]{2,1,0:T(4,128)S(1)} %slice.1655), channel_id=1, source_target_pairs={{63,0},{0,1},{1,2},{2,3},{3,4},{4,5},{5,6},{6,7},{7,8},{8,9},{9,10... | collective-permute-start | bytes 15368 | tf_op jit(solution)/shard_map/while/body/eval_jaxpr/ppermute | solution.py:30
  468.6 32.6 %collective-permute-start.17 = (f32[5,4,64]{2,1,0:T(4,128)S(1)}, f32[5,4,64]{2,1,0:T(4,128)S(1)}, u32[]{:S(2)}, u32[]{:S(2)}) collective-permute-start(f32[5,4,64]{2,1,0:T(4,128)S(1)} %bitcast.1237), channel_id=1, source_target_pairs={{1,0},{2,1},{3,2},{4,3},{5,4},{6,5},{7,6},{8,7},{9,8},{10,9},{11,1... | collective-permute-start | bytes 15368 | tf_op jit(solution)/shard_map/ppermute | solution.py:30
  475.6 26.8 %collective-permute-start.16 = (f32[5,4,64]{2,1,0:T(4,128)S(1)}, f32[5,4,64]{2,1,0:T(4,128)S(1)}, u32[]{:S(2)}, u32[]{:S(2)}) collective-permute-start(f32[5,4,64]{2,1,0:T(4,128)S(1)} %slice.1293), channel_id=1, source_target_pairs={{63,0},{0,1},{1,2},{2,3},{3,4},{4,5},{5,6},{6,7},{7,8},{8,9},{9,10... | collective-permute-start | bytes 15368 | tf_op jit(solution)/shard_map/ppermute | solution.py:30
  482.1 67.0 %collective-permute-start.14 = (f32[2,5,16,64]{3,2,1,0:T(8,128)S(1)}, f32[2,5,16,64]{3,2,1,0:T(8,128)S(1)}, u32[]{:S(2)}, u32[]{:S(2)}) collective-permute-start(f32[2,5,16,64]{3,2,1,0:T(8,128)S(1)} %get-tuple-element.703), channel_id=1, source_target_pairs={{0,1},{1,2},{2,3},{3,4},{4,5},{5,6},{6,7},{7,8},{8,9},{9,10},{10,1... | collective-permute-start | bytes 122888 | tf_op jit(solution)/shard_map/ppermute | solution.py:21
  484.0 65.1 %collective-permute-start.15 = (f32[2,5,16,64]{3,2,1,0:T(8,128)S(1)}, f32[2,5,16,64]{3,2,1,0:T(8,128)S(1)}, u32[]{:S(2)}, u32[]{:S(2)}) collective-permute-start(f32[2,5,16,64]{3,2,1,0:T(8,128)S(1)} %get-tuple-element.704), channel_id=1, source_target_pairs={{1,0},{2,1},{3,2},{4,3},{5,4},{6,5},{7,6},{8,7},{9,8},{10,9},{11,1... | collective-permute-start | bytes 122888 | tf_op jit(solution)/shard_map/ppermute | solution.py:22
  506.7 22.5 %collective-permute-start.18 = (f32[5,4,64]{2,1,0:T(4,128)S(1)}, f32[5,4,64]{2,1,0:T(4,128)S(1)}, u32[]{:S(2)}, u32[]{:S(2)}) collective-permute-start(f32[5,4,64]{2,1,0:T(4,128)S(1)} %slice.1301), channel_id=1, source_target_pairs={{63,0},{0,1},{1,2},{2,3},{3,4},{4,5},{5,6},{6,7},{7,8},{8,9},{9,10... | collective-permute-start | bytes 15368 | tf_op jit(solution)/shard_map/ppermute | solution.py:30
  554.9 19.3 %collective-permute-start.22 = (f32[2,5,16,64]{3,2,1,0:T(8,128)S(1)}, f32[2,5,16,64]{3,2,1,0:T(8,128)S(1)}, u32[]{:S(2)}, u32[]{:S(2)}) collective-permute-start(f32[2,5,16,64]{3,2,1,0:T(8,128)S(1)} %get-tuple-element.701), channel_id=1, source_target_pairs={{0,1},{1,2},{2,3},{3,4},{4,5},{5,6},{6,7},{7,8},{8,9},{9,10},{10,1... | collective-permute-start | bytes 122888 | tf_op jit(solution)/shard_map/ppermute | solution.py:21
  582.9 22.0 %collective-permute-start.24 = (f32[2,5,16,64]{3,2,1,0:T(8,128)S(1)}, f32[2,5,16,64]{3,2,1,0:T(8,128)S(1)}, u32[]{:S(2)}, u32[]{:S(2)}) collective-permute-start(f32[2,5,16,64]{3,2,1,0:T(8,128)S(1)} %get-tuple-element.699), channel_id=1, source_target_pairs={{0,1},{1,2},{2,3},{3,4},{4,5},{5,6},{6,7},{7,8},{8,9},{9,10},{10,1... | collective-permute-start | bytes 122888 | tf_op jit(solution)/shard_map/ppermute | solution.py:21
  584.8 20.1 %collective-permute-start.25 = (f32[2,5,16,64]{3,2,1,0:T(8,128)S(1)}, f32[2,5,16,64]{3,2,1,0:T(8,128)S(1)}, u32[]{:S(2)}, u32[]{:S(2)}) collective-permute-start(f32[2,5,16,64]{3,2,1,0:T(8,128)S(1)} %get-tuple-element.700), channel_id=1, source_target_pairs={{1,0},{2,1},{3,2},{4,3},{5,4},{6,5},{7,6},{8,7},{9,8},{10,9},{11,1... | collective-permute-start | bytes 122888 | tf_op jit(solution)/shard_map/ppermute | solution.py:22
  609.1 26.2 %collective-permute-start.26 = (f32[2,5,64,128]{3,1,2,0:T(8,128)S(1)}, f32[2,5,64,128]{3,1,2,0:T(8,128)S(1)}, u32[]{:S(2)}, u32[]{:S(2)}) collective-permute-start(f32[2,5,64,128]{3,1,2,0:T(8,128)S(1)} %pad_maximum_fusion.8), channel_id=1, source_target_pairs={{0,64},{64,128},{128,192},{192,256},{256,320},{320,384},{384,448},... | collective-permute-start | bytes 983048 | tf_op jit(solution)/shard_map/ppermute | solution.py:36
  653.8 19.1 %collective-permute-start.5 = (f32[5,4,64]{2,1,0:T(4,128)S(1)}, f32[5,4,64]{2,1,0:T(4,128)S(1)}, u32[]{:S(2)}, u32[]{:S(2)}) collective-permute-start(f32[5,4,64]{2,1,0:T(4,128)S(1)} %slice.1681), channel_id=1, source_target_pairs={{63,0},{0,1},{1,2},{2,3},{3,4},{4,5},{5,6},{6,7},{7,8},{8,9},{9,10... | collective-permute-start | bytes 15368 | tf_op jit(solution)/shard_map/while/body/eval_jaxpr/ppermute | solution.py:30
  713.0 19.1 %collective-permute-start.5 = (f32[5,4,64]{2,1,0:T(4,128)S(1)}, f32[5,4,64]{2,1,0:T(4,128)S(1)}, u32[]{:S(2)}, u32[]{:S(2)}) collective-permute-start(f32[5,4,64]{2,1,0:T(4,128)S(1)} %slice.1681), channel_id=1, source_target_pairs={{63,0},{0,1},{1,2},{2,3},{3,4},{4,5},{5,6},{6,7},{7,8},{8,9},{9,10... | collective-permute-start | bytes 15368 | tf_op jit(solution)/shard_map/while/body/eval_jaxpr/ppermute | solution.py:30
  772.2 19.1 %collective-permute-start.5 = (f32[5,4,64]{2,1,0:T(4,128)S(1)}, f32[5,4,64]{2,1,0:T(4,128)S(1)}, u32[]{:S(2)}, u32[]{:S(2)}) collective-permute-start(f32[5,4,64]{2,1,0:T(4,128)S(1)} %slice.1681), channel_id=1, source_target_pairs={{63,0},{0,1},{1,2},{2,3},{3,4},{4,5},{5,6},{6,7},{7,8},{8,9},{9,10... | collective-permute-start | bytes 15368 | tf_op jit(solution)/shard_map/while/body/eval_jaxpr/ppermute | solution.py:30
  831.4 19.1 %collective-permute-start.5 = (f32[5,4,64]{2,1,0:T(4,128)S(1)}, f32[5,4,64]{2,1,0:T(4,128)S(1)}, u32[]{:S(2)}, u32[]{:S(2)}) collective-permute-start(f32[5,4,64]{2,1,0:T(4,128)S(1)} %slice.1681), channel_id=1, source_target_pairs={{63,0},{0,1},{1,2},{2,3},{3,4},{4,5},{5,6},{6,7},{7,8},{8,9},{9,10... | collective-permute-start | bytes 15368 | tf_op jit(solution)/shard_map/while/body/eval_jaxpr/ppermute | solution.py:30
  949.9 19.1 %collective-permute-start.5 = (f32[5,4,64]{2,1,0:T(4,128)S(1)}, f32[5,4,64]{2,1,0:T(4,128)S(1)}, u32[]{:S(2)}, u32[]{:S(2)}) collective-permute-start(f32[5,4,64]{2,1,0:T(4,128)S(1)} %slice.1681), channel_id=1, source_target_pairs={{63,0},{0,1},{1,2},{2,3},{3,4},{4,5},{5,6},{6,7},{7,8},{8,9},{9,10... | collective-permute-start | bytes 15368 | tf_op jit(solution)/shard_map/while/body/eval_jaxpr/ppermute | solution.py:30
  1009.1 19.1 %collective-permute-start.5 = (f32[5,4,64]{2,1,0:T(4,128)S(1)}, f32[5,4,64]{2,1,0:T(4,128)S(1)}, u32[]{:S(2)}, u32[]{:S(2)}) collective-permute-start(f32[5,4,64]{2,1,0:T(4,128)S(1)} %slice.1681), channel_id=1, source_target_pairs={{63,0},{0,1},{1,2},{2,3},{3,4},{4,5},{5,6},{6,7},{7,8},{8,9},{9,10... | collective-permute-start | bytes 15368 | tf_op jit(solution)/shard_map/while/body/eval_jaxpr/ppermute | solution.py:30
  1068.9 34.2 %collective-permute-start.34 = (f32[5,4,64]{2,1,0:T(4,128)S(1)}, f32[5,4,64]{2,1,0:T(4,128)S(1)}, u32[]{:S(2)}, u32[]{:S(2)}) collective-permute-start(f32[5,4,64]{2,1,0:T(4,128)S(1)} %bitcast.1239), channel_id=1, source_target_pairs={{1,0},{2,1},{3,2},{4,3},{5,4},{6,5},{7,6},{8,7},{9,8},{10,9},{11,1... | collective-permute-start | bytes 15368 | tf_op jit(solution)/shard_map/ppermute | solution.py:30
  1075.9 28.6 %collective-permute-start.33 = (f32[5,4,64]{2,1,0:T(4,128)S(1)}, f32[5,4,64]{2,1,0:T(4,128)S(1)}, u32[]{:S(2)}, u32[]{:S(2)}) collective-permute-start(f32[5,4,64]{2,1,0:T(4,128)S(1)} %slice.1365), channel_id=1, source_target_pairs={{63,0},{0,1},{1,2},{2,3},{3,4},{4,5},{5,6},{6,7},{7,8},{8,9},{9,10... | collective-permute-start | bytes 15368 | tf_op jit(solution)/shard_map/ppermute | solution.py:30
  1083.5 63.6 %collective-permute-start.31 = (f32[2,5,16,64]{3,2,1,0:T(8,128)}, f32[2,5,16,64]{3,2,1,0:T(8,128)S(1)}, u32[]{:S(2)}, u32[]{:S(2)}) collective-permute-start(f32[2,5,16,64]{3,2,1,0:T(8,128)} %get-tuple-element.697), channel_id=1, source_target_pairs={{0,1},{1,2},{2,3},{3,4},{4,5},{5,6},{6,7},{7,8},{8,9},{9,10},{10,1... | collective-permute-start | bytes 122888 | tf_op jit(solution)/shard_map/ppermute | solution.py:21
  1085.4 61.7 %collective-permute-start.32 = (f32[2,5,16,64]{3,2,1,0:T(8,128)}, f32[2,5,16,64]{3,2,1,0:T(8,128)}, u32[]{:S(2)}, u32[]{:S(2)}) collective-permute-start(f32[2,5,16,64]{3,2,1,0:T(8,128)} %get-tuple-element.698), channel_id=1, source_target_pairs={{1,0},{2,1},{3,2},{4,3},{5,4},{6,5},{7,6},{8,7},{9,8},{10,9},{11,1... | collective-permute-start | bytes 122888 | tf_op jit(solution)/shard_map/ppermute | solution.py:22
  1124.4 19.1 %collective-permute-start.37 = (f32[5,4,64]{2,1,0:T(4,128)S(1)}, f32[5,4,64]{2,1,0:T(4,128)S(1)}, u32[]{:S(2)}, u32[]{:S(2)}) collective-permute-start(f32[5,4,64]{2,1,0:T(4,128)S(1)} %slice.1381), channel_id=1, source_target_pairs={{63,0},{0,1},{1,2},{2,3},{3,4},{4,5},{5,6},{6,7},{7,8},{8,9},{9,10... | collective-permute-start | bytes 15368 | tf_op jit(solution)/shard_map/ppermute | solution.py:30
  1155.2 19.2 %collective-permute-start.39 = (f32[2,5,16,64]{3,2,1,0:T(8,128)}, f32[2,5,16,64]{3,2,1,0:T(8,128)S(1)}, u32[]{:S(2)}, u32[]{:S(2)}) collective-permute-start(f32[2,5,16,64]{3,2,1,0:T(8,128)} %get-tuple-element.695), channel_id=1, source_target_pairs={{0,1},{1,2},{2,3},{3,4},{4,5},{5,6},{6,7},{7,8},{8,9},{9,10},{10,1... | collective-permute-start | bytes 122888 | tf_op jit(solution)/shard_map/ppermute | solution.py:21
  (99 other events, 3927.2 us)
where the time goes:
time: 1190 us; the launch traced here: 1180 us
  starting transfers between devices  686 us (58%)
  local copies, waits for them, and re-layouts  308 us (26%)
  waiting for transfers between devices  133 us (11%)
  matrix products  29.8 us (3%)
  other arithmetic  13 us (1%)
    ppermute x74, starting transfers between devices, passed_along(): return lax.ppermute(block, axis, route)  468 us
    gather x344, local copies, waits for them, and re-layouts, assemble(): jnp.take(surfaces[which], index_ext[which] - width, axis=-1)  148 us
    ppermute x15, starting transfers between devices, from_behind(): lax.ppermute(value, axis, [(source, source + steps) for source in range(l...  129 us
    ppermute x15, waiting for transfers between devices, from_behind(): lax.ppermute(value, axis, [(source, source + steps) for source in range(l...  97.4 us
    ppermute x6, starting transfers between devices, extended(): after = lax.ppermute(leading, axis, down)  77.2 us
    gather x86, local copies, waits for them, and re-layouts, assemble(): pieces.append(jnp.take(lower_side, index_ext[5] - lower_base, axis=-1))  40 us
    gather x86, local copies, waits for them, and re-layouts, assemble(): pieces.append(jnp.take(upper_side, index_ext[4] - upper_base, axis=-1))  39.9 us
    ppermute x74, waiting for transfers between devices, passed_along(): return lax.ppermute(block, axis, route)  35.7 us
  transfers between devices with their start and end apart: 101, of which 20 were waited for; matrix products, arithmetic and copies ran while one was open for 22% of the time, Pallas kernels for 0%

commit v1 on v0

v1 whole, which is shorter than its diff:
```python
import functools

import jax
import jax.numpy as jnp
from jax import lax
from jax.experimental import pallas as pl
from jax.experimental.pallas import tpu as pltpu
from jax.sharding import PartitionSpec as P

LAYER = 64
FIELDS = 5
DT = 0.125
HALF = 0.7071067811865476
EXACT = lax.Precision.HIGHEST
F32 = jnp.float32
VMEM_LIMIT = 48 * 1024 * 1024


def iota(shape, dim):
    return lax.broadcasted_iota(jnp.int32, shape, dim)


def nn(a, b):
    return lax.dot_general(a, b, (((1,), (0,)), ((), ())), precision=EXACT, preferred_element_type=F32)


def nt(a, b):
    return lax.dot_general(a, b, (((1,), (1,)), ((), ())), precision=EXACT, preferred_element_type=F32)


def eighth_cos(turn):
    turn = turn & 7
    diagonal = jnp.where((turn == 1) | (turn == 7), HALF, jnp.where((turn == 3) | (turn == 5), -HALF, 0.0))
    return jnp.where(turn == 0, 1.0, jnp.where(turn == 4, -1.0, diagonal)).astype(F32)


def wave_numbers(unit):
    low = unit - 23
    high = unit - 26
    kx = jnp.where(unit < 24, unit & 7, jnp.where(unit < 27, low, jnp.where(unit < 30, high, 0)))
    ky = jnp.where(unit < 24, 1 + (unit >> 3), jnp.where(unit < 27, 0, jnp.where(unit == 30, 0, 4)))
    paired = jnp.where(unit < 30, 1, 0)
    kx_other = jnp.where(unit < 30, kx, 4)
    return kx, ky, kx_other, ky, paired


def to_modes_kernel(initial_ref, neighbours_ref, sent_ref, basis_ref):
    place = lax.axis_index("space")
    total = lax.axis_size("space") * 2 * LAYER
    base = place * 2 * LAYER
    lane = iota((1, 128), 1)
    upper = lane >= LAYER
    beside = neighbours_ref[...]
    target = iota((128, 128), 0)

    def steps(face):
        one = jnp.where(beside[face : face + 1] - base == target, 1.0, 0.0).astype(jnp.bfloat16)
        two = jnp.dot(one, one, preferred_element_type=F32).astype(jnp.bfloat16)
        four = jnp.dot(two, two, preferred_element_type=F32).astype(jnp.bfloat16)
        return one, two, four

    row = iota((8, 128), 0)
    found = jnp.where((row == 0) & ((iota((8, 128), 1) & (LAYER - 1)) == 0), 1.0, 0.0).astype(F32)
    for part, moves in ((1, steps(0)), (2, steps(2))):
        for power, move in enumerate(moves):
            shifted = jnp.dot(found.astype(jnp.bfloat16), move, preferred_element_type=F32)
            found = found + shifted + jnp.where(row == part, shifted[0:1] * (1 << power), 0.0)
    along_x = found[1:2]
    along_y = found[2:3]

    below = jnp.where(upper, base, (base + total - LAYER) % total)
    hit = beside[4:5] == below
    extra = jnp.zeros((1, 128), F32)
    for slot, (layer_upper, value) in enumerate(
        ((False, along_x), (False, along_y), (True, along_x), (True, along_y))
    ):
        part = jnp.where(hit & (upper == layer_upper), value, 0.0)
        extra = jnp.where(lane == slot, jnp.sum(part, axis=1, keepdims=True), extra)

    mode = iota((LAYER, 128), 0)
    kx, ky, kx_other, ky_other, paired = wave_numbers(mode >> 1)
    second = (mode & 1) == 1
    turns = (
        jnp.where(second, kx_other, kx) * along_x.astype(jnp.int32)
        + jnp.where(second, ky_other, ky) * along_y.astype(jnp.int32)
        + jnp.where(second, 2 * paired, 0)
    )
    basis = eighth_cos(turns)
    basis_ref[...] = basis
    for field in range(FIELDS):
        state = initial_ref[field]
        apart = jnp.concatenate([jnp.where(upper, 0.0, state), jnp.where(upper, state, 0.0)], axis=0)
        sent_ref[:, field * 128 : (field + 1) * 128] = nt(basis, apart)
    sent_ref[:, FIELDS * 128 :] = jnp.broadcast_to(extra, (LAYER, 128))


def from_modes_kernel(modes_ref, basis_ref, out_ref):
    mode = iota((LAYER, 128), 0)
    scale = jnp.where(mode < 60, 2.0 / LAYER, 1.0 / LAYER).astype(F32)
    back = basis_ref[...] * scale
    upper = iota((LAYER, 128), 1) >= LAYER
    for field in range(FIELDS):
        part = jnp.transpose(modes_ref[:, field * 128 : (field + 1) * 128])
        whole = nn(part, back)
        out_ref[0, field] = jnp.where(upper, whole[LAYER:], whole[:LAYER])


def beside_layers(state, from_below):
    even, odd = state[:LAYER], state[LAYER:]
    return jnp.concatenate(
        [
            jnp.where(from_below, pltpu.roll(odd, 1, 0), odd),
            jnp.where(from_below, even, pltpu.roll(even, LAYER - 1, 0)),
        ],
        axis=0,
    )


def face_weights(shape, per_edge, node, weights):
    column = iota(shape, 1)
    face = column // (per_edge * per_edge)
    trace = column % (per_edge * per_edge)
    a, b, c = (node // (per_edge * per_edge), (node // per_edge) % per_edge, node % per_edge)
    first = [a, a, b, b, c, c]
    rest = [b * per_edge + c] * 2 + [a * per_edge + c] * 2 + [a * per_edge + b] * 2
    result = jnp.zeros(shape, F32)
    for which, weight in weights.items():
        edge = per_edge - 1 if which % 2 == 0 else 0
        on = (face == which) & (first[which] == edge) & (rest[which] == trace)
        result = jnp.where(on, weight, result)
    return result


def iterate_kernel(
    slices,
    received_ref,
    volume_ref,
    lift_ref,
    coarse_volume_ref,
    coarse_lift_ref,
    mixing_ref,
    mixing_smem,
    restrict_ref,
    prolong_ref,
    sent_ref,
    fine_op,
    coarse_op,
    restrict_all,
    prolong_all,
    start,
    start_rate,
    before,
    before_rate,
    mid_rate,
    end_rate,
    chain,
    chain_rate,
    ends,
    ends_rate,
    mids,
    ends_coarse_rate,
):
    place = lax.axis_index("space")
    mine = lax.axis_index("tm")
    core = place & 1
    kx, ky, kx_other, ky_other, paired = wave_numbers(place >> 1)
    single = paired == 0

    def turn_cos(first, second, second_half):
        return jnp.where(second_half, eighth_cos(second), eighth_cos(first))

    wide = iota((128, 128), 1)
    tall = iota((128, 128), 0)
    row = iota((128, 96), 0)
    half = row >= 64
    same = (wide >= 64) == (tall >= 64)
    cos_x = turn_cos(kx, kx_other, half)
    cos_y = turn_cos(ky, ky_other, half)
    sin_x = jnp.where(single, 0.0, eighth_cos(kx - 2))
    sin_y = jnp.where(single, 0.0, eighth_cos(ky - 2))
    sign = jnp.where(half, -1.0, 1.0)
    along = face_weights((128, 96), 4, row & 63, {0: cos_x, 1: cos_x, 2: cos_y, 3: cos_y})
    across = face_weights(
        (128, 96), 4, row & 63, {0: -sin_x * sign, 1: sin_x * sign, 2: -sin_y * sign, 3: sin_y * sign}
    )
    ahead = face_weights((128, 96), 4, row & 63, {4: 1.0, 5: 1.0})
    lift2 = jnp.concatenate([lift_ref[...]] * 2, axis=0)
    volume2 = jnp.concatenate([volume_ref[...]] * 2, axis=0)
    twice = jnp.where((iota((128, 64), 0) & 63) == iota((128, 64), 1), 1.0, 0.0).astype(F32)
    fine_op[:128] = jnp.where(same, nt(twice, volume2) + nt(along, lift2), nt(across, lift2))
    fine_op[128:] = jnp.where(same, nt(ahead, lift2), 0.0)

    row = iota((128, 24), 0)
    half = ((row >> 3) & 1) == 1
    cos_x = turn_cos(kx, kx_other, half)
    cos_y = turn_cos(ky, ky_other, half)
    sign = jnp.where(half, -1.0, 1.0)
    along = face_weights((128, 24), 2, row & 7, {0: cos_x, 1: cos_x, 2: cos_y, 3: cos_y})
    across = face_weights(
        (128, 24), 2, row & 7, {0: -sin_x * sign, 1: sin_x * sign, 2: -sin_y * sign, 3: sin_y * sign}
    )
    ahead = face_weights((128, 24), 2, row & 7, {4: 1.0, 5: 1.0})
    node8 = jnp.where((iota((128, 8), 0) & 7) == iota((128, 8), 1), 1.0, 0.0).astype(F32)
    field8 = jnp.where((iota((128, FIELDS), 0) >> 4) == iota((128, FIELDS), 1), 1.0, 0.0).astype(F32)
    same = ((wide >> 3) & 1) == ((tall >> 3) & 1)
    clift = coarse_lift_ref[...]
    coupled = nt(nt(field8, mixing_ref[...]), field8)
    along = nt(nt(node8, coarse_volume_ref[...]) + nt(along, clift), node8)
    across = nt(nt(across, clift), node8)
    ahead = nt(nt(ahead, clift), node8)
    coarse_op[:128] = coupled * jnp.where(same, along, across)
    coarse_op[128:] = coupled * jnp.where(same, ahead, 0.0)

    restricting = nt(twice, nn(node8, restrict_ref[...]))
    prolonging = nt(node8, jnp.concatenate([prolong_ref[...]] * 2, axis=0))
    down = (tall >= 64) == (((wide >> 3) & 1) == 1)
    up = (wide >= 64) == (((tall >> 3) & 1) == 1)
    for field in range(FIELDS):
        restrict_all[field * 128 : (field + 1) * 128] = jnp.where(
            down & ((wide >> 4) == field), restricting, 0.0
        )
        prolong_all[:, field * 128 : (field + 1) * 128] = jnp.where(
            up & ((tall >> 4) == field), prolonging, 0.0
        )

    lane = iota((LAYER, 128), 1)
    fine_below = (lane & 3) == 3
    coarse_below = (lane & 1) == 1
    halved = lane >= 64

    def fields_of(state):
        return [state[field * 128 : (field + 1) * 128] for field in range(FIELDS)]

    def fine(state):
        parts = fields_of(state)
        pieces = []
        for field in range(FIELDS):
            mixed = mixing_smem[field, 0] * parts[0]
            for other in range(1, FIELDS):
                mixed = mixed + mixing_smem[field, other] * parts[other]
            pieces.append(jnp.concatenate([mixed, beside_layers(mixed, fine_below)], axis=1))
        return nn(jnp.concatenate(pieces, axis=0), fine_op[...])

    def coarse(state):
        return nn(jnp.concatenate([state, beside_layers(state, coarse_below)], axis=1), coarse_op[...])

    def restrict(state):
        return nn(jnp.concatenate(fields_of(state), axis=1), restrict_all[...])

    def prolong(state):
        wide_state = nn(state, prolong_all[...])
        return jnp.concatenate(
            [wide_state[:, field * 128 : (field + 1) * 128] for field in range(FIELDS)], axis=0
        )

    shifts = received_ref[:LAYER, FIELDS * 128 :]
    lower_triangle = jnp.where(iota((LAYER, LAYER), 1) < iota((LAYER, LAYER), 0), 1.0, 0.0).astype(F32)
    first_x, first_y = shifts[:, 0:1], shifts[:, 1:2]
    both_x, both_y = first_x + shifts[:, 2:3], first_y + shifts[:, 3:4]
    passed_x = nn(lower_triangle, jnp.broadcast_to(both_x, (LAYER, 128)))
    passed_y = nn(lower_triangle, jnp.broadcast_to(both_y, (LAYER, 128)))
    turning = []
    for add_x, add_y in ((first_x, first_y), (both_x, both_y)):
        shift_x = (passed_x + add_x).astype(jnp.int32)
        shift_y = (passed_y + add_y).astype(jnp.int32)
        turns = jnp.where(halved, kx_other, kx) * shift_x + jnp.where(halved, ky_other, ky) * shift_y
        cos = eighth_cos(turns)
        sin = jnp.where(single, 0.0, eighth_cos(turns - 2))
        turning.append((cos, jnp.where(halved, sin, -sin)))

    for field in range(FIELDS):
        real = received_ref[:LAYER, field * 128 : (field + 1) * 128]
        imaginary = received_ref[LAYER:, field * 128 : (field + 1) * 128]
        even = jnp.where(halved, pltpu.roll(imaginary, 64, 1), real)
        odd = jnp.where(halved, imaginary, pltpu.roll(real, 64, 1))
        for index, value in enumerate((even, odd)):
            cos, sin = turning[index]
            begin = field * 128 + index * LAYER
            start[begin : begin + LAYER] = value * cos + pltpu.roll(value, 64, 1) * sin

    def relay(step, first_part, second_part):
        head, head_rate = chain[step], chain_rate[step]
        tail = head + DT * head_rate + first_part
        tail = head + (DT / 2) * (head_rate + coarse(tail)) + second_part
        chain[step + 1] = tail
        chain_rate[step + 1] = coarse(tail)

    initial = start[...]
    start_rate[...] = fine(initial)
    rate = start_rate[...]
    begin = restrict(initial)
    begin_rate = coarse(begin)
    rate_coarse = restrict(rate)
    tau = DT * rate_coarse - DT * begin_rate
    chain[0] = begin
    chain_rate[0] = begin_rate

    def first_relay(step, carry):
        relay(step, tau, tau)
        return carry

    lax.fori_loop(0, slices, first_relay, 0)

    before[...] = initial
    before_rate[...] = rate
    ends[0] = begin
    ends_rate[0] = rate_coarse
    ends_coarse_rate[0] = begin_rate

    def first_sweep(step, carry):
        head, head_rate, tail_rate = chain[step], chain_rate[step], chain_rate[step + 1]
        state = start[...] + prolong(head - begin)
        push = prolong((DT / 8) * (tail_rate - head_rate))
        state = state + (DT / 2) * fine(state) + push
        middle_rate = fine(state)
        state = state + (DT / 2) * middle_rate + push
        last_rate = fine(state)
        coarse_end = restrict(state)
        ends[step + 1] = coarse_end
        mids[step] = restrict(middle_rate)
        ends_rate[step + 1] = restrict(last_rate)
        ends_coarse_rate[step + 1] = coarse(coarse_end)

        @pl.when(step + 1 == mine)
        def _():
            before[...] = state
            before_rate[...] = last_rate

        @pl.when(step == mine)
        def _():
            mid_rate[...] = middle_rate
            end_rate[...] = last_rate

        return carry

    lax.fori_loop(0, slices, first_sweep, 0)

    def second_relay(step, carry):
        integral = (DT / 6) * (ends_rate[step] + 4.0 * mids[step] + ends_rate[step + 1])
        old_head_rate, old_tail_rate = ends_coarse_rate[step], ends_coarse_rate[step + 1]
        relay(step, integral - DT * old_head_rate, integral - (DT / 2) * (old_head_rate + old_tail_rate))
        return carry

    lax.fori_loop(0, slices, second_relay, 0)

    state = before[...] + prolong(chain[mine] - ends[mine])
    push = prolong(
        (DT / 8)
        * (
            (chain_rate[mine + 1] - ends_coarse_rate[mine + 1])
            - (chain_rate[mine] - ends_coarse_rate[mine])
        )
    )
    head_rate, middle_rate, last_rate = before_rate[...], mid_rate[...], end_rate[...]
    state = (
        state
        + (DT / 2) * fine(state)
        + (DT / 24) * (8.0 * middle_rate - 7.0 * head_rate - last_rate)
        + push
    )
    state = (
        state
        + (DT / 2) * fine(state)
        + (DT / 24) * (5.0 * last_rate - 4.0 * middle_rate - head_rate)
        + push
    )
    for field in range(FIELDS):
        halves = []
        for index in range(2):
            cos, sin = turning[index]
            begin_row = field * 128 + index * LAYER
            value = state[begin_row : begin_row + LAYER]
            halves.append(value * cos - pltpu.roll(value, 64, 1) * sin)
        even, odd = halves
        real = jnp.where(halved, pltpu.roll(odd, 64, 1), even)
        imaginary = jnp.where(halved, odd, pltpu.roll(even, 64, 1))
        sent_ref[:, field * 128 : (field + 1) * 128] = jnp.where(core == 0, real, imaginary)


def on_device(
    initial,
    neighbours,
    volume_op,
    lift_op,
    coarse_volume,
    coarse_lift,
    mixing,
    restrict_op,
    prolong_op,
):
    in_vmem = pl.BlockSpec(memory_space=pltpu.VMEM)
    params = pltpu.CompilerParams(vmem_limit_bytes=VMEM_LIMIT)
    sent, basis = pl.pallas_call(
        to_modes_kernel,
        out_shape=(
            jax.ShapeDtypeStruct((LAYER, (FIELDS + 1) * 128), F32),
            jax.ShapeDtypeStruct((LAYER, 128), F32),
        ),
        in_specs=[in_vmem] * 2,
        out_specs=(in_vmem, in_vmem),
        compiler_params=params,
        name="to_modes",
    )(initial, neighbours)
    arrived = lax.all_to_all(sent[:, None, :], "space", 0, 0, tiled=True)
    pairs = [[i, i + 1] for i in range(0, lax.axis_size("space"), 2)]
    pair = lax.all_gather(arrived, "space", axis_index_groups=pairs)
    received = pair.reshape(2 * LAYER, (FIELDS + 1) * 128)

    slices = lax.axis_size("tm")
    fine_shape = pltpu.VMEM((FIELDS * 128, 128), F32)
    coarse_shape = pltpu.VMEM((slices + 1, 128, 128), F32)
    modes = pl.pallas_call(
        functools.partial(iterate_kernel, slices),
        out_shape=jax.ShapeDtypeStruct((LAYER, FIELDS * 128), F32),
        in_specs=[in_vmem] * 6 + [pl.BlockSpec(memory_space=pltpu.SMEM)] + [in_vmem] * 2,
        out_specs=in_vmem,
        scratch_shapes=[
            pltpu.VMEM((256, 128), F32),
            pltpu.VMEM((256, 128), F32),
            pltpu.VMEM((FIELDS * 128, 128), F32),
            pltpu.VMEM((128, FIELDS * 128), F32),
        ]
        + [fine_shape] * 6
        + [coarse_shape] * 6,
        compiler_params=params,
        name="iterate",
    )(
        received,
        volume_op,
        lift_op,
        coarse_volume,
        coarse_lift,
        mixing,
        mixing,
        restrict_op,
        prolong_op,
    )
    returned = lax.all_to_all(modes[:, None, :], "space", 0, 0, tiled=True)
    return pl.pallas_call(
        from_modes_kernel,
        out_shape=jax.ShapeDtypeStruct((1, FIELDS, LAYER, 128), F32),
        in_specs=[in_vmem] * 2,
        out_specs=in_vmem,
        compiler_params=params,
        name="from_modes",
    )(returned.reshape(LAYER, FIELDS * 128), basis)


def solution(mesh):
    return jax.shard_map(
        on_device,
        mesh=mesh,
        in_specs=(P(None, None, "space"), P(None, "space"), P(), P(), P(), P(), P(), P(), P()),
        out_specs=P("tm", None, None, "space"),
        check_vma=False,
    )
```

time: 1190 us -> 117 us (0.10)
  the two profiles are of different devices: /device:TPU:2 before, /device:TPU:1 now
where the time goes in v1:
time: 117 us
  Pallas kernels  55.3 us (47%)
  blocking collectives  23.9 us (20%)
  starting transfers between devices  17.3 us (15%)
  waiting for transfers between devices  17.2 us (15%)
  local copies, waits for them, and re-layouts  2.81 us (2%)
    pallas_call x1, Pallas kernels, on_device(): pl.pallas_call(functools.partial(iterate_kernel, slices), out_shape=jax.S...  52.7 us
    all_to_all x1, blocking collectives, on_device(): returned = lax.all_to_all(modes[:, None, :], 'space', 0, 0, tiled=True)  21.6 us
    all_to_all x1, starting transfers between devices, on_device(): arrived = lax.all_to_all(sent[:, None, :], 'space', 0, 0, tiled=True)  17.3 us
    all_to_all x1, waiting for transfers between devices, on_device(): arrived = lax.all_to_all(sent[:, None, :], 'space', 0, 0, tiled=True)  17.2 us
  transfers between devices with their start and end apart: 1, of which 1 were waited for; matrix products, arithmetic and copies ran while one was open for 0% of the time, Pallas kernels for 0%

profile of v1, /device:TPU:1, one launch (start us, length us, event | category | flops | bytes accessed | tf_op | source)
XLA Modules:
  0.0 116.6 jit_solution(13133305074584256377)
XLA Ops:
  0.0 0.0 copy-start
  0.0 0.9 copy-done
  0.9 0.0 copy-start.7
  0.9 0.7 copy-done.7
  1.6 1.5 %to_modes.1 = (f32[64,768]{1,0:T(8,128)S(1)}, f32[64,128]{1,0:T(8,128)S(1)}) custom-call(f32[5,64,128]{2,1,0:T(8,128)S(1)} %copy-done, s32[6,128]{1,0:T(8,128)S(1)} %copy-done.7), custom_call_target="tpu_custom_call" | custom-call | tf_op jit(solution)/shard_map/to_modes/pallas_call | solution.py:393
  3.1 0.9 copy.11
  4.0 0.0 copy-start.8
  4.0 17.3 %all-to-all-start = ((f32[64,1,768]{2,1,0:T(1,128)}), f32[64,1,768]{2,1,0:T(1,128)S(1)}, u32[]{:S(2)}, u32[]{:S(2)}) async-start(f32[64,1,768]{2,1,0:T(1,128)} %copy.11), calls=%async_computation | async-start | bytes 393216 | tf_op jit(solution)/shard_map/all_to_all | solution.py:404
  21.3 0.0 copy-done.8
  21.3 0.1 copy.13.prolong_ref
  21.4 17.2 %all-to-all-done = f32[64,1,768]{2,1,0:T(1,128)S(1)} async-done(((f32[64,1,768]{2,1,0:T(1,128)}), f32[64,1,768]{2,1,0:T(1,128)S(1)}, u32[]{:S(2)}, u32[]{:S(2)}) %all-to-all-start) | async-done | bytes 196640 | tf_op jit(solution)/shard_map/all_to_all | solution.py:404
  38.6 0.0 copy-start.1
  38.7 0.0 copy-start.2
  38.7 0.0 copy-start.3
  38.7 0.0 copy-start.4
  38.7 0.0 copy-start.5
  38.7 0.0 copy-start.6
  38.7 2.2 %all-gather = f32[128,1,768]{2,0,1:T(8,128)S(1)} all-gather(f32[64,1,768]{2,0,1:T(8,128)S(1)} %copy.12), channel_id=2, replica_groups={{0,1},{2,3},{4,5},{6,7},{8,9},{10,11},{12,13},{14,15},{16,17},{18,19},{..., dimensions={0}, use_global_device_ids=true | all-gather | bytes 589824 | tf_op jit(solution)/shard_map/all_gather | solution.py:406
  41.0 0.0 copy-done.1
  41.0 0.0 copy-done.2
  41.0 0.0 copy-done.3
  41.0 0.0 copy-done.4
  41.0 0.0 copy-done.5
  41.0 0.0 copy-done.6
  41.0 52.7 %iterate.1 = f32[64,640]{1,0:T(8,128)S(1)} custom-call(f32[128,768]{1,0:T(8,128)S(1)} %bitcast.6, f32[64,64]{1,0:T(8,128)S(1)} %copy-done.1, f32[64,96]{1,0:T(8,128)S(1)} %copy-done.2, f32[8,8]{1,0:T(8,128)S(1)} %copy-done.4, f32[8,24]{1,0:T(8,128)S(1)} %copy-done.5, f32[5,5]{1,0:T(8,128)S(1)} %copy-done.3, f32[5,5]{1,0:T(8,128)S(1)} %copy-done.3, ...), custom_call_target="tpu_custom_call" | custom-call | tf_op jit(solution)/shard_map/iterate/pallas_call | solution.py:412
  93.7 0.2 copy.14
  93.9 21.6 %all_to_all.10 = f32[64,1,640]{2,1,0:T(1,128)S(1)} all-to-all(f32[64,1,640]{2,1,0:T(1,128)S(1)} %copy.14), channel_id=1, replica_groups=mesh['tm'=8,'space'=64] {'space'}, dimensions={0} | all-to-all | bytes 327680 | tf_op jit(solution)/shard_map/all_to_all | solution.py:438
  115.5 1.1 from_modes.1
  (2 shorter events, 0.0 us)
Async XLA Ops:
  0.0 0.9 copy-start
  0.9 0.7 copy-start.7
  4.0 17.4 %copy-start.8 = (f32[64,8]{0,1:T(8,128)S(1)}, f32[64,8]{0,1:T(8,128)}, u32[]{:S(2)}) copy-start(f32[64,8]{0,1:T(8,128)} %param.17) | copy-start | bytes 6148
  4.0 34.6 %all-to-all-start = ((f32[64,1,768]{2,1,0:T(1,128)}), f32[64,1,768]{2,1,0:T(1,128)S(1)}, u32[]{:S(2)}, u32[]{:S(2)}) async-start(f32[64,1,768]{2,1,0:T(1,128)} %copy.11), calls=%async_computation | async-start | bytes 393216 | tf_op jit(solution)/shard_map/all_to_all | solution.py:404
  38.6 2.3 %copy-start.1 = (f32[64,64]{1,0:T(8,128)S(1)}, f32[64,64]{1,0:T(8,128)}, u32[]{:S(2)}) copy-start(f32[64,64]{1,0:T(8,128)} %volume_ref.1) | copy-start | bytes 49156
  38.7 2.3 %copy-start.2 = (f32[64,96]{1,0:T(8,128)S(1)}, f32[64,96]{1,0:T(8,128)}, u32[]{:S(2)}) copy-start(f32[64,96]{1,0:T(8,128)} %lift_ref.1) | copy-start | bytes 73732
  38.7 2.3 %copy-start.3 = (f32[5,5]{1,0:T(8,128)S(1)}, f32[5,5]{1,0:T(8,128)}, u32[]{:S(2)}) copy-start(f32[5,5]{1,0:T(8,128)} %mixing_smem.1) | copy-start | bytes 304
  38.7 2.3 %copy-start.4 = (f32[8,8]{1,0:T(8,128)S(1)}, f32[8,8]{1,0:T(8,128)}, u32[]{:S(2)}) copy-start(f32[8,8]{1,0:T(8,128)} %coarse_volume_ref.1) | copy-start | bytes 772
  38.7 2.3 %copy-start.5 = (f32[8,24]{1,0:T(8,128)S(1)}, f32[8,24]{1,0:T(8,128)}, u32[]{:S(2)}) copy-start(f32[8,24]{1,0:T(8,128)} %coarse_lift_ref.1) | copy-start | bytes 2308
  38.7 2.3 %copy-start.6 = (f32[8,64]{1,0:T(8,128)S(1)}, f32[8,64]{1,0:T(8,128)}, u32[]{:S(2)}) copy-start(f32[8,64]{1,0:T(8,128)} %restrict_ref.1) | copy-start | bytes 6148

commit v2 on v1

--- a/solution.py
+++ b/solution.py
@@ -2,6 +2,7 @@
 
 import jax
 import jax.numpy as jnp
+import numpy as np
 from jax import lax
 from jax.experimental import pallas as pl
 from jax.experimental.pallas import tpu as pltpu
@@ -13,6 +14,7 @@
 HALF = 0.7071067811865476
 EXACT = lax.Precision.HIGHEST
 F32 = jnp.float32
+BF16 = jnp.bfloat16
 VMEM_LIMIT = 48 * 1024 * 1024
 
 
@@ -105,15 +107,13 @@
         out_ref[0, field] = jnp.where(upper, whole[LAYER:], whole[:LAYER])
 
 
-def beside_layers(state, from_below):
-    even, odd = state[:LAYER], state[LAYER:]
-    return jnp.concatenate(
-        [
-            jnp.where(from_below, pltpu.roll(odd, 1, 0), odd),
-            jnp.where(from_below, even, pltpu.roll(even, LAYER - 1, 0)),
-        ],
-        axis=0,
-    )
+SHIFTS_A = (0, 1, -1, 2, -2)
+SHIFTS_B = (0, 1, -1)
+FAR_A = (3, -3)
+FAR_B = (2, -2)
+NEAR = len(SHIFTS_A) + len(SHIFTS_B)
+BLOCKS = NEAR + len(FAR_A) + len(FAR_B)
+RING = 8
 
 
 def face_weights(shape, per_edge, node, weights):
@@ -131,43 +131,49 @@
     return result
 
 
-def iterate_kernel(
-    slices,
-    received_ref,
+def split(value):
+    high = value.astype(BF16)
+    return high, (value - high.astype(F32)).astype(BF16)
+
+
+def bdot(a, b):
+    return jnp.dot(a, b, preferred_element_type=F32)
+
+
+def operators_kernel(
     volume_ref,
     lift_ref,
     coarse_volume_ref,
     coarse_lift_ref,
     mixing_ref,
-    mixing_smem,
     restrict_ref,
     prolong_ref,
-    sent_ref,
-    fine_op,
-    coarse_op,
-    restrict_all,
-    prolong_all,
-    start,
-    start_rate,
-    before,
-    before_rate,
-    mid_rate,
-    end_rate,
-    chain,
-    chain_rate,
-    ends,
-    ends_rate,
-    mids,
-    ends_coarse_rate,
+    fine_ref,
+    chain_high_ref,
+    chain_low_ref,
+    restrict_all_ref,
+    prolong_high_ref,
+    prolong_low_ref,
+    near_high_ref,
+    near_low_ref,
+    far_ref,
 ):
     place = lax.axis_index("space")
-    mine = lax.axis_index("tm")
-    core = place & 1
     kx, ky, kx_other, ky_other, paired = wave_numbers(place >> 1)
     single = paired == 0
 
     def turn_cos(first, second, second_half):
         return jnp.where(second_half, eighth_cos(second), eighth_cos(first))
+
+    def put_packed(ref, rows, value):
+        high, low = split(value)
+        ref[rows, :128] = high
+        ref[rows, 128:] = low
+
+    def put(high_ref, low_ref, rows, columns, value):
+        high, low = split(value)
+        high_ref[rows, columns] = high
+        low_ref[rows, columns] = low
 
     wide = iota((128, 128), 1)
     tall = iota((128, 128), 0)
@@ -187,8 +193,11 @@
     lift2 = jnp.concatenate([lift_ref[...]] * 2, axis=0)
     volume2 = jnp.concatenate([volume_ref[...]] * 2, axis=0)
     twice = jnp.where((iota((128, 64), 0) & 63) == iota((128, 64), 1), 1.0, 0.0).astype(F32)
-    fine_op[:128] = jnp.where(same, nt(twice, volume2) + nt(along, lift2), nt(across, lift2))
-    fine_op[128:] = jnp.where(same, nt(ahead, lift2), 0.0)
+    inside = (DT / 2) * jnp.where(same, nt(twice, volume2) + nt(along, lift2), nt(across, lift2))
+    beside = (DT / 2) * jnp.where(same, nt(ahead, lift2), 0.0)
+    put_packed(fine_ref, slice(0, 128), inside)
+    put_packed(fine_ref, slice(128, 256), beside)
+    psi = jnp.concatenate([inside, beside], axis=0)
 
     row = iota((128, 24), 0)
     half = ((row >> 3) & 1) == 1
@@ -204,34 +213,163 @@
     field8 = jnp.where((iota((128, FIELDS), 0) >> 4) == iota((128, FIELDS), 1), 1.0, 0.0).astype(F32)
     same = ((wide >> 3) & 1) == ((tall >> 3) & 1)
     clift = coarse_lift_ref[...]
-    coupled = nt(nt(field8, mixing_ref[...]), field8)
+    mixing = mixing_ref[...]
+    power = nt(field8, mixing)
+    coupled = [nt(field8, field8), nt(power, field8)]
+    for _ in range(2):
+        power = nt(power, mixing)
+        coupled.append(nt(power, field8))
     along = nt(nt(node8, coarse_volume_ref[...]) + nt(along, clift), node8)
     across = nt(nt(across, clift), node8)
     ahead = nt(nt(ahead, clift), node8)
-    coarse_op[:128] = coupled * jnp.where(same, along, across)
-    coarse_op[128:] = coupled * jnp.where(same, ahead, 0.0)
+    level = DT * coupled[1] * jnp.where(same, along, across)
+    beside = DT * coupled[1] * jnp.where(same, ahead, 0.0)
+    upper = (tall & 1) == 1
+    below = jnp.where(upper, beside, 0.0)
+    above = jnp.where(upper, 0.0, beside)
+    level_level = nn(level, level)
+    below_all = nn(below, jnp.concatenate([level, below, above], axis=1))
+    above_all = nn(above, jnp.concatenate([level, below, above], axis=1))
+    once = [level, below, above, jnp.zeros((128, 128), F32)]
+    squared = [
+        level_level + below_all[:, 256:] + above_all[:, 128:256],
+        nn(level, below) + below_all[:, :128],
+        nn(level, above) + above_all[:, :128],
+        below_all[:, 128:256] + above_all[:, 256:],
+    ]
+    for block in range(4):
+        rows = slice(block * 128, (block + 1) * 128)
+        put(chain_high_ref, chain_low_ref, rows, slice(0, 128), once[block])
+        put(chain_high_ref, chain_low_ref, rows, slice(128, 256), 0.5 * squared[block])
 
     restricting = nt(twice, nn(node8, restrict_ref[...]))
     prolonging = nt(node8, jnp.concatenate([prolong_ref[...]] * 2, axis=0))
     down = (tall >= 64) == (((wide >> 3) & 1) == 1)
     up = (wide >= 64) == (((tall >> 3) & 1) == 1)
+    restricting = jnp.where(down, restricting, 0.0)
+    prolonging = jnp.where(up, prolonging, 0.0)
     for field in range(FIELDS):
-        restrict_all[field * 128 : (field + 1) * 128] = jnp.where(
-            down & ((wide >> 4) == field), restricting, 0.0
-        )
-        prolong_all[:, field * 128 : (field + 1) * 128] = jnp.where(
-            up & ((tall >> 4) == field), prolonging, 0.0
-        )
-
+        part = slice(field * 128, (field + 1) * 128)
+        put_packed(restrict_all_ref, part, jnp.where((wide >> 4) == field, restricting, 0.0))
+        put(prolong_high_ref, prolong_low_ref, slice(0, 128), part, jnp.where((tall >> 4) == field, prolonging, 0.0))
+
+    response = jnp.where(tall < 16, prolonging, 0.0)
+    fine_below = (wide & 3) == 3
+    responses = [nn(response, restricting)]
+    for _ in range(3):
+        near = jnp.where(fine_below, pltpu.roll(response, 16, 0), pltpu.roll(response, 112, 0))
+        response = nn(jnp.concatenate([response, near], axis=1), psi)
+        responses.append(nn(response, restricting))
+
+    def block(shift, weights):
+        rows = slice((shift % RING) * 16, (shift % RING) * 16 + 16)
+        total = jnp.zeros((128, 128), F32)
+        for order, weight in weights.items():
+            if abs(shift) <= order:
+                total = total + weight * coupled[order] * jnp.concatenate([responses[order][rows]] * 8, axis=0)
+        return total
+
+    kinds = [(shift, 0) for shift in SHIFTS_A] + [(shift, 1) for shift in SHIFTS_B]
+    kinds += [(shift, 0) for shift in FAR_A] + [(shift, 1) for shift in FAR_B]
+    ends = ({0: 1.0, 1: 2.0, 2: 1.0}, {0: 2.0, 1: 1.0})
+    mid_rates = ({1: 1.0, 2: 1.0}, {1: 1.0})
+    end_rates = ({1: 1.0, 2: 2.0, 3: 1.0}, {1: 2.0, 2: 1.0})
+    for index, (shift, kind) in enumerate(kinds):
+        rows = slice(index * 128, (index + 1) * 128)
+        if index < NEAR:
+            put(near_high_ref, near_low_ref, rows, slice(0, 128), block(shift, ends[kind]))
+            put(near_high_ref, near_low_ref, rows, slice(128, 256), block(shift, mid_rates[kind]))
+        put_packed(far_ref, rows, block(shift, end_rates[kind]))
+
+
+def shifted(even, odd, shift):
+    def rolled(value, by):
+        return value if by == 0 else pltpu.roll(value, by % LAYER, 0)
+
+    if shift % 2 == 0:
+        return rolled(even, shift // 2), rolled(odd, shift // 2)
+    return rolled(odd, (shift + 1) // 2), rolled(even, (shift - 1) // 2)
+
+
+def beside_layers(state, from_below, reach=1):
+    even, odd = state[:LAYER], state[LAYER:]
+    below = shifted(even, odd, reach)
+    above = shifted(even, odd, -reach)
+    return jnp.concatenate([jnp.where(from_below, low, high) for low, high in zip(below, above)], axis=0)
+
+
+def moved(state, shift):
+    return jnp.concatenate(shifted(state[:LAYER], state[LAYER:], shift), axis=0)
+
+
+def polynomials():
+    once = np.array([1.0, 1.0])
+    twice = np.polymul(once, once)
+    two = np.array([1.0, 2.0])
+    on_start = np.array([5 / 12, 4 / 3, 1.0])
+    on_mid = np.array([2 / 3, 1 / 3, 0.0])
+    on_end = np.array([-1 / 12, 1 / 3, 0.0])
+    own = np.polyadd(np.polymul(on_mid, once), np.polymul(on_end, twice))
+    table = {
+        "first": np.polyadd(on_start, own),
+        "later": np.polyadd(np.polymul(on_start, twice), own),
+        "head": own,
+        "push": np.polyadd(on_mid, np.polymul(on_end, two)),
+        "head_before": np.polymul(on_start, twice),
+        "push_before": np.polymul(on_start, two),
+        "new_head": twice,
+        "new_push": two,
+    }
+    return {name: [float(x) for x in np.pad(p[::-1], (0, 5 - len(p)))] for name, p in table.items()}
+
+
+def iterate_kernel(
+    slices,
+    received_ref,
+    fine_ref,
+    chain_high_ref,
+    chain_low_ref,
+    restrict_all_ref,
+    prolong_high_ref,
+    prolong_low_ref,
+    near_high_ref,
+    near_low_ref,
+    far_ref,
+    mixing_smem,
+    sent_ref,
+    start,
+    head1,
+    rate1,
+    head2,
+    rate2,
+    ends,
+    ends_rate,
+    left_high,
+    left_low,
+):
+    place = lax.axis_index("space")
+    mine = lax.axis_index("tm")
+    core = place & 1
+    kx, ky, kx_other, ky_other, paired = wave_numbers(place >> 1)
+    single = paired == 0
     lane = iota((LAYER, 128), 1)
     fine_below = (lane & 3) == 3
     coarse_below = (lane & 1) == 1
     halved = lane >= 64
 
+    def packed_dot(value, packed):
+        high, low = split(value)
+        both = bdot(high, packed)
+        return both[:, :128] + (both[:, 128:] + bdot(low, packed[:, :128]))
+
+    def dot3(value, high_op, low_op):
+        high, low = split(value)
+        return bdot(high, high_op) + (bdot(high, low_op) + bdot(low, high_op))
+
     def fields_of(state):
         return [state[field * 128 : (field + 1) * 128] for field in range(FIELDS)]
 
-    def fine(state):
+    def psi(state):
         parts = fields_of(state)
         pieces = []
         for field in range(FIELDS):
@@ -239,19 +377,15 @@
             for other in range(1, FIELDS):
                 mixed = mixed + mixing_smem[field, other] * parts[other]
             pieces.append(jnp.concatenate([mixed, beside_layers(mixed, fine_below)], axis=1))
-        return nn(jnp.concatenate(pieces, axis=0), fine_op[...])
-
-    def coarse(state):
-        return nn(jnp.concatenate([state, beside_layers(state, coarse_below)], axis=1), coarse_op[...])
+        return packed_dot(jnp.concatenate(pieces, axis=0), fine_ref[...])
 
     def restrict(state):
-        return nn(jnp.concatenate(fields_of(state), axis=1), restrict_all[...])
-
-    def prolong(state):
-        wide_state = nn(state, prolong_all[...])
-        return jnp.concatenate(
-            [wide_state[:, field * 128 : (field + 1) * 128] for field in range(FIELDS)], axis=0
-        )
+        return packed_dot(jnp.concatenate(fields_of(state), axis=1), restrict_all_ref[...])
+
+    def stage(state):
+        wide = [state, moved(state, 1), moved(state, -1), beside_layers(state, coarse_below, 2)]
+        both = dot3(jnp.concatenate(wide, axis=1), chain_high_ref[...], chain_low_ref[...])
+        return both[:, :128], both[:, 128:]
 
     shifts = received_ref[:LAYER, FIELDS * 128 :]
     lower_triangle = jnp.where(iota((LAYER, LAYER), 1) < iota((LAYER, LAYER), 0), 1.0, 0.0).astype(F32)
@@ -278,92 +412,96 @@
             begin = field * 128 + index * LAYER
             start[begin : begin + LAYER] = value * cos + pltpu.roll(value, 64, 1) * sin
 
-    def relay(step, first_part, second_part):
-        head, head_rate = chain[step], chain_rate[step]
-        tail = head + DT * head_rate + first_part
-        tail = head + (DT / 2) * (head_rate + coarse(tail)) + second_part
-        chain[step + 1] = tail
-        chain_rate[step + 1] = coarse(tail)
-
     initial = start[...]
-    start_rate[...] = fine(initial)
-    rate = start_rate[...]
+    power = psi(initial)
     begin = restrict(initial)
-    begin_rate = coarse(begin)
-    rate_coarse = restrict(rate)
-    tau = DT * rate_coarse - DT * begin_rate
-    chain[0] = begin
-    chain_rate[0] = begin_rate
-
-    def first_relay(step, carry):
-        relay(step, tau, tau)
-        return carry
-
-    lax.fori_loop(0, slices, first_relay, 0)
-
-    before[...] = initial
-    before_rate[...] = rate
+    power_coarse = [begin, restrict(power)]
+    for _ in range(2):
+        power = psi(power)
+        power_coarse.append(restrict(power))
+    begin_rate, begin_twice = stage(begin)
+    defect = 2.0 * power_coarse[1] - begin_rate
+    head, rate = begin, begin_rate
+    head1[0] = head
+    rate1[0] = rate
+    for step in range(slices):
+        once, half_twice = stage(rate + defect)
+        head, rate = head + rate + defect + 0.5 * once, rate + once + half_twice
+        head1[step + 1] = head
+        rate1[step + 1] = rate
+        change = head1[step] - begin
+        push = (rate - rate1[step]) * 0.125
+        rows = slice(step * 128, (step + 1) * 128)
+        kinds = [(shift, change) for shift in SHIFTS_A] + [(shift, push) for shift in SHIFTS_B]
+        kinds += [(shift, change) for shift in FAR_A] + [(shift, push) for shift in FAR_B]
+        for index, (shift, value) in enumerate(kinds):
+            high, low = split(moved(value, shift))
+            columns = slice(index * 128, (index + 1) * 128)
+            left_high[rows, columns] = high
+            left_low[rows, columns] = low
+
+    near_high = left_high[:, : NEAR * 128]
+    near_low = left_low[:, : NEAR * 128]
+    near = bdot(near_high, near_high_ref[...]) + (
+        bdot(near_high, near_low_ref[...]) + bdot(near_low, near_high_ref[...])
+    )
+    far = bdot(left_high[...], far_ref[...])
+    far = far[:, :128] + (far[:, 128:] + bdot(left_low[...], far_ref[:, :128]))
+    end_start = power_coarse[0] + 2.0 * power_coarse[1] + power_coarse[2]
+    mid_rate_start = power_coarse[1] + power_coarse[2]
+    end_rate_start = power_coarse[1] + 2.0 * power_coarse[2] + power_coarse[3]
+
     ends[0] = begin
-    ends_rate[0] = rate_coarse
-    ends_coarse_rate[0] = begin_rate
-
-    def first_sweep(step, carry):
-        head, head_rate, tail_rate = chain[step], chain_rate[step], chain_rate[step + 1]
-        state = start[...] + prolong(head - begin)
-        push = prolong((DT / 8) * (tail_rate - head_rate))
-        state = state + (DT / 2) * fine(state) + push
-        middle_rate = fine(state)
-        state = state + (DT / 2) * middle_rate + push
-        last_rate = fine(state)
-        coarse_end = restrict(state)
-        ends[step + 1] = coarse_end
-        mids[step] = restrict(middle_rate)
-        ends_rate[step + 1] = restrict(last_rate)
-        ends_coarse_rate[step + 1] = coarse(coarse_end)
-
-        @pl.when(step + 1 == mine)
-        def _():
-            before[...] = state
-            before_rate[...] = last_rate
-
-        @pl.when(step == mine)
-        def _():
-            mid_rate[...] = middle_rate
-            end_rate[...] = last_rate
-
-        return carry
-
-    lax.fori_loop(0, slices, first_sweep, 0)
-
-    def second_relay(step, carry):
-        integral = (DT / 6) * (ends_rate[step] + 4.0 * mids[step] + ends_rate[step + 1])
-        old_head_rate, old_tail_rate = ends_coarse_rate[step], ends_coarse_rate[step + 1]
-        relay(step, integral - DT * old_head_rate, integral - (DT / 2) * (old_head_rate + old_tail_rate))
-        return carry
-
-    lax.fori_loop(0, slices, second_relay, 0)
-
-    state = before[...] + prolong(chain[mine] - ends[mine])
-    push = prolong(
-        (DT / 8)
-        * (
-            (chain_rate[mine + 1] - ends_coarse_rate[mine + 1])
-            - (chain_rate[mine] - ends_coarse_rate[mine])
-        )
-    )
-    head_rate, middle_rate, last_rate = before_rate[...], mid_rate[...], end_rate[...]
-    state = (
-        state
-        + (DT / 2) * fine(state)
-        + (DT / 24) * (8.0 * middle_rate - 7.0 * head_rate - last_rate)
-        + push
-    )
-    state = (
-        state
-        + (DT / 2) * fine(state)
-        + (DT / 24) * (5.0 * last_rate - 4.0 * middle_rate - head_rate)
-        + push
-    )
+    ends_rate[0] = begin_rate
+    old_rate, old_twice = begin_rate, begin_twice
+    last = power_coarse[1]
+    head, rate = begin, begin_rate
+    head2[0] = head
+    rate2[0] = rate
+    tails = []
+    for step in range(slices):
+        rows = slice(step * 128, (step + 1) * 128)
+        tail = near[rows, :128] + end_start
+        tail_rate, tail_twice = stage(tail)
+        ends[step + 1] = tail
+        ends_rate[step + 1] = tail_rate
+        next_last = far[rows] + end_rate_start
+        integral = (last + 4.0 * (near[rows, 128:] + mid_rate_start) + next_last) * (1.0 / 3.0)
+        defect = integral - old_rate
+        spread = 0.5 * (old_rate - tail_rate)
+        tails.append((defect, defect + spread, old_twice - tail_twice))
+        old_rate, old_twice, last = tail_rate, tail_twice, next_last
+    for step in range(slices):
+        defect, tau, spread_rate = tails[step]
+        once, half_twice = stage(rate + defect)
+        head, rate = head + rate + tau + 0.5 * once, rate + once + half_twice + spread_rate
+        head2[step + 1] = head
+        rate2[step + 1] = rate
+
+    previous = jnp.maximum(mine - 1, 0)
+    later = jnp.where(mine > 0, 1.0, 0.0).astype(F32)
+    table = polynomials()
+    parts = {
+        "head": head1[mine] - begin,
+        "push": (rate1[mine + 1] - rate1[mine]) * 0.125,
+        "head_before": (head1[previous] - begin) * later,
+        "push_before": (rate1[mine] - rate1[previous]) * (0.125 * later),
+        "new_head": head2[mine] - ends[mine],
+        "new_push": ((rate2[mine + 1] - ends_rate[mine + 1]) - (rate2[mine] - ends_rate[mine])) * 0.125,
+    }
+    initial = start[...]
+    state = None
+    for order in (4, 3, 2, 1, 0):
+        total = jnp.zeros((128, 128), F32)
+        for name, value in parts.items():
+            if table[name][order] != 0.0:
+                total = total + table[name][order] * value
+        wide = dot3(total, prolong_high_ref[...], prolong_low_ref[...])
+        added = jnp.concatenate([wide[:, f * 128 : (f + 1) * 128] for f in range(FIELDS)], axis=0)
+        weight = jnp.where(mine > 0, table["later"][order], table["first"][order]).astype(F32)
+        added = added + weight * initial
+        state = added if state is None else psi(state) + added
+
     for field in range(FIELDS):
         halves = []
         for index in range(2):
@@ -377,6 +515,54 @@
         sent_ref[:, field * 128 : (field + 1) * 128] = jnp.where(core == 0, real, imaginary)
 
 
+IN_VMEM = pl.BlockSpec(memory_space=pltpu.VMEM)
+
+
+def operators_call(volume_op, lift_op, coarse_volume, coarse_lift, mixing, restrict_op, prolong_op):
+    shapes = [
+        (256, 256),
+        (512, 256),
+        (512, 256),
+        (FIELDS * 128, 256),
+        (128, FIELDS * 128),
+        (128, FIELDS * 128),
+        (NEAR * 128, 256),
+        (NEAR * 128, 256),
+        (BLOCKS * 128, 256),
+    ]
+    return pl.pallas_call(
+        operators_kernel,
+        out_shape=[jax.ShapeDtypeStruct(shape, BF16) for shape in shapes],
+        in_specs=[IN_VMEM] * 7,
+        out_specs=[IN_VMEM] * len(shapes),
+        compiler_params=pltpu.CompilerParams(vmem_limit_bytes=VMEM_LIMIT),
+        cost_estimate=pl.CostEstimate(flops=10**8, bytes_accessed=3 * 10**6, transcendentals=0),
+        name="operators",
+    )(volume_op, lift_op, coarse_volume, coarse_lift, mixing, restrict_op, prolong_op)
+
+
+def iterate_kernel_call(slices, received, operators, mixing):
+    coarse_shape = pltpu.VMEM((slices + 1, 128, 128), F32)
+    return pl.pallas_call(
+        functools.partial(iterate_kernel, slices),
+        out_shape=jax.ShapeDtypeStruct((LAYER, FIELDS * 128), F32),
+        in_specs=[IN_VMEM] * (1 + len(operators)) + [pl.BlockSpec(memory_space=pltpu.SMEM)],
+        out_specs=IN_VMEM,
+        scratch_shapes=[pltpu.VMEM((FIELDS * 128, 128), F32)]
+        + [coarse_shape] * 6
+        + [pltpu.VMEM((slices * 128, BLOCKS * 128), BF16)] * 2,
+        compiler_params=pltpu.CompilerParams(vmem_limit_bytes=VMEM_LIMIT),
+        name="iterate",
+    )(received, *operators, mixing)
+
+
+def iterate_call(slices, received, volume_op, lift_op, coarse_volume, coarse_lift, mixing, restrict_op, prolong_op):
+    operators = operators_call(
+        volume_op, lift_op, coarse_volume, coarse_lift, mixing, restrict_op, prolong_op
+    )
+    return iterate_kernel_call(slices, received, operators, mixing)
+
+
 def on_device(
     initial,
     neighbours,
@@ -388,7 +574,6 @@
     restrict_op,
     prolong_op,
 ):
-    in_vmem = pl.BlockSpec(memory_space=pltpu.VMEM)
     params = pltpu.CompilerParams(vmem_limit_bytes=VMEM_LIMIT)
     sent, basis = pl.pallas_call(
         to_modes_kernel,
@@ -396,8 +581,8 @@
             jax.ShapeDtypeStruct((LAYER, (FIELDS + 1) * 128), F32),
             jax.ShapeDtypeStruct((LAYER, 128), F32),
         ),
-        in_specs=[in_vmem] * 2,
-        out_specs=(in_vmem, in_vmem),
+        in_specs=[IN_VMEM] * 2,
+        out_specs=(IN_VMEM, IN_VMEM),
         compiler_params=params,
         name="to_modes",
     )(initial, neighbours)
@@ -406,41 +591,16 @@
     pair = lax.all_gather(arrived, "space", axis_index_groups=pairs)
     received = pair.reshape(2 * LAYER, (FIELDS + 1) * 128)
 
-    slices = lax.axis_size("tm")
-    fine_shape = pltpu.VMEM((FIELDS * 128, 128), F32)
-    coarse_shape = pltpu.VMEM((slices + 1, 128, 128), F32)
-    modes = pl.pallas_call(
-        functools.partial(iterate_kernel, slices),
-        out_shape=jax.ShapeDtypeStruct((LAYER, FIELDS * 128), F32),
-        in_specs=[in_vmem] * 6 + [pl.BlockSpec(memory_space=pltpu.SMEM)] + [in_vmem] * 2,
-        out_specs=in_vmem,
-        scratch_shapes=[
-            pltpu.VMEM((256, 128), F32),
-            pltpu.VMEM((256, 128), F32),
-            pltpu.VMEM((FIELDS * 128, 128), F32),
-            pltpu.VMEM((128, FIELDS * 128), F32),
-        ]
-        + [fine_shape] * 6
-        + [coarse_shape] * 6,
-        compiler_params=params,
-        name="iterate",
-    )(
-        received,
-        volume_op,
-        lift_op,
-        coarse_volume,
-        coarse_lift,
-        mixing,
-        mixing,
-        restrict_op,
-        prolong_op,
+    operators = operators_call(
+        volume_op, lift_op, coarse_volume, coarse_lift, mixing, restrict_op, prolong_op
     )
+    modes = iterate_kernel_call(lax.axis_size("tm"), received, operators, mixing)
     returned = lax.all_to_all(modes[:, None, :], "space", 0, 0, tiled=True)
     return pl.pallas_call(
         from_modes_kernel,
         out_shape=jax.ShapeDtypeStruct((1, FIELDS, LAYER, 128), F32),
-        in_specs=[in_vmem] * 2,
-        out_specs=in_vmem,
+        in_specs=[IN_VMEM] * 2,
+        out_specs=IN_VMEM,
         compiler_params=params,
         name="from_modes",
     )(returned.reshape(LAYER, FIELDS * 128), basis)

time: 117 us -> 77.8 us (0.66)
  Pallas kernels: 55.3 us -> 20.9 us
  waiting for transfers between devices: 17.2 us -> 11.7 us
    pallas_call x1 -> x2, Pallas kernels: 52.7 us -> 18.3 us  [the longest x1 13.5 us: iterate_kernel_call(): pl.pallas_call(functools.partial(iterate_kernel, slices), out_shape=jax.S...]
    all_to_all x1, waiting for transfers between devices: 17.2 us -> 11.7 us  [on_device(): arrived = lax.all_to_all(sent[:, None, :], 'space', 0, 0, tiled=True)]
  transfers between devices with their start and end apart: 1 -> 1, of which waited for: 1 -> 1; matrix products, arithmetic and copies ran while one was open for 0% -> 0% of each run, Pallas kernels for 0% -> 6%
where the time goes in v2:
time: 77.8 us; the launch traced here: 77.4 us
  blocking collectives  23.9 us (31%)
  Pallas kernels  20.9 us (27%)
  starting transfers between devices  17.4 us (22%)
  waiting for transfers between devices  11.7 us (15%)
  local copies, waits for them, and re-layouts  3.43 us (4%)
    all_to_all x1, blocking collectives, on_device(): returned = lax.all_to_all(modes[:, None, :], 'space', 0, 0, tiled=True)  21.6 us
    all_to_all x1, starting transfers between devices, on_device(): arrived = lax.all_to_all(sent[:, None, :], 'space', 0, 0, tiled=True)  17.4 us
    pallas_call x1, Pallas kernels, iterate_kernel_call(): pl.pallas_call(functools.partial(iterate_kernel, slices), out_shape=jax.S...  13.5 us
    all_to_all x1, waiting for transfers between devices, on_device(): arrived = lax.all_to_all(sent[:, None, :], 'space', 0, 0, tiled=True)  11.7 us
    pallas_call x1, Pallas kernels, operators_call(): pl.pallas_call(operators_kernel, out_shape=[jax.ShapeDtypeStruct(shape, B...  4.78 us
    unnamed x20, local copies, waits for them, and re-layouts  2.36 us
    all_gather x1, blocking collectives, on_device(): pair = lax.all_gather(arrived, 'space', axis_index_groups=pairs)  2.29 us
  transfers between devices with their start and end apart: 1, of which 1 were waited for; matrix products, arithmetic and copies ran while one was open for 0% of the time, Pallas kernels for 6%

profile of v2, /device:TPU:1, one launch (start us, length us, event | category | flops | bytes accessed | tf_op | source)
XLA Modules:
  0.0 77.4 jit_solution(2515266214365698904)
XLA Ops:
  0.0 0.0 copy-start
  0.0 0.9 %copy-done = f32[5,64,128]{2,1,0:T(8,128)S(1)} copy-done((f32[5,64,128]{2,1,0:T(8,128)S(1)}, f32[5,64,128]{2,1,0:T(8,128)}, u32[]{:S(2)}) %copy-start) | copy-done | bytes 163864
  0.9 0.0 copy-start.1
  0.9 0.7 copy-done.1
  1.6 1.5 %to_modes.1 = (f32[64,768]{1,0:T(8,128)S(1)}, f32[64,128]{1,0:T(8,128)S(1)}) custom-call(f32[5,64,128]{2,1,0:T(8,128)S(1)} %copy-done, s32[6,128]{1,0:T(8,128)S(1)} %copy-done.1), custom_call_target="tpu_custom_call" | custom-call | tf_op jit(solution)/shard_map/to_modes/pallas_call | solution.py:578
  3.1 0.9 %copy.11 = f32[64,1,768]{2,1,0:T(1,128)} copy(f32[64,1,768]{2,0,1:T(8,128)S(1)} %bitcast.9) | data formatting | bytes 393216 | tf_op jit(solution)/shard_map/broadcast_in_dim | solution.py:589
  4.0 0.0 copy-start.8
  4.0 0.0 copy-start.4
  4.0 0.0 copy-start.5
  4.0 0.0 copy-start.6
  4.0 0.0 copy-start.7
  4.0 17.4 %all-to-all-start = ((f32[64,1,768]{2,1,0:T(1,128)}), f32[64,1,768]{2,1,0:T(1,128)S(1)}, u32[]{:S(2)}, u32[]{:S(2)}) async-start(f32[64,1,768]{2,1,0:T(1,128)} %copy.11), calls=%async_computation | async-start | bytes 393216 | tf_op jit(solution)/shard_map/all_to_all | solution.py:589
  21.4 0.0 copy-done.8
  21.4 0.0 copy-start.2
  21.4 0.0 copy-start.3
  21.4 0.1 copy.13.prolong_ref
  21.5 0.0 copy-done.4
  21.5 0.0 copy-done.5
  21.5 0.0 copy-done.6
  21.5 0.0 copy-done.7
  21.5 0.6 copy-done.2
  22.1 0.1 copy-done.3
  22.2 4.8 %operators.1 = (bf16[256,256]{1,0:T(8,128)(2,1)S(1)}, bf16[512,256]{1,0:T(8,128)(2,1)S(1)}, bf16[512,256]{1,0:T(8,128)(2,1)S(1)}, bf16[640,256]{1,0:T(8,128)(2,1...) custom-call(f32[64,64]{1,0:T(8,128)S(1)} %copy-done.3, ...), custom_call_target="tpu_custom_call" | custom-call | flops 100000000 | bytes 3000000 | tf_op jit(solution)/shard_map/operators/pallas_call | solution.py:533
  26.9 11.7 %all-to-all-done = f32[64,1,768]{2,1,0:T(1,128)S(1)} async-done(((f32[64,1,768]{2,1,0:T(1,128)}), f32[64,1,768]{2,1,0:T(1,128)S(1)}, u32[]{:S(2)}, u32[]{:S(2)}) %all-to-all-start) | async-done | bytes 196640 | tf_op jit(solution)/shard_map/all_to_all | solution.py:589
  38.7 2.3 %all-gather = f32[128,1,768]{2,0,1:T(8,128)S(1)} all-gather(f32[64,1,768]{2,0,1:T(8,128)S(1)} %copy.12), channel_id=2, replica_groups={{0,1},{2,3},{4,5},{6,7},{8,9},{10,11},{12,13},{14,15},{16,17},{18,19},{..., dimensions={0}, use_global_device_ids=true | all-gather | bytes 589824 | tf_op jit(solution)/shard_map/all_gather | solution.py:591
  41.0 13.5 %iterate.1 = f32[64,640]{1,0:T(8,128)S(1)} custom-call(f32[128,768]{1,0:T(8,128)S(1)} %bitcast.6, bf16[256,256]{1,0:T(8,128)(2,1)S(1)} %get-tuple-element.17.fine_ref, bf16[512,256]{1,0:T(8,128)(2,1)S(1)} %get-tuple-element.18.chain_high_ref, bf16[512,256]{1,0:T(8,128)(2,1)S(1)} %get-tuple-element.19.chain_low_ref, ...), custom_call_target="tpu_custom_call" | custom-call | tf_op jit(solution)/shard_map/iterate/pallas_call | solution.py:546
  54.5 0.2 copy.14
  54.7 21.6 %all_to_all.10 = f32[64,1,640]{2,1,0:T(1,128)S(1)} all-to-all(f32[64,1,640]{2,1,0:T(1,128)S(1)} %copy.14), channel_id=1, replica_groups=mesh['tm'=8,'space'=64] {'space'}, dimensions={0} | all-to-all | bytes 327680 | tf_op jit(solution)/shard_map/all_to_all | solution.py:598
  76.3 1.1 %from_modes.1 = f32[1,5,64,128]{3,2,1,0:T(8,128)} custom-call(f32[64,640]{1,0:T(8,128)S(1)} %bitcast.8, f32[64,128]{1,0:T(8,128)S(1)} %get-tuple-element.26.basis_ref), custom_call_target="tpu_custom_call" | custom-call | tf_op jit(solution)/shard_map/from_modes/pallas_call | solution.py:599
  (2 shorter events, 0.0 us)
Async XLA Ops:
  0.0 0.9 %copy-start = (f32[5,64,128]{2,1,0:T(8,128)S(1)}, f32[5,64,128]{2,1,0:T(8,128)}, u32[]{:S(2)}) copy-start(f32[5,64,128]{2,1,0:T(8,128)} %initial_ref.1) | copy-start | bytes 491524
  0.9 0.7 copy-start.1
  4.0 17.4 %copy-start.8 = (f32[64,8]{0,1:T(8,128)S(1)}, f32[64,8]{0,1:T(8,128)}, u32[]{:S(2)}) copy-start(f32[64,8]{0,1:T(8,128)} %param.17) | copy-start | bytes 6148
  4.0 17.5 %copy-start.4 = (f32[64,96]{1,0:T(8,128)S(1)}, f32[64,96]{1,0:T(8,128)}, u32[]{:S(2)}) copy-start(f32[64,96]{1,0:T(8,128)} %lift_ref.1) | copy-start | bytes 73732
  4.0 17.5 %copy-start.5 = (f32[8,8]{1,0:T(8,128)S(1)}, f32[8,8]{1,0:T(8,128)}, u32[]{:S(2)}) copy-start(f32[8,8]{1,0:T(8,128)} %coarse_volume_ref.1) | copy-start | bytes 772
  4.0 17.5 %copy-start.6 = (f32[8,24]{1,0:T(8,128)S(1)}, f32[8,24]{1,0:T(8,128)}, u32[]{:S(2)}) copy-start(f32[8,24]{1,0:T(8,128)} %coarse_lift_ref.1) | copy-start | bytes 2308
  4.0 17.5 %copy-start.7 = (f32[8,64]{1,0:T(8,128)S(1)}, f32[8,64]{1,0:T(8,128)}, u32[]{:S(2)}) copy-start(f32[8,64]{1,0:T(8,128)} %restrict_ref.1) | copy-start | bytes 6148
  4.0 34.7 %all-to-all-start = ((f32[64,1,768]{2,1,0:T(1,128)}), f32[64,1,768]{2,1,0:T(1,128)S(1)}, u32[]{:S(2)}, u32[]{:S(2)}) async-start(f32[64,1,768]{2,1,0:T(1,128)} %copy.11), calls=%async_computation | async-start | bytes 393216 | tf_op jit(solution)/shard_map/all_to_all | solution.py:589
  21.4 0.7 copy-start.2
  21.4 0.8 copy-start.3

commit v3 on v2

--- a/solution.py
+++ b/solution.py
@@ -12,6 +12,10 @@
 FIELDS = 5
 DT = 0.125
 HALF = 0.7071067811865476
+UNITS = 32
+STATE = FIELDS * 2 * 128
+EDGE = 16
+MARGIN = 8
 EXACT = lax.Precision.HIGHEST
 F32 = jnp.float32
 BF16 = jnp.bfloat16
@@ -28,6 +32,11 @@
 
 def nt(a, b):
     return lax.dot_general(a, b, (((1,), (1,)), ((), ())), precision=EXACT, preferred_element_type=F32)
+
+
+def nt3(a, b):
+    dims = (((1,), (1,)), ((), ()))
+    return lax.dot_general(a, b, dims, precision=lax.Precision.HIGH, preferred_element_type=F32)
 
 
 def eighth_cos(turn):
@@ -46,64 +55,107 @@
     return kx, ky, kx_other, ky, paired
 
 
-def to_modes_kernel(initial_ref, neighbours_ref, sent_ref, basis_ref):
-    place = lax.axis_index("space")
-    total = lax.axis_size("space") * 2 * LAYER
-    base = place * 2 * LAYER
+def grid_places(links, base, total, first_slot):
     lane = iota((1, 128), 1)
     upper = lane >= LAYER
-    beside = neighbours_ref[...]
     target = iota((128, 128), 0)
 
     def steps(face):
-        one = jnp.where(beside[face : face + 1] - base == target, 1.0, 0.0).astype(jnp.bfloat16)
-        two = jnp.dot(one, one, preferred_element_type=F32).astype(jnp.bfloat16)
-        four = jnp.dot(two, two, preferred_element_type=F32).astype(jnp.bfloat16)
+        one = jnp.where(links[face : face + 1] - base == target, 1.0, 0.0).astype(BF16)
+        two = jnp.dot(one, one, preferred_element_type=F32).astype(BF16)
+        four = jnp.dot(two, two, preferred_element_type=F32).astype(BF16)
         return one, two, four
 
     row = iota((8, 128), 0)
     found = jnp.where((row == 0) & ((iota((8, 128), 1) & (LAYER - 1)) == 0), 1.0, 0.0).astype(F32)
     for part, moves in ((1, steps(0)), (2, steps(2))):
         for power, move in enumerate(moves):
-            shifted = jnp.dot(found.astype(jnp.bfloat16), move, preferred_element_type=F32)
+            shifted = jnp.dot(found.astype(BF16), move, preferred_element_type=F32)
             found = found + shifted + jnp.where(row == part, shifted[0:1] * (1 << power), 0.0)
     along_x = found[1:2]
     along_y = found[2:3]
 
     below = jnp.where(upper, base, (base + total - LAYER) % total)
-    hit = beside[4:5] == below
+    hit = links[4:5] == below
     extra = jnp.zeros((1, 128), F32)
     for slot, (layer_upper, value) in enumerate(
         ((False, along_x), (False, along_y), (True, along_x), (True, along_y))
     ):
         part = jnp.where(hit & (upper == layer_upper), value, 0.0)
-        extra = jnp.where(lane == slot, jnp.sum(part, axis=1, keepdims=True), extra)
-
+        extra = jnp.where(lane == first_slot + slot, jnp.sum(part, axis=1, keepdims=True), extra)
+    return along_x.astype(jnp.int32), along_y.astype(jnp.int32), extra
+
+
+def layer_modes(ref, where, places, first_slot):
+    upper = iota((1, 128), 1) >= LAYER
+    halved = iota((UNITS, 128), 1) >= LAYER
     mode = iota((LAYER, 128), 0)
-    kx, ky, kx_other, ky_other, paired = wave_numbers(mode >> 1)
-    second = (mode & 1) == 1
-    turns = (
-        jnp.where(second, kx_other, kx) * along_x.astype(jnp.int32)
-        + jnp.where(second, ky_other, ky) * along_y.astype(jnp.int32)
-        + jnp.where(second, 2 * paired, 0)
-    )
-    basis = eighth_cos(turns)
+    kx, ky, kx_other, ky_other, paired = wave_numbers(mode & (UNITS - 1))
+    second = mode >= UNITS
+    links = ref[FIELDS * LAYER :].astype(jnp.int32)
+    along_x, along_y, extra = grid_places(links, where * 2 * LAYER, places * 2 * LAYER, first_slot)
+    turns = jnp.where(second, kx_other, kx) * along_x + jnp.where(second, ky_other, ky) * along_y
+    basis = eighth_cos(turns + jnp.where(second, 2 * paired, 0))
+    apart = jnp.concatenate([jnp.where(upper, 0.0, basis), jnp.where(upper, basis, 0.0)], axis=0)
+
+    def of_field(field):
+        state = ref[field * LAYER : (field + 1) * LAYER]
+        modes = nt3(apart, jnp.concatenate([state, state], axis=0))
+        return [
+            jnp.where(
+                halved,
+                modes[index * LAYER + UNITS : (index + 1) * LAYER],
+                modes[index * LAYER : index * LAYER + UNITS],
+            )
+            for index in range(2)
+        ]
+
+    return basis, of_field, extra
+
+
+def own_modes_kernel(own_ref, modes_ref, basis_ref):
+    basis, of_field, extra = layer_modes(own_ref, lax.axis_index("space"), lax.axis_size("space"), 0)
     basis_ref[...] = basis
     for field in range(FIELDS):
-        state = initial_ref[field]
-        apart = jnp.concatenate([jnp.where(upper, 0.0, state), jnp.where(upper, state, 0.0)], axis=0)
-        sent_ref[:, field * 128 : (field + 1) * 128] = nt(basis, apart)
-    sent_ref[:, FIELDS * 128 :] = jnp.broadcast_to(extra, (LAYER, 128))
+        for index, value in enumerate(of_field(field)):
+            column = (field * 2 + index) * 128
+            modes_ref[:, column : column + 128] = value
+    modes_ref[:, STATE:] = jnp.broadcast_to(extra, (UNITS, 128))
+
+
+def both_modes_kernel(own_ref, beside_ref, sent_ref, blocks, semaphores):
+    place = lax.axis_index("space")
+    places = lax.axis_size("space")
+    partner = (jnp.where(((place >> 3) & 3) < 2, place - EDGE, place + EDGE) + places) % places
+    for column in range(0, STATE, 128):
+        blocks[:, 0, column : column + 128] = own_ref[:, column : column + 128]
+    first = pltpu.make_async_copy(blocks.at[:, :, :STATE], sent_ref.at[:, :, :STATE], semaphores.at[0])
+    first.start()
+    _, of_field, extra = layer_modes(beside_ref, partner, places, 4)
+    for field in range(FIELDS):
+        for index, value in enumerate(of_field(field)):
+            column = STATE + (field * 2 + index) * 128
+            blocks[:, 0, column : column + 128] = value
+    blocks[:, 0, 2 * STATE :] = own_ref[:, STATE:] + jnp.broadcast_to(extra, (UNITS, 128))
+    second = pltpu.make_async_copy(blocks.at[:, :, STATE:], sent_ref.at[:, :, STATE:], semaphores.at[1])
+    second.start()
+    first.wait()
+    second.wait()
 
 
 def from_modes_kernel(modes_ref, basis_ref, out_ref):
-    mode = iota((LAYER, 128), 0)
-    scale = jnp.where(mode < 60, 2.0 / LAYER, 1.0 / LAYER).astype(F32)
+    unit = iota((LAYER, 128), 0) & (UNITS - 1)
+    scale = jnp.where(unit < 30, 2.0 / LAYER, 1.0 / LAYER).astype(F32)
     back = basis_ref[...] * scale
     upper = iota((LAYER, 128), 1) >= LAYER
+    halved = iota((UNITS, 128), 1) >= LAYER
     for field in range(FIELDS):
-        part = jnp.transpose(modes_ref[:, field * 128 : (field + 1) * 128])
-        whole = nn(part, back)
+        column = field * 256
+        even = modes_ref[:, 0, column : column + 128]
+        odd = modes_ref[:, 0, column + 128 : column + 256]
+        real = jnp.where(halved, pltpu.roll(odd, 64, 1), even)
+        imaginary = jnp.where(halved, odd, pltpu.roll(even, 64, 1))
+        whole = nn(jnp.transpose(jnp.concatenate([real, imaginary], axis=0)), back)
         out_ref[0, field] = jnp.where(upper, whole[LAYER:], whole[:LAYER])
 
 
@@ -157,9 +209,29 @@
     near_high_ref,
     near_low_ref,
     far_ref,
+    *scratch,
 ):
+    *held, semaphores = scratch
+    operands = (
+        volume_ref,
+        lift_ref,
+        coarse_volume_ref,
+        coarse_lift_ref,
+        mixing_ref,
+        restrict_ref,
+        prolong_ref,
+    )
+    copies = [
+        pltpu.make_async_copy(operand, place_for, semaphores.at[index])
+        for index, (operand, place_for) in enumerate(zip(operands, held))
+    ]
+    for copy in copies:
+        copy.start()
+    for copy in copies:
+        copy.wait()
+    volume_ref, lift_ref, coarse_volume_ref, coarse_lift_ref, mixing_ref, restrict_ref, prolong_ref = held
     place = lax.axis_index("space")
-    kx, ky, kx_other, ky_other, paired = wave_numbers(place >> 1)
+    kx, ky, kx_other, ky_other, paired = wave_numbers(place & (UNITS - 1))
     single = paired == 0
 
     def turn_cos(first, second, second_half):
@@ -284,7 +356,7 @@
 
 def shifted(even, odd, shift):
     def rolled(value, by):
-        return value if by == 0 else pltpu.roll(value, by % LAYER, 0)
+        return value if by == 0 else pltpu.roll(value, by % len(value), 0)
 
     if shift % 2 == 0:
         return rolled(even, shift // 2), rolled(odd, shift // 2)
@@ -292,7 +364,8 @@
 
 
 def beside_layers(state, from_below, reach=1):
-    even, odd = state[:LAYER], state[LAYER:]
+    half = len(state) // 2
+    even, odd = state[:half], state[half:]
     below = shifted(even, odd, reach)
     above = shifted(even, odd, -reach)
     return jnp.concatenate([jnp.where(from_below, low, high) for low, high in zip(below, above)], axis=0)
@@ -335,7 +408,7 @@
     near_high_ref,
     near_low_ref,
     far_ref,
-    mixing_smem,
+    mixing_ref,
     sent_ref,
     start,
     head1,
@@ -344,13 +417,14 @@
     rate2,
     ends,
     ends_rate,
-    left_high,
-    left_low,
+    mixing_smem,
+    semaphore,
 ):
+    fetch = pltpu.make_async_copy(mixing_ref, mixing_smem, semaphore)
+    fetch.start()
     place = lax.axis_index("space")
     mine = lax.axis_index("tm")
-    core = place & 1
-    kx, ky, kx_other, ky_other, paired = wave_numbers(place >> 1)
+    kx, ky, kx_other, ky_other, paired = wave_numbers(place & (UNITS - 1))
     single = paired == 0
     lane = iota((LAYER, 128), 1)
     fine_below = (lane & 3) == 3
@@ -367,7 +441,8 @@
         return bdot(high, high_op) + (bdot(high, low_op) + bdot(low, high_op))
 
     def fields_of(state):
-        return [state[field * 128 : (field + 1) * 128] for field in range(FIELDS)]
+        rows = len(state) // FIELDS
+        return [state[field * rows : (field + 1) * rows] for field in range(FIELDS)]
 
     def psi(state):
         parts = fields_of(state)
@@ -376,18 +451,33 @@
             mixed = mixing_smem[field, 0] * parts[0]
             for other in range(1, FIELDS):
                 mixed = mixed + mixing_smem[field, other] * parts[other]
-            pieces.append(jnp.concatenate([mixed, beside_layers(mixed, fine_below)], axis=1))
+            pieces.append(jnp.concatenate([mixed, beside_layers(mixed, fine_below[: len(mixed) // 2])], axis=1))
         return packed_dot(jnp.concatenate(pieces, axis=0), fine_ref[...])
 
     def restrict(state):
         return packed_dot(jnp.concatenate(fields_of(state), axis=1), restrict_all_ref[...])
 
-    def stage(state):
-        wide = [state, moved(state, 1), moved(state, -1), beside_layers(state, coarse_below, 2)]
-        both = dot3(jnp.concatenate(wide, axis=1), chain_high_ref[...], chain_low_ref[...])
-        return both[:, :128], both[:, 128:]
-
-    shifts = received_ref[:LAYER, FIELDS * 128 :]
+    def stages(states):
+        wide = [
+            jnp.concatenate(
+                [state, moved(state, 1), moved(state, -1), beside_layers(state, coarse_below, 2)], axis=1
+            )
+            for state in states
+        ]
+        both = dot3(jnp.concatenate(wide, axis=0), chain_high_ref[...], chain_low_ref[...])
+        both = [both[i * 128 : (i + 1) * 128] for i in range(len(states))]
+        return [(part[:, :128], part[:, 128:]) for part in both]
+
+    def in_order(column):
+        begin = column if column < STATE else 2 * STATE
+        own = received_ref[:, 0, begin : begin + 128]
+        if column < STATE:
+            other = received_ref[:, 0, STATE + column : STATE + column + 128]
+        else:
+            other = pltpu.roll(own, 124, 1)
+        return jnp.concatenate([other[:EDGE], own, other[EDGE:]], axis=0)
+
+    shifts = in_order(STATE)
     lower_triangle = jnp.where(iota((LAYER, LAYER), 1) < iota((LAYER, LAYER), 0), 1.0, 0.0).astype(F32)
     first_x, first_y = shifts[:, 0:1], shifts[:, 1:2]
     both_x, both_y = first_x + shifts[:, 2:3], first_y + shifts[:, 3:4]
@@ -403,119 +493,129 @@
         turning.append((cos, jnp.where(halved, sin, -sin)))
 
     for field in range(FIELDS):
-        real = received_ref[:LAYER, field * 128 : (field + 1) * 128]
-        imaginary = received_ref[LAYER:, field * 128 : (field + 1) * 128]
-        even = jnp.where(halved, pltpu.roll(imaginary, 64, 1), real)
-        odd = jnp.where(halved, imaginary, pltpu.roll(real, 64, 1))
-        for index, value in enumerate((even, odd)):
+        for index in range(2):
+            value = in_order((field * 2 + index) * 128)
             cos, sin = turning[index]
             begin = field * 128 + index * LAYER
             start[begin : begin + LAYER] = value * cos + pltpu.roll(value, 64, 1) * sin
+
+    fetch.wait()
 
     initial = start[...]
     power = psi(initial)
     begin = restrict(initial)
     power_coarse = [begin, restrict(power)]
-    for _ in range(2):
-        power = psi(power)
-        power_coarse.append(restrict(power))
-    begin_rate, begin_twice = stage(begin)
+    ((begin_rate, begin_twice),) = stages([begin])
     defect = 2.0 * power_coarse[1] - begin_rate
     head, rate = begin, begin_rate
-    head1[0] = head
-    rate1[0] = rate
-    for step in range(slices):
-        once, half_twice = stage(rate + defect)
-        head, rate = head + rate + defect + 0.5 * once, rate + once + half_twice
-        head1[step + 1] = head
-        rate1[step + 1] = rate
-        change = head1[step] - begin
-        push = (rate - rate1[step]) * 0.125
-        rows = slice(step * 128, (step + 1) * 128)
+    later_head, later_rate = begin, begin_rate
+    old_rate, old_twice, last = begin_rate, begin_twice, power_coarse[1]
+    head1[0], rate1[0] = begin, begin_rate
+    head2[0], rate2[0] = begin, begin_rate
+    ends[0], ends_rate[0] = begin, begin_rate
+
+    def needed(change, push):
         kinds = [(shift, change) for shift in SHIFTS_A] + [(shift, push) for shift in SHIFTS_B]
         kinds += [(shift, change) for shift in FAR_A] + [(shift, push) for shift in FAR_B]
-        for index, (shift, value) in enumerate(kinds):
-            high, low = split(moved(value, shift))
-            columns = slice(index * 128, (index + 1) * 128)
-            left_high[rows, columns] = high
-            left_low[rows, columns] = low
-
-    near_high = left_high[:, : NEAR * 128]
-    near_low = left_low[:, : NEAR * 128]
-    near = bdot(near_high, near_high_ref[...]) + (
-        bdot(near_high, near_low_ref[...]) + bdot(near_low, near_high_ref[...])
-    )
-    far = bdot(left_high[...], far_ref[...])
-    far = far[:, :128] + (far[:, 128:] + bdot(left_low[...], far_ref[:, :128]))
-    end_start = power_coarse[0] + 2.0 * power_coarse[1] + power_coarse[2]
-    mid_rate_start = power_coarse[1] + power_coarse[2]
-    end_rate_start = power_coarse[1] + 2.0 * power_coarse[2] + power_coarse[3]
-
-    ends[0] = begin
-    ends_rate[0] = begin_rate
-    old_rate, old_twice = begin_rate, begin_twice
-    last = power_coarse[1]
-    head, rate = begin, begin_rate
-    head2[0] = head
-    rate2[0] = rate
-    tails = []
-    for step in range(slices):
-        rows = slice(step * 128, (step + 1) * 128)
-        tail = near[rows, :128] + end_start
-        tail_rate, tail_twice = stage(tail)
-        ends[step + 1] = tail
-        ends_rate[step + 1] = tail_rate
-        next_last = far[rows] + end_rate_start
-        integral = (last + 4.0 * (near[rows, 128:] + mid_rate_start) + next_last) * (1.0 / 3.0)
-        defect = integral - old_rate
-        spread = 0.5 * (old_rate - tail_rate)
-        tails.append((defect, defect + spread, old_twice - tail_twice))
-        old_rate, old_twice, last = tail_rate, tail_twice, next_last
-    for step in range(slices):
-        defect, tau, spread_rate = tails[step]
-        once, half_twice = stage(rate + defect)
-        head, rate = head + rate + tau + 0.5 * once, rate + once + half_twice + spread_rate
-        head2[step + 1] = head
-        rate2[step + 1] = rate
+        parts = [split(moved(value, shift)) for shift, value in kinds]
+        high = jnp.concatenate([part[0] for part in parts], axis=1)
+        low = jnp.concatenate([part[1] for part in parts], axis=1)
+        near_high, near_low = high[:, : NEAR * 128], low[:, : NEAR * 128]
+        near = bdot(near_high, near_high_ref[...]) + (
+            bdot(near_high, near_low_ref[...]) + bdot(near_low, near_high_ref[...])
+        )
+        far = bdot(high, far_ref[...])
+        return near[:, :128], near[:, 128:], far[:, :128] + (far[:, 128:] + bdot(low, far_ref[:, :128]))
 
     previous = jnp.maximum(mine - 1, 0)
     later = jnp.where(mine > 0, 1.0, 0.0).astype(F32)
     table = polynomials()
-    parts = {
-        "head": head1[mine] - begin,
-        "push": (rate1[mine + 1] - rate1[mine]) * 0.125,
-        "head_before": (head1[previous] - begin) * later,
-        "push_before": (rate1[mine] - rate1[previous]) * (0.125 * later),
-        "new_head": head2[mine] - ends[mine],
-        "new_push": ((rate2[mine + 1] - ends_rate[mine + 1]) - (rate2[mine] - ends_rate[mine])) * 0.125,
-    }
-    initial = start[...]
-    state = None
-    for order in (4, 3, 2, 1, 0):
-        total = jnp.zeros((128, 128), F32)
+
+    def around(state):
+        half = len(state) // 2
+        return jnp.concatenate(
+            [state[EDGE - MARGIN : EDGE + UNITS + MARGIN], state[half + EDGE - MARGIN : half + EDGE + UNITS + MARGIN]],
+            axis=0,
+        )
+
+    initial_around = jnp.concatenate([around(part) for part in fields_of(initial)], axis=0)
+
+    def added(order):
+        total = None
         for name, value in parts.items():
             if table[name][order] != 0.0:
-                total = total + table[name][order] * value
+                term = table[name][order] * value
+                total = term if total is None else total + term
         wide = dot3(total, prolong_high_ref[...], prolong_low_ref[...])
-        added = jnp.concatenate([wide[:, f * 128 : (f + 1) * 128] for f in range(FIELDS)], axis=0)
+        wide = jnp.concatenate([wide[:, f * 128 : (f + 1) * 128] for f in range(FIELDS)], axis=0)
         weight = jnp.where(mine > 0, table["later"][order], table["first"][order]).astype(F32)
-        added = added + weight * initial
-        state = added if state is None else psi(state) + added
-
+        return wide + weight * initial_around
+
+    waiting = []
+    ready = None
+    for step in range(slices + 2):
+        states = []
+        if step < slices:
+            states.append(rate + defect)
+        if ready is not None:
+            tail = ready[0] + end_start
+            next_last = ready[2] + end_rate_start
+            integral = (last + 4.0 * (ready[1] + mid_rate_start) + next_last) * (1.0 / 3.0)
+            later_defect = integral - old_rate
+            states += [tail, later_rate + later_defect]
+        found = stages(states)
+        if ready is not None:
+            (tail_rate, tail_twice), (once, half_twice) = found[-2:]
+            later_head = later_head + later_rate + later_defect + 0.5 * (old_rate - tail_rate + once)
+            later_rate = later_rate + once + half_twice + (old_twice - tail_twice)
+            old_rate, old_twice, last = tail_rate, tail_twice, next_last
+            slot = step - 1
+            head2[slot], rate2[slot] = later_head, later_rate
+            ends[slot], ends_rate[slot] = tail, tail_rate
+        ready = needed(*waiting.pop()) if waiting else None
+        if step < slices:
+            once, half_twice = found[0]
+            change = head - begin
+            head, next_rate = head + rate + defect + 0.5 * once, rate + once + half_twice
+            waiting.append((change, (next_rate - rate) * 0.125))
+            rate = next_rate
+            head1[step + 1], rate1[step + 1] = head, rate
+        if step == slices - 1:
+            parts = {
+                "head": around(head1[mine] - begin),
+                "push": around((rate1[mine + 1] - rate1[mine]) * 0.125),
+                "head_before": around((head1[previous] - begin) * later),
+                "push_before": around((rate1[mine] - rate1[previous]) * (0.125 * later)),
+            }
+            state = added(4)
+            state = psi(state) + added(3)
+        if step < 2:
+            power = psi(power)
+            power_coarse.append(restrict(power))
+        if step == 1:
+            end_start = power_coarse[0] + 2.0 * power_coarse[1] + power_coarse[2]
+            mid_rate_start = power_coarse[1] + power_coarse[2]
+            end_rate_start = power_coarse[1] + 2.0 * power_coarse[2] + power_coarse[3]
+
+    new_head = head2[mine] - ends[mine]
+    new_push = ((rate2[mine + 1] - ends_rate[mine + 1]) - (rate2[mine] - ends_rate[mine])) * 0.125
+    parts["new_head"], parts["new_push"] = around(new_head), around(new_push)
+    for order in (2, 1, 0):
+        state = psi(state) + added(order)
+    turned = [(cos[EDGE - MARGIN : EDGE + UNITS + MARGIN], sin[EDGE - MARGIN : EDGE + UNITS + MARGIN]) for cos, sin in turning]
+    rows = len(state) // (2 * FIELDS)
     for field in range(FIELDS):
-        halves = []
         for index in range(2):
-            cos, sin = turning[index]
-            begin_row = field * 128 + index * LAYER
-            value = state[begin_row : begin_row + LAYER]
-            halves.append(value * cos - pltpu.roll(value, 64, 1) * sin)
-        even, odd = halves
-        real = jnp.where(halved, pltpu.roll(odd, 64, 1), even)
-        imaginary = jnp.where(halved, odd, pltpu.roll(even, 64, 1))
-        sent_ref[:, field * 128 : (field + 1) * 128] = jnp.where(core == 0, real, imaginary)
+            cos, sin = turned[index]
+            begin_row = (field * 2 + index) * rows
+            value = state[begin_row : begin_row + rows]
+            value = value * cos - pltpu.roll(value, 64, 1) * sin
+            column = (field * 2 + index) * 128
+            sent_ref[:, 0, column : column + 128] = value[MARGIN : MARGIN + UNITS]
 
 
 IN_VMEM = pl.BlockSpec(memory_space=pltpu.VMEM)
+ANYWHERE = pl.BlockSpec(memory_space=pltpu.HBM)
 
 
 def operators_call(volume_op, lift_op, coarse_volume, coarse_lift, mixing, restrict_op, prolong_op):
@@ -533,8 +633,13 @@
     return pl.pallas_call(
         operators_kernel,
         out_shape=[jax.ShapeDtypeStruct(shape, BF16) for shape in shapes],
-        in_specs=[IN_VMEM] * 7,
+        in_specs=[ANYWHERE] * 7,
         out_specs=[IN_VMEM] * len(shapes),
+        scratch_shapes=[
+            pltpu.VMEM(operand.shape, F32)
+            for operand in (volume_op, lift_op, coarse_volume, coarse_lift, mixing, restrict_op, prolong_op)
+        ]
+        + [pltpu.SemaphoreType.DMA((7,))],
         compiler_params=pltpu.CompilerParams(vmem_limit_bytes=VMEM_LIMIT),
         cost_estimate=pl.CostEstimate(flops=10**8, bytes_accessed=3 * 10**6, transcendentals=0),
         name="operators",
@@ -545,12 +650,12 @@
     coarse_shape = pltpu.VMEM((slices + 1, 128, 128), F32)
     return pl.pallas_call(
         functools.partial(iterate_kernel, slices),
-        out_shape=jax.ShapeDtypeStruct((LAYER, FIELDS * 128), F32),
-        in_specs=[IN_VMEM] * (1 + len(operators)) + [pl.BlockSpec(memory_space=pltpu.SMEM)],
+        out_shape=jax.ShapeDtypeStruct((UNITS, 1, STATE), F32),
+        in_specs=[IN_VMEM] * (1 + len(operators)) + [ANYWHERE],
         out_specs=IN_VMEM,
         scratch_shapes=[pltpu.VMEM((FIELDS * 128, 128), F32)]
         + [coarse_shape] * 6
-        + [pltpu.VMEM((slices * 128, BLOCKS * 128), BF16)] * 2,
+        + [pltpu.SMEM((FIELDS, FIELDS), F32), pltpu.SemaphoreType.DMA],
         compiler_params=pltpu.CompilerParams(vmem_limit_bytes=VMEM_LIMIT),
         name="iterate",
     )(received, *operators, mixing)
@@ -560,7 +665,21 @@
     operators = operators_call(
         volume_op, lift_op, coarse_volume, coarse_lift, mixing, restrict_op, prolong_op
     )
-    return iterate_kernel_call(slices, received, operators, mixing)
+    return iterate_kernel_call(slices, received[:, None, :], operators, mixing)
+
+
+def window_partners(slices, places):
+    per_chip_row = 8
+    depth = places // per_chip_row
+    ring = 2 * depth
+    route = []
+    for slot in range(slices):
+        for place in range(places):
+            z = slot % 2 * depth + place // per_chip_row
+            other = (z - 2 if z % 4 < 2 else z + 2) % ring
+            partner = (slot - slot % 2 + other // depth) * places + other % depth * per_chip_row
+            route.append((partner + place % per_chip_row, slot * places + place))
+    return route
 
 
 def on_device(
@@ -575,27 +694,44 @@
     prolong_op,
 ):
     params = pltpu.CompilerParams(vmem_limit_bytes=VMEM_LIMIT)
-    sent, basis = pl.pallas_call(
-        to_modes_kernel,
+    rows = FIELDS * LAYER
+    own = jnp.pad(initial.reshape(rows, -1), ((0, len(neighbours)), (0, 0)))
+    own = own + jnp.pad(neighbours, ((rows, 0), (0, 0))).astype(F32)
+    beside = lax.ppermute(own, ("tm", "space"), window_partners(lax.axis_size("tm"), lax.axis_size("space")))
+    modes, basis = pl.pallas_call(
+        own_modes_kernel,
         out_shape=(
-            jax.ShapeDtypeStruct((LAYER, (FIELDS + 1) * 128), F32),
+            jax.ShapeDtypeStruct((UNITS, STATE + 128), F32),
             jax.ShapeDtypeStruct((LAYER, 128), F32),
         ),
-        in_specs=[IN_VMEM] * 2,
+        in_specs=[IN_VMEM],
         out_specs=(IN_VMEM, IN_VMEM),
         compiler_params=params,
-        name="to_modes",
-    )(initial, neighbours)
-    arrived = lax.all_to_all(sent[:, None, :], "space", 0, 0, tiled=True)
-    pairs = [[i, i + 1] for i in range(0, lax.axis_size("space"), 2)]
-    pair = lax.all_gather(arrived, "space", axis_index_groups=pairs)
-    received = pair.reshape(2 * LAYER, (FIELDS + 1) * 128)
-
+        name="own_modes",
+    )(own)
+    sent = pl.pallas_call(
+        both_modes_kernel,
+        out_shape=jax.ShapeDtypeStruct((UNITS, 1, 2 * STATE + 128), F32),
+        in_specs=[IN_VMEM] * 2,
+        out_specs=pl.BlockSpec(memory_space=pl.ANY),
+        scratch_shapes=[
+            pltpu.VMEM((UNITS, 1, 2 * STATE + 128), F32),
+            pltpu.SemaphoreType.DMA((2,)),
+        ],
+        compiler_params=params,
+        name="both_modes",
+    )(modes, beside)
+    windows = [[first + i for i in range(UNITS)] for first in range(0, lax.axis_size("space"), UNITS)]
+
+    def exchange(blocks):
+        return lax.all_to_all(blocks, "space", 0, 0, axis_index_groups=windows, tiled=True)
+
+    received = exchange(sent)
     operators = operators_call(
         volume_op, lift_op, coarse_volume, coarse_lift, mixing, restrict_op, prolong_op
     )
     modes = iterate_kernel_call(lax.axis_size("tm"), received, operators, mixing)
-    returned = lax.all_to_all(modes[:, None, :], "space", 0, 0, tiled=True)
+    returned = exchange(modes)
     return pl.pallas_call(
         from_modes_kernel,
         out_shape=jax.ShapeDtypeStruct((1, FIELDS, LAYER, 128), F32),
@@ -603,7 +739,7 @@
         out_specs=IN_VMEM,
         compiler_params=params,
         name="from_modes",
-    )(returned.reshape(LAYER, FIELDS * 128), basis)
+    )(returned, basis)
 
 
 def solution(mesh):

time: 77.8 us -> 68.5 us (0.88)
  blocking collectives: 23.9 us -> 13.2 us
  waiting for transfers between devices: 11.7 us -> 9.29 us
  starting transfers between devices: 17.4 us -> 19.2 us
  local copies, waits for them, and re-layouts: 3.43 us -> 5.04 us
  other arithmetic: 0 us -> 0.94 us
    ppermute x0 -> x1, starting transfers between devices: none -> 12.4 us  [on_device(): lax.ppermute(own, ('tm', 'space'), window_partners(lax.axis_size('tm'), l...]
    all_to_all x1, starting transfers between devices: 17.4 us -> 6.8 us  [exchange(): lax.all_to_all(blocks, 'space', 0, 0, axis_index_groups=windows, tiled=True)]
    all_to_all x1, blocking collectives: 21.6 us -> 13.2 us  [exchange(): lax.all_to_all(blocks, 'space', 0, 0, axis_index_groups=windows, tiled=True)]
    all_to_all x1, waiting for transfers between devices: 11.7 us -> 3.44 us  [exchange(): lax.all_to_all(blocks, 'space', 0, 0, axis_index_groups=windows, tiled=True)]
    ppermute x0 -> x1, waiting for transfers between devices: none -> 5.85 us  [on_device(): lax.ppermute(own, ('tm', 'space'), window_partners(lax.axis_size('tm'), l...]
    pallas_call x1, Pallas kernels: 13.5 us -> 10.8 us  [iterate_kernel_call(): pl.pallas_call(functools.partial(iterate_kernel, slices), out_shape=jax.S...]
    unnamed x20 -> x17, local copies, waits for them, and re-layouts: 2.36 us -> 5.04 us
    all_gather x1 -> x0, blocking collectives: 2.29 us -> none  [on_device(): pair = lax.all_gather(arrived, 'space', axis_index_groups=pairs)]
  transfers between devices with their start and end apart: 1 -> 2, of which waited for: 1 -> 2; matrix products, arithmetic and copies ran while one was open for 0% -> 0% of each run, Pallas kernels for 6% -> 9%
where the time goes in v3:
time: 68.5 us; the launch traced here: 68 us
  Pallas kernels  20.2 us (29%)
  starting transfers between devices  19.2 us (28%)
  blocking collectives  13.2 us (19%)
  waiting for transfers between devices  9.29 us (14%)
  local copies, waits for them, and re-layouts  5.04 us (7%)
  other arithmetic  0.94 us (1%)
    all_to_all x1, blocking collectives, exchange(): lax.all_to_all(blocks, 'space', 0, 0, axis_index_groups=windows, tiled=True)  13.2 us
    ppermute x1, starting transfers between devices, on_device(): lax.ppermute(own, ('tm', 'space'), window_partners(lax.axis_size('tm'), l...  12.4 us
    pallas_call x1, Pallas kernels, iterate_kernel_call(): pl.pallas_call(functools.partial(iterate_kernel, slices), out_shape=jax.S...  10.8 us
    all_to_all x1, starting transfers between devices, exchange(): lax.all_to_all(blocks, 'space', 0, 0, axis_index_groups=windows, tiled=True)  6.8 us
    ppermute x1, waiting for transfers between devices, on_device(): lax.ppermute(own, ('tm', 'space'), window_partners(lax.axis_size('tm'), l...  5.85 us
    unnamed x17, local copies, waits for them, and re-layouts  5.04 us
    pallas_call x1, Pallas kernels, operators_call(): pl.pallas_call(operators_kernel, out_shape=[jax.ShapeDtypeStruct(shape, B...  4.97 us
    all_to_all x1, waiting for transfers between devices, exchange(): lax.all_to_all(blocks, 'space', 0, 0, axis_index_groups=windows, tiled=True)  3.44 us
  transfers between devices with their start and end apart: 2, of which 2 were waited for; matrix products, arithmetic and copies ran while one was open for 0% of the time, Pallas kernels for 9%

profile of v3, /device:TPU:1, one launch (start us, length us, event | category | flops | bytes accessed | tf_op | source)
XLA Modules:
  0.0 68.0 jit_solution(1727744880332200300)
XLA Ops:
  0.0 0.9 %convert_add_fusion.own_ref = f32[326,128]{1,0:T(8,128)S(1)} fusion(s32[6,128]{1,0:T(8,128)} %param.10, f32[320,128]{1,0:T(8,128)} %bitcast.1), kind=kLoop, calls=%fused_computation | loop fusion | flops 83456 | bytes 333824 | tf_op jit(solution)/shard_map/add | solution.py:699
  0.9 12.4 %collective-permute-start = (f32[326,128]{1,0:T(8,128)S(1)}, f32[326,128]{1,0:T(8,128)S(1)}, u32[]{:S(2)}, u32[]{:S(2)}) collective-permute-start(f32[326,128]{1,0:T(8,128)S(1)} %convert_add_fusion.own_ref), channel_id=1, source_target_pairs={{112,0},{113,1},{114,2},{115,3},{116,4},{117,5},{118,6},{119,7},{1... | collective-permute-start | bytes 500744 | tf_op jit(solution)/shard_map/ppermute | solution.py:700
  13.4 1.3 %own_modes.1 = (f32[32,1408]{1,0:T(8,128)S(1)}, f32[64,128]{1,0:T(8,128)S(1)}) custom-call(f32[326,128]{1,0:T(8,128)S(1)} %convert_add_fusion.own_ref), custom_call_target="tpu_custom_call" | custom-call | tf_op jit(solution)/shard_map/own_modes/pallas_call | solution.py:701
  14.6 5.9 %collective-permute-done.beside_ref = f32[326,128]{1,0:T(8,128)S(1)} collective-permute-done((f32[326,128]{1,0:T(8,128)S(1)}, f32[326,128]{1,0:T(8,128)S(1)}, u32[]{:S(2)}, u32[]{:S(2)}) %collective-permute-start) | collective-permute-done | bytes 166944 | tf_op jit(solution)/shard_map/ppermute | solution.py:700
  20.5 1.9 %both_modes.1 = f32[32,1,2688]{2,1,0:T(1,128)} custom-call(f32[32,1408]{1,0:T(8,128)S(1)} %get-tuple-element.16.own_ref, f32[326,128]{1,0:T(8,128)S(1)} %collective-permute-done.beside_ref), custom_call_target="tpu_custom_call" | custom-call | tf_op jit(solution)/shard_map/both_modes/pallas_call | solution.py:712
  22.4 0.0 copy-start.7
  22.4 6.8 %all-to-all-start = ((f32[32,1,2688]{2,1,0:T(1,128)}), f32[32,1,2688]{2,1,0:T(1,128)S(1)}, u32[]{:S(2)}, u32[]{:S(2)}) async-start(f32[32,1,2688]{2,1,0:T(1,128)} %both_modes.1), calls=%async_computation | async-start | bytes 688128 | tf_op jit(solution)/shard_map/all_to_all | solution.py:727
  29.2 0.0 copy-done.7
  29.2 0.1 copy.10.prolong_ref
  29.3 0.0 copy-start
  29.3 0.7 %copy-done = f32[5,5]{1,0:T(8,128)S(1)} copy-done((f32[5,5]{1,0:T(8,128)S(1)}, f32[5,5]{1,0:T(8,128)}, u32[]{:S(2)}) %copy-start) | copy-done | bytes 124
  30.0 0.0 copy-start.2
  30.0 0.8 %copy-done.2 = f32[64,64]{1,0:T(8,128)S(1)} copy-done((f32[64,64]{1,0:T(8,128)S(1)}, f32[64,64]{1,0:T(8,128)}, u32[]{:S(2)}) %copy-start.2) | copy-done | bytes 16408
  30.8 0.0 copy-start.3
  30.8 0.8 %copy-done.3 = f32[64,96]{1,0:T(8,128)S(1)} copy-done((f32[64,96]{1,0:T(8,128)S(1)}, f32[64,96]{1,0:T(8,128)}, u32[]{:S(2)}) %copy-start.3) | copy-done | bytes 24600
  31.5 0.0 copy-start.4
  31.5 0.7 %copy-done.4 = f32[8,8]{1,0:T(8,128)S(1)} copy-done((f32[8,8]{1,0:T(8,128)S(1)}, f32[8,8]{1,0:T(8,128)}, u32[]{:S(2)}) %copy-start.4) | copy-done | bytes 280
  32.2 0.0 copy-start.5
  32.2 0.7 %copy-done.5 = f32[8,24]{1,0:T(8,128)S(1)} copy-done((f32[8,24]{1,0:T(8,128)S(1)}, f32[8,24]{1,0:T(8,128)}, u32[]{:S(2)}) %copy-start.5) | copy-done | bytes 792
  32.9 0.0 copy-start.6
  32.9 0.7 %copy-done.6 = f32[8,64]{1,0:T(8,128)S(1)} copy-done((f32[8,64]{1,0:T(8,128)S(1)}, f32[8,64]{1,0:T(8,128)}, u32[]{:S(2)}) %copy-start.6) | copy-done | bytes 2072
  33.6 5.0 %operators.1 = (bf16[256,256]{1,0:T(8,128)(2,1)S(1)}, bf16[512,256]{1,0:T(8,128)(2,1)S(1)}, bf16[512,256]{1,0:T(8,128)(2,1)S(1)}, bf16[640,256]{1,0:T(8,128)(2,1...) custom-call(f32[64,64]{1,0:T(8,128)S(1)} %copy-done.2, ...), custom_call_target="tpu_custom_call" | custom-call | flops 100000000 | bytes 3000000 | tf_op jit(solution)/shard_map/operators/pallas_call | solution.py:633
  38.6 3.4 %all-to-all-done.received_ref = f32[32,1,2688]{2,1,0:T(1,128)S(1)} async-done(((f32[32,1,2688]{2,1,0:T(1,128)}), f32[32,1,2688]{2,1,0:T(1,128)S(1)}, u32[]{:S(2)}, u32[]{:S(2)}) %all-to-all-start) | async-done | bytes 344096 | tf_op jit(solution)/shard_map/all_to_all | solution.py:727
  42.0 0.0 copy-start.1
  42.0 0.7 %copy-done.1 = f32[5,5]{1,0:T(8,128)S(1)} copy-done((f32[5,5]{1,0:T(8,128)S(1)}, f32[5,5]{1,0:T(8,128)}, u32[]{:S(2)}) %copy-start.1) | copy-done | bytes 124
  42.7 10.8 %iterate.1 = f32[32,1,1280]{2,1,0:T(1,128)S(1)} custom-call(f32[32,1,2688]{2,1,0:T(1,128)S(1)} %all-to-all-done.received_ref, bf16[256,256]{1,0:T(8,128)(2,1)S(1)} %get-tuple-element.17.fine_ref, bf16[512,256]{1,0:T(8,128)(2,1)S(1)} %get-tuple-element.18.chain_high_ref, bf16[512,256]{1,0:T(8,128)(2,1)S(1)} %get-tuple-element.19.chain_low_ref, ...), custom_call_target="tpu_custom_call" | custom-call | tf_op jit(solution)/shard_map/iterate/pallas_call | solution.py:651
  53.5 13.2 %all_to_all.10.modes_ref = f32[32,1,1280]{2,1,0:T(1,128)S(1)} all-to-all(f32[32,1,1280]{2,1,0:T(1,128)S(1)} %iterate.1), channel_id=1, replica_groups={{0,1,2,3,4,5,6,7,8,9,10,11,12,13,14,15,16,17,18,19,20,21,22,23,24,25,26..., dimensions={0} | all-to-all | bytes 327680 | tf_op jit(solution)/shard_map/all_to_all | solution.py:727
  66.7 1.3 %from_modes.1 = f32[1,5,64,128]{3,2,1,0:T(8,128)} custom-call(f32[32,1,1280]{2,1,0:T(1,128)S(1)} %all_to_all.10.modes_ref, f32[64,128]{1,0:T(8,128)S(1)} %get-tuple-element.26.basis_ref), custom_call_target="tpu_custom_call" | custom-call | tf_op jit(solution)/shard_map/from_modes/pallas_call | solution.py:735
Async XLA Ops:
  0.9 19.5 %collective-permute-start = (f32[326,128]{1,0:T(8,128)S(1)}, f32[326,128]{1,0:T(8,128)S(1)}, u32[]{:S(2)}, u32[]{:S(2)}) collective-permute-start(f32[326,128]{1,0:T(8,128)S(1)} %convert_add_fusion.own_ref), channel_id=1, source_target_pairs={{112,0},{113,1},{114,2},{115,3},{116,4},{117,5},{118,6},{119,7},{1... | collective-permute-start | bytes 500744 | tf_op jit(solution)/shard_map/ppermute | solution.py:700
  22.4 6.8 %copy-start.7 = (f32[64,8]{0,1:T(8,128)S(1)}, f32[64,8]{0,1:T(8,128)}, u32[]{:S(2)}) copy-start(f32[64,8]{0,1:T(8,128)} %param.17) | copy-start | bytes 6148
  22.4 19.6 %all-to-all-start = ((f32[32,1,2688]{2,1,0:T(1,128)}), f32[32,1,2688]{2,1,0:T(1,128)S(1)}, u32[]{:S(2)}, u32[]{:S(2)}) async-start(f32[32,1,2688]{2,1,0:T(1,128)} %both_modes.1), calls=%async_computation | async-start | bytes 688128 | tf_op jit(solution)/shard_map/all_to_all | solution.py:727
  29.3 0.7 %copy-start = (f32[5,5]{1,0:T(8,128)S(1)}, f32[5,5]{1,0:T(8,128)}, u32[]{:S(2)}) copy-start(f32[5,5]{1,0:T(8,128)} %mixing_ref.3) | copy-start | bytes 304
  30.0 0.8 %copy-start.2 = (f32[64,64]{1,0:T(8,128)S(1)}, f32[64,64]{1,0:T(8,128)}, u32[]{:S(2)}) copy-start(f32[64,64]{1,0:T(8,128)} %volume_ref.1) | copy-start | bytes 49156
  30.8 0.8 %copy-start.3 = (f32[64,96]{1,0:T(8,128)S(1)}, f32[64,96]{1,0:T(8,128)}, u32[]{:S(2)}) copy-start(f32[64,96]{1,0:T(8,128)} %lift_ref.1) | copy-start | bytes 73732
  31.5 0.7 %copy-start.4 = (f32[8,8]{1,0:T(8,128)S(1)}, f32[8,8]{1,0:T(8,128)}, u32[]{:S(2)}) copy-start(f32[8,8]{1,0:T(8,128)} %coarse_volume_ref.1) | copy-start | bytes 772
  32.2 0.7 %copy-start.5 = (f32[8,24]{1,0:T(8,128)S(1)}, f32[8,24]{1,0:T(8,128)}, u32[]{:S(2)}) copy-start(f32[8,24]{1,0:T(8,128)} %coarse_lift_ref.1) | copy-start | bytes 2308
  32.9 0.7 %copy-start.6 = (f32[8,64]{1,0:T(8,128)S(1)}, f32[8,64]{1,0:T(8,128)}, u32[]{:S(2)}) copy-start(f32[8,64]{1,0:T(8,128)} %restrict_ref.1) | copy-start | bytes 6148
  42.0 0.7 %copy-start.1 = (f32[5,5]{1,0:T(8,128)S(1)}, f32[5,5]{1,0:T(8,128)}, u32[]{:S(2)}) copy-start(f32[5,5]{1,0:T(8,128)} %mixing_ref.3) | copy-start | bytes 304

commit v4 on v3

--- a/solution.py
+++ b/solution.py
@@ -19,7 +19,7 @@
 EXACT = lax.Precision.HIGHEST
 F32 = jnp.float32
 BF16 = jnp.bfloat16
-VMEM_LIMIT = 48 * 1024 * 1024
+VMEM_LIMIT = 20 * 1024 * 1024
 
 
 def iota(shape, dim):
@@ -86,13 +86,12 @@
     return along_x.astype(jnp.int32), along_y.astype(jnp.int32), extra
 
 
-def layer_modes(ref, where, places, first_slot):
+def layer_modes(ref, links, where, places, first_slot):
     upper = iota((1, 128), 1) >= LAYER
     halved = iota((UNITS, 128), 1) >= LAYER
     mode = iota((LAYER, 128), 0)
     kx, ky, kx_other, ky_other, paired = wave_numbers(mode & (UNITS - 1))
     second = mode >= UNITS
-    links = ref[FIELDS * LAYER :].astype(jnp.int32)
     along_x, along_y, extra = grid_places(links, where * 2 * LAYER, places * 2 * LAYER, first_slot)
     turns = jnp.where(second, kx_other, kx) * along_x + jnp.where(second, ky_other, ky) * along_y
     basis = eighth_cos(turns + jnp.where(second, 2 * paired, 0))
@@ -113,8 +112,8 @@
     return basis, of_field, extra
 
 
-def own_modes_kernel(own_ref, modes_ref, basis_ref):
-    basis, of_field, extra = layer_modes(own_ref, lax.axis_index("space"), lax.axis_size("space"), 0)
+def own_modes_kernel(own_ref, links_ref, modes_ref, basis_ref):
+    basis, of_field, extra = layer_modes(own_ref, links_ref[...], lax.axis_index("space"), lax.axis_size("space"), 0)
     basis_ref[...] = basis
     for field in range(FIELDS):
         for index, value in enumerate(of_field(field)):
@@ -123,7 +122,7 @@
     modes_ref[:, STATE:] = jnp.broadcast_to(extra, (UNITS, 128))
 
 
-def both_modes_kernel(own_ref, beside_ref, sent_ref, blocks, semaphores):
+def both_modes_kernel(own_ref, beside_ref, links_ref, sent_ref, blocks, semaphores):
     place = lax.axis_index("space")
     places = lax.axis_size("space")
     partner = (jnp.where(((place >> 3) & 3) < 2, place - EDGE, place + EDGE) + places) % places
@@ -131,7 +130,7 @@
         blocks[:, 0, column : column + 128] = own_ref[:, column : column + 128]
     first = pltpu.make_async_copy(blocks.at[:, :, :STATE], sent_ref.at[:, :, :STATE], semaphores.at[0])
     first.start()
-    _, of_field, extra = layer_modes(beside_ref, partner, places, 4)
+    _, of_field, extra = layer_modes(beside_ref, links_ref[...], partner, places, 4)
     for field in range(FIELDS):
         for index, value in enumerate(of_field(field)):
             column = STATE + (field * 2 + index) * 128
@@ -143,7 +142,8 @@
     second.wait()
 
 
-def from_modes_kernel(modes_ref, basis_ref, out_ref):
+def from_modes_kernel(modes_ref, basis_ref, out_ref, fields, semaphores):
+    copies = []
     unit = iota((LAYER, 128), 0) & (UNITS - 1)
     scale = jnp.where(unit < 30, 2.0 / LAYER, 1.0 / LAYER).astype(F32)
     back = basis_ref[...] * scale
@@ -156,7 +156,11 @@
         real = jnp.where(halved, pltpu.roll(odd, 64, 1), even)
         imaginary = jnp.where(halved, odd, pltpu.roll(even, 64, 1))
         whole = nn(jnp.transpose(jnp.concatenate([real, imaginary], axis=0)), back)
-        out_ref[0, field] = jnp.where(upper, whole[LAYER:], whole[:LAYER])
+        fields[field] = jnp.where(upper, whole[LAYER:], whole[:LAYER])
+        copies.append(pltpu.make_async_copy(fields.at[field], out_ref.at[0, field], semaphores.at[field]))
+        copies[-1].start()
+    for copy in copies:
+        copy.wait()
 
 
 SHIFTS_A = (0, 1, -1, 2, -2)
@@ -166,6 +170,8 @@
 NEAR = len(SHIFTS_A) + len(SHIFTS_B)
 BLOCKS = NEAR + len(FAR_A) + len(FAR_B)
 RING = 8
+ENTRIES = 256 + FIELDS * 128
+PACKED = ((0, 64, 64), (64, 64, 96), (128, 8, 8), (136, 8, 24), (144, FIELDS, FIELDS), (152, 8, 64), (160, 64, 8))
 
 
 def face_weights(shape, per_edge, node, weights):
@@ -193,43 +199,21 @@
 
 
 def operators_kernel(
-    volume_ref,
-    lift_ref,
-    coarse_volume_ref,
-    coarse_lift_ref,
-    mixing_ref,
-    restrict_ref,
-    prolong_ref,
-    fine_ref,
+    packed_ref,
+    level_ref,
     chain_high_ref,
     chain_low_ref,
-    restrict_all_ref,
     prolong_high_ref,
     prolong_low_ref,
     near_high_ref,
     near_low_ref,
     far_ref,
-    *scratch,
 ):
-    *held, semaphores = scratch
-    operands = (
-        volume_ref,
-        lift_ref,
-        coarse_volume_ref,
-        coarse_lift_ref,
-        mixing_ref,
-        restrict_ref,
-        prolong_ref,
+    volume, lift, coarse_volume, clift, mixing, restriction, prolongation = (
+        packed_ref[first : first + rows, :columns] for first, rows, columns in PACKED
     )
-    copies = [
-        pltpu.make_async_copy(operand, place_for, semaphores.at[index])
-        for index, (operand, place_for) in enumerate(zip(operands, held))
-    ]
-    for copy in copies:
-        copy.start()
-    for copy in copies:
-        copy.wait()
-    volume_ref, lift_ref, coarse_volume_ref, coarse_lift_ref, mixing_ref, restrict_ref, prolong_ref = held
+    fine_ref = level_ref.at[:256]
+    restrict_all_ref = level_ref.at[256:ENTRIES]
     place = lax.axis_index("space")
     kx, ky, kx_other, ky_other, paired = wave_numbers(place & (UNITS - 1))
     single = paired == 0
@@ -262,8 +246,8 @@
         (128, 96), 4, row & 63, {0: -sin_x * sign, 1: sin_x * sign, 2: -sin_y * sign, 3: sin_y * sign}
     )
     ahead = face_weights((128, 96), 4, row & 63, {4: 1.0, 5: 1.0})
-    lift2 = jnp.concatenate([lift_ref[...]] * 2, axis=0)
-    volume2 = jnp.concatenate([volume_ref[...]] * 2, axis=0)
+    lift2 = jnp.concatenate([lift] * 2, axis=0)
+    volume2 = jnp.concatenate([volume] * 2, axis=0)
     twice = jnp.where((iota((128, 64), 0) & 63) == iota((128, 64), 1), 1.0, 0.0).astype(F32)
     inside = (DT / 2) * jnp.where(same, nt(twice, volume2) + nt(along, lift2), nt(across, lift2))
     beside = (DT / 2) * jnp.where(same, nt(ahead, lift2), 0.0)
@@ -284,14 +268,22 @@
     node8 = jnp.where((iota((128, 8), 0) & 7) == iota((128, 8), 1), 1.0, 0.0).astype(F32)
     field8 = jnp.where((iota((128, FIELDS), 0) >> 4) == iota((128, FIELDS), 1), 1.0, 0.0).astype(F32)
     same = ((wide >> 3) & 1) == ((tall >> 3) & 1)
-    clift = coarse_lift_ref[...]
-    mixing = mixing_ref[...]
+    number = iota((32, FIELDS), 0)
+    entries = nn(jnp.where(number // FIELDS == iota((32, FIELDS), 1), 1.0, 0.0).astype(F32), mixing)
+    entries = jnp.where(number % FIELDS == iota((32, FIELDS), 1), entries, 0.0)
+    entries = jnp.broadcast_to(jnp.sum(entries, axis=1, keepdims=True), (32, 128))
+    high, middle = split(entries)
+    low = (entries - high.astype(F32) - middle.astype(F32)).astype(BF16)
+    level_ref[ENTRIES : ENTRIES + 32, :128] = high
+    level_ref[ENTRIES : ENTRIES + 32, 128:] = middle
+    level_ref[ENTRIES + 32 :, :128] = low
+    level_ref[ENTRIES + 32 :, 128:] = jnp.zeros((32, 128), BF16)
     power = nt(field8, mixing)
     coupled = [nt(field8, field8), nt(power, field8)]
     for _ in range(2):
         power = nt(power, mixing)
         coupled.append(nt(power, field8))
-    along = nt(nt(node8, coarse_volume_ref[...]) + nt(along, clift), node8)
+    along = nt(nt(node8, coarse_volume) + nt(along, clift), node8)
     across = nt(nt(across, clift), node8)
     ahead = nt(nt(ahead, clift), node8)
     level = DT * coupled[1] * jnp.where(same, along, across)
@@ -314,8 +306,8 @@
         put(chain_high_ref, chain_low_ref, rows, slice(0, 128), once[block])
         put(chain_high_ref, chain_low_ref, rows, slice(128, 256), 0.5 * squared[block])
 
-    restricting = nt(twice, nn(node8, restrict_ref[...]))
-    prolonging = nt(node8, jnp.concatenate([prolong_ref[...]] * 2, axis=0))
+    restricting = nt(twice, nn(node8, restriction))
+    prolonging = nt(node8, jnp.concatenate([prolongation] * 2, axis=0))
     down = (tall >= 64) == (((wide >> 3) & 1) == 1)
     up = (wide >= 64) == (((tall >> 3) & 1) == 1)
     restricting = jnp.where(down, restricting, 0.0)
@@ -323,7 +315,9 @@
     for field in range(FIELDS):
         part = slice(field * 128, (field + 1) * 128)
         put_packed(restrict_all_ref, part, jnp.where((wide >> 4) == field, restricting, 0.0))
-        put(prolong_high_ref, prolong_low_ref, slice(0, 128), part, jnp.where((tall >> 4) == field, prolonging, 0.0))
+        value = jnp.where((tall >> 4) == field, prolonging, 0.0)
+        put(prolong_high_ref, prolong_low_ref, slice(0, 128), part, value)
+        prolong_high_ref[128:, part] = value.astype(BF16)
 
     response = jnp.where(tall < 16, prolonging, 0.0)
     fine_below = (wide & 3) == 3
@@ -399,17 +393,16 @@
 def iterate_kernel(
     slices,
     received_ref,
-    fine_ref,
+    level_ref,
     chain_high_ref,
     chain_low_ref,
-    restrict_all_ref,
     prolong_high_ref,
     prolong_low_ref,
     near_high_ref,
     near_low_ref,
     far_ref,
+    sent_ref,
     mixing_ref,
-    sent_ref,
     start,
     head1,
     rate1,
@@ -417,11 +410,14 @@
     rate2,
     ends,
     ends_rate,
-    mixing_smem,
-    semaphore,
 ):
-    fetch = pltpu.make_async_copy(mixing_ref, mixing_smem, semaphore)
-    fetch.start()
+    fine_ref = level_ref.at[:256]
+    restrict_all_ref = level_ref.at[256:ENTRIES]
+    mixing_ref[...] = (
+        level_ref[ENTRIES : ENTRIES + 32, :128].astype(F32)
+        + level_ref[ENTRIES : ENTRIES + 32, 128:].astype(F32)
+        + level_ref[ENTRIES + 32 :, :128].astype(F32)
+    )
     place = lax.axis_index("space")
     mine = lax.axis_index("tm")
     kx, ky, kx_other, ky_other, paired = wave_numbers(place & (UNITS - 1))
@@ -448,9 +444,10 @@
         parts = fields_of(state)
         pieces = []
         for field in range(FIELDS):
-            mixed = mixing_smem[field, 0] * parts[0]
+            first = field * FIELDS
+            mixed = mixing_ref[first : first + 1] * parts[0]
             for other in range(1, FIELDS):
-                mixed = mixed + mixing_smem[field, other] * parts[other]
+                mixed = mixed + mixing_ref[first + other : first + other + 1] * parts[other]
             pieces.append(jnp.concatenate([mixed, beside_layers(mixed, fine_below[: len(mixed) // 2])], axis=1))
         return packed_dot(jnp.concatenate(pieces, axis=0), fine_ref[...])
 
@@ -499,8 +496,6 @@
             begin = field * 128 + index * LAYER
             start[begin : begin + LAYER] = value * cos + pltpu.roll(value, 64, 1) * sin
 
-    fetch.wait()
-
     initial = start[...]
     power = psi(initial)
     begin = restrict(initial)
@@ -546,7 +541,9 @@
             if table[name][order] != 0.0:
                 term = table[name][order] * value
                 total = term if total is None else total + term
-        wide = dot3(total, prolong_high_ref[...], prolong_low_ref[...])
+        high, low = split(total)
+        wide = bdot(jnp.concatenate([high, low], axis=1), prolong_high_ref[...])
+        wide = wide + bdot(high, prolong_low_ref[...])
         wide = jnp.concatenate([wide[:, f * 128 : (f + 1) * 128] for f in range(FIELDS)], axis=0)
         weight = jnp.where(mine > 0, table["later"][order], table["first"][order]).astype(F32)
         return wide + weight * initial_around
@@ -615,57 +612,53 @@
 
 
 IN_VMEM = pl.BlockSpec(memory_space=pltpu.VMEM)
-ANYWHERE = pl.BlockSpec(memory_space=pltpu.HBM)
 
 
 def operators_call(volume_op, lift_op, coarse_volume, coarse_lift, mixing, restrict_op, prolong_op):
     shapes = [
-        (256, 256),
+        (ENTRIES + 64, 256),
         (512, 256),
         (512, 256),
-        (FIELDS * 128, 256),
-        (128, FIELDS * 128),
+        (256, FIELDS * 128),
         (128, FIELDS * 128),
         (NEAR * 128, 256),
         (NEAR * 128, 256),
         (BLOCKS * 128, 256),
     ]
+    operands = (volume_op, lift_op, coarse_volume, coarse_lift, mixing, restrict_op, prolong_op)
+    packed = jnp.zeros((224, 128), F32)
+    for operand, (first, rows, columns) in zip(operands, PACKED):
+        packed = packed + jnp.pad(operand, ((first, 224 - first - rows), (0, 128 - columns)))
     return pl.pallas_call(
         operators_kernel,
         out_shape=[jax.ShapeDtypeStruct(shape, BF16) for shape in shapes],
-        in_specs=[ANYWHERE] * 7,
+        in_specs=[IN_VMEM],
         out_specs=[IN_VMEM] * len(shapes),
-        scratch_shapes=[
-            pltpu.VMEM(operand.shape, F32)
-            for operand in (volume_op, lift_op, coarse_volume, coarse_lift, mixing, restrict_op, prolong_op)
-        ]
-        + [pltpu.SemaphoreType.DMA((7,))],
         compiler_params=pltpu.CompilerParams(vmem_limit_bytes=VMEM_LIMIT),
         cost_estimate=pl.CostEstimate(flops=10**8, bytes_accessed=3 * 10**6, transcendentals=0),
         name="operators",
-    )(volume_op, lift_op, coarse_volume, coarse_lift, mixing, restrict_op, prolong_op)
-
-
-def iterate_kernel_call(slices, received, operators, mixing):
+    )(packed)
+
+
+def iterate_kernel_call(slices, received, operators):
     coarse_shape = pltpu.VMEM((slices + 1, 128, 128), F32)
     return pl.pallas_call(
         functools.partial(iterate_kernel, slices),
         out_shape=jax.ShapeDtypeStruct((UNITS, 1, STATE), F32),
-        in_specs=[IN_VMEM] * (1 + len(operators)) + [ANYWHERE],
+        in_specs=[IN_VMEM] * (1 + len(operators)),
         out_specs=IN_VMEM,
-        scratch_shapes=[pltpu.VMEM((FIELDS * 128, 128), F32)]
-        + [coarse_shape] * 6
-        + [pltpu.SMEM((FIELDS, FIELDS), F32), pltpu.SemaphoreType.DMA],
+        scratch_shapes=[pltpu.VMEM((32, 128), F32), pltpu.VMEM((FIELDS * 128, 128), F32)]
+        + [coarse_shape] * 6,
         compiler_params=pltpu.CompilerParams(vmem_limit_bytes=VMEM_LIMIT),
         name="iterate",
-    )(received, *operators, mixing)
+    )(received, *operators)
 
 
 def iterate_call(slices, received, volume_op, lift_op, coarse_volume, coarse_lift, mixing, restrict_op, prolong_op):
     operators = operators_call(
         volume_op, lift_op, coarse_volume, coarse_lift, mixing, restrict_op, prolong_op
     )
-    return iterate_kernel_call(slices, received[:, None, :], operators, mixing)
+    return iterate_kernel_call(slices, received[:, None, :], operators)
 
 
 def window_partners(slices, places):
@@ -694,25 +687,25 @@
     prolong_op,
 ):
     params = pltpu.CompilerParams(vmem_limit_bytes=VMEM_LIMIT)
-    rows = FIELDS * LAYER
-    own = jnp.pad(initial.reshape(rows, -1), ((0, len(neighbours)), (0, 0)))
-    own = own + jnp.pad(neighbours, ((rows, 0), (0, 0))).astype(F32)
-    beside = lax.ppermute(own, ("tm", "space"), window_partners(lax.axis_size("tm"), lax.axis_size("space")))
+    route = window_partners(lax.axis_size("tm"), lax.axis_size("space"))
+    state = initial.reshape(FIELDS * LAYER, -1)
+    state_beside = lax.ppermute(state, ("tm", "space"), route)
+    links_beside = lax.ppermute(neighbours, ("tm", "space"), route)
     modes, basis = pl.pallas_call(
         own_modes_kernel,
         out_shape=(
             jax.ShapeDtypeStruct((UNITS, STATE + 128), F32),
             jax.ShapeDtypeStruct((LAYER, 128), F32),
         ),
-        in_specs=[IN_VMEM],
+        in_specs=[IN_VMEM] * 2,
         out_specs=(IN_VMEM, IN_VMEM),
         compiler_params=params,
         name="own_modes",
-    )(own)
+    )(state, neighbours)
     sent = pl.pallas_call(
         both_modes_kernel,
         out_shape=jax.ShapeDtypeStruct((UNITS, 1, 2 * STATE + 128), F32),
-        in_specs=[IN_VMEM] * 2,
+        in_specs=[IN_VMEM] * 3,
         out_specs=pl.BlockSpec(memory_space=pl.ANY),
         scratch_shapes=[
             pltpu.VMEM((UNITS, 1, 2 * STATE + 128), F32),
@@ -720,7 +713,7 @@
         ],
         compiler_params=params,
         name="both_modes",
-    )(modes, beside)
+    )(modes, state_beside, links_beside)
     windows = [[first + i for i in range(UNITS)] for first in range(0, lax.axis_size("space"), UNITS)]
 
     def exchange(blocks):
@@ -730,13 +723,14 @@
     operators = operators_call(
         volume_op, lift_op, coarse_volume, coarse_lift, mixing, restrict_op, prolong_op
     )
-    modes = iterate_kernel_call(lax.axis_size("tm"), received, operators, mixing)
+    modes = iterate_kernel_call(lax.axis_size("tm"), received, operators)
     returned = exchange(modes)
     return pl.pallas_call(
         from_modes_kernel,
         out_shape=jax.ShapeDtypeStruct((1, FIELDS, LAYER, 128), F32),
         in_specs=[IN_VMEM] * 2,
-        out_specs=IN_VMEM,
+        out_specs=pl.BlockSpec(memory_space=pl.ANY),
+        scratch_shapes=[pltpu.VMEM((FIELDS, LAYER, 128), F32), pltpu.SemaphoreType.DMA((FIELDS,))],
         compiler_params=params,
         name="from_modes",
     )(returned, basis)

time: 68.5 us -> 67.7 us (0.988)
  starting transfers between devices: 19.2 us -> 21.2 us
  local copies, waits for them, and re-layouts: 5.04 us -> 3.92 us
  other arithmetic: 0.94 us -> 0.01 us
    ppermute x1 -> x2, waiting for transfers between devices: 5.85 us -> 2.55 us  [the longest x1 2.55 us: on_device(): links_beside = lax.ppermute(neighbours, ('tm', 'space'), route)]
    all_to_all x1, waiting for transfers between devices: 3.44 us -> 6.5 us  [exchange(): lax.all_to_all(blocks, 'space', 0, 0, axis_index_groups=windows, tiled=True)]
    ppermute x1 -> x2, starting transfers between devices: 12.4 us -> 14.3 us  [the longest x1 12.4 us: on_device(): state_beside = lax.ppermute(state, ('tm', 'space'), route)]
    unnamed x17 -> x23, local copies, waits for them, and re-layouts: 5.04 us -> 3.92 us
    add x1, other arithmetic: 0.94 us -> 0.01 us  [operators_call(): packed + jnp.pad(operand, ((first, 224 - first - rows), (0, 128 - columns)))]
  transfers between devices with their start and end apart: 2 -> 3, of which waited for: 2 -> 2; matrix products, arithmetic and copies ran while one was open for 0% -> 0% of each run, Pallas kernels for 9% -> 9%
where the time goes in v4:
time: 67.7 us; the launch traced here: 67.2 us
  starting transfers between devices  21.2 us (31%)
  Pallas kernels  19.9 us (29%)
  blocking collectives  12.8 us (19%)
  waiting for transfers between devices  9.06 us (13%)
  local copies, waits for them, and re-layouts  3.92 us (6%)
    all_to_all x1, blocking collectives, exchange(): lax.all_to_all(blocks, 'space', 0, 0, axis_index_groups=windows, tiled=True)  12.8 us
    ppermute x1, starting transfers between devices, on_device(): state_beside = lax.ppermute(state, ('tm', 'space'), route)  12.4 us
    pallas_call x1, Pallas kernels, iterate_kernel_call(): pl.pallas_call(functools.partial(iterate_kernel, slices), out_shape=jax.S...  10.7 us
    all_to_all x1, starting transfers between devices, exchange(): lax.all_to_all(blocks, 'space', 0, 0, axis_index_groups=windows, tiled=True)  6.87 us
    all_to_all x1, waiting for transfers between devices, exchange(): lax.all_to_all(blocks, 'space', 0, 0, axis_index_groups=windows, tiled=True)  6.5 us
    pallas_call x1, Pallas kernels, operators_call(): pl.pallas_call(operators_kernel, out_shape=[jax.ShapeDtypeStruct(shape, B...  4.81 us
    unnamed x23, local copies, waits for them, and re-layouts  3.92 us
    ppermute x1, waiting for transfers between devices, on_device(): links_beside = lax.ppermute(neighbours, ('tm', 'space'), route)  2.55 us
  transfers between devices with their start and end apart: 3, of which 2 were waited for; matrix products, arithmetic and copies ran while one was open for 0% of the time, Pallas kernels for 9%

profile of v4, /device:TPU:1, one launch (start us, length us, event | category | flops | bytes accessed | tf_op | source)
XLA Modules:
  0.0 67.2 jit_solution(14105745147792093195)
XLA Ops:
  0.0 12.4 %collective-permute-start = (f32[320,128]{1,0:T(8,128)}, f32[320,128]{1,0:T(8,128)S(1)}, u32[]{:S(2)}, u32[]{:S(2)}) collective-permute-start(f32[320,128]{1,0:T(8,128)} %bitcast.1), channel_id=1, source_target_pairs={{112,0},{113,1},{114,2},{115,3},{116,4},{117,5},{118,6},{119,7},{1... | collective-permute-start | bytes 491528 | tf_op jit(solution)/shard_map/ppermute | solution.py:692
  12.4 1.9 %collective-permute-start.1 = (s32[6,128]{1,0:T(8,128)}, s32[6,128]{1,0:T(8,128)S(1)}, u32[]{:S(2)}, u32[]{:S(2)}) collective-permute-start(s32[6,128]{1,0:T(8,128)} %links_ref.1), channel_id=1, source_target_pairs={{112,0},{113,1},{114,2},{115,3},{116,4},{117,5},{118,6},{119,7},{1... | collective-permute-start | bytes 9224 | tf_op jit(solution)/shard_map/ppermute | solution.py:693
  14.3 0.0 copy-start
  14.3 0.9 %copy-done = f32[5,64,128]{2,1,0:T(8,128)S(1)} copy-done((f32[5,64,128]{2,1,0:T(8,128)S(1)}, f32[5,64,128]{2,1,0:T(8,128)}, u32[]{:S(2)}) %copy-start) | copy-done | bytes 163864
  15.2 0.7 %copy-done.3 = s32[6,128]{1,0:T(8,128)S(1)} copy-done((s32[6,128]{1,0:T(8,128)S(1)}, s32[6,128]{1,0:T(8,128)}, u32[]{:S(2)}) %copy-start.3) | copy-done | bytes 3096
  15.9 1.2 %own_modes.1 = (f32[32,1408]{1,0:T(8,128)S(1)}, f32[64,128]{1,0:T(8,128)S(1)}) custom-call(f32[320,128]{1,0:T(8,128)S(1)} %bitcast.2, s32[6,128]{1,0:T(8,128)S(1)} %copy-done.3), custom_call_target="tpu_custom_call" | custom-call | tf_op jit(solution)/shard_map/own_modes/pallas_call | solution.py:694
  17.2 2.6 %collective-permute-done.1.links_ref = s32[6,128]{1,0:T(8,128)S(1)} collective-permute-done((s32[6,128]{1,0:T(8,128)}, s32[6,128]{1,0:T(8,128)S(1)}, u32[]{:S(2)}, u32[]{:S(2)}) %collective-permute-start.1) | collective-permute-done | bytes 3104 | tf_op jit(solution)/shard_map/ppermute | solution.py:693
  19.7 0.0 collective-permute-done.beside_ref
  19.7 2.0 %both_modes.1 = f32[32,1,2688]{2,1,0:T(1,128)} custom-call(f32[32,1408]{1,0:T(8,128)S(1)} %get-tuple-element.15.own_ref, f32[320,128]{1,0:T(8,128)S(1)} %collective-permute-done.beside_ref, s32[6,128]{1,0:T(8,128)S(1)} %collective-permute-done.1.links_ref), custom_call_target="tpu_custom_call" | custom-call | tf_op jit(solution)/shard_map/both_modes/pallas_call | solution.py:705
  21.7 0.0 copy-start.10
  21.7 0.0 copy-start.5
  21.7 0.0 copy-start.7
  21.7 0.0 copy-start.8
  21.7 0.0 copy-start.9
  21.8 6.9 %all-to-all-start = ((f32[32,1,2688]{2,1,0:T(1,128)}), f32[32,1,2688]{2,1,0:T(1,128)S(1)}, u32[]{:S(2)}, u32[]{:S(2)}) async-start(f32[32,1,2688]{2,1,0:T(1,128)} %both_modes.1), calls=%async_computation | async-start | bytes 688128 | tf_op jit(solution)/shard_map/all_to_all | solution.py:720
  28.6 0.0 copy-done.10
  28.6 0.0 copy-start.4
  28.7 0.0 copy-start.6
  28.7 0.1 copy.10
  28.8 0.0 copy-done.5
  28.8 0.0 copy-done.7
  28.8 0.0 copy-done.8
  28.8 0.6 copy-done.4
  29.4 0.0 copy-done.6
  29.4 4.8 %operators.1 = (bf16[960,256]{1,0:T(8,128)(2,1)S(1)}, bf16[512,256]{1,0:T(8,128)(2,1)S(1)}, bf16[512,256]{1,0:T(8,128)(2,1)S(1)}, bf16[256,640]{1,0:T(8,128)(2,1...) custom-call(f32[224,128]{1,0:T(8,128)S(1)} %pad_add_fusion.packed_ref), custom_call_target="tpu_custom_call" | custom-call | flops 100000000 | bytes 3000000 | tf_op jit(solution)/shard_map/operators/pallas_call | solution.py:632
  34.2 0.0 copy-start.1
  34.3 0.7 copy-done.1
  34.9 6.5 %all-to-all-done.received_ref = f32[32,1,2688]{2,1,0:T(1,128)S(1)} async-done(((f32[32,1,2688]{2,1,0:T(1,128)}), f32[32,1,2688]{2,1,0:T(1,128)S(1)}, u32[]{:S(2)}, u32[]{:S(2)}) %all-to-all-start) | async-done | bytes 344096 | tf_op jit(solution)/shard_map/all_to_all | solution.py:720
  41.4 0.9 %copy-done.2 = bf16[128,640]{1,0:T(8,128)(2,1)S(1)} copy-done((bf16[128,640]{1,0:T(8,128)(2,1)S(1)}, bf16[128,640]{1,0:T(8,128)(2,1)}, u32[]{:S(2)}) %copy-start.2) | copy-done | bytes 163864
  42.3 10.7 %iterate.1 = f32[32,1,1280]{2,1,0:T(1,128)S(1)} custom-call(f32[32,1,2688]{2,1,0:T(1,128)S(1)} %all-to-all-done.received_ref, bf16[960,256]{1,0:T(8,128)(2,1)S(1)} %get-tuple-element.16.level_ref, bf16[512,256]{1,0:T(8,128)(2,1)S(1)} %get-tuple-element.17.chain_high_ref, bf16[512,256]{1,0:T(8,128)(2,1)S(1)} %get-tuple-element.18.chain_low_ref, ...), custom_call_target="tpu_custom_call" | custom-call | tf_op jit(solution)/shard_map/iterate/pallas_call | solution.py:645
  53.0 12.8 %all_to_all.10.modes_ref = f32[32,1,1280]{2,1,0:T(1,128)S(1)} all-to-all(f32[32,1,1280]{2,1,0:T(1,128)S(1)} %iterate.1), channel_id=1, replica_groups={{0,1,2,3,4,5,6,7,8,9,10,11,12,13,14,15,16,17,18,19,20,21,22,23,24,25,26..., dimensions={0} | all-to-all | bytes 327680 | tf_op jit(solution)/shard_map/all_to_all | solution.py:720
  65.8 1.3 %from_modes.1 = f32[1,5,64,128]{3,2,1,0:T(8,128)} custom-call(f32[32,1,1280]{2,1,0:T(1,128)S(1)} %all_to_all.10.modes_ref, f32[64,128]{1,0:T(8,128)S(1)} %get-tuple-element.24.basis_ref), custom_call_target="tpu_custom_call" | custom-call | tf_op jit(solution)/shard_map/from_modes/pallas_call | solution.py:728
  (4 shorter events, 0.0 us)
Async XLA Ops:
  0.0 19.7 %collective-permute-start = (f32[320,128]{1,0:T(8,128)}, f32[320,128]{1,0:T(8,128)S(1)}, u32[]{:S(2)}, u32[]{:S(2)}) collective-permute-start(f32[320,128]{1,0:T(8,128)} %bitcast.1), channel_id=1, source_target_pairs={{112,0},{113,1},{114,2},{115,3},{116,4},{117,5},{118,6},{119,7},{1... | collective-permute-start | bytes 491528 | tf_op jit(solution)/shard_map/ppermute | solution.py:692
  12.4 7.3 %collective-permute-start.1 = (s32[6,128]{1,0:T(8,128)}, s32[6,128]{1,0:T(8,128)S(1)}, u32[]{:S(2)}, u32[]{:S(2)}) collective-permute-start(s32[6,128]{1,0:T(8,128)} %links_ref.1), channel_id=1, source_target_pairs={{112,0},{113,1},{114,2},{115,3},{116,4},{117,5},{118,6},{119,7},{1... | collective-permute-start | bytes 9224 | tf_op jit(solution)/shard_map/ppermute | solution.py:693
  14.3 0.9 %copy-start = (f32[5,64,128]{2,1,0:T(8,128)S(1)}, f32[5,64,128]{2,1,0:T(8,128)}, u32[]{:S(2)}) copy-start(f32[5,64,128]{2,1,0:T(8,128)} %param.9) | copy-start | bytes 491524
  15.2 0.7 %copy-start.3 = (s32[6,128]{1,0:T(8,128)S(1)}, s32[6,128]{1,0:T(8,128)}, u32[]{:S(2)}) copy-start(s32[6,128]{1,0:T(8,128)} %links_ref.1) | copy-start | bytes 9220
  21.7 6.9 %copy-start.10 = (f32[64,8]{0,1:T(8,128)S(1)}, f32[64,8]{0,1:T(8,128)}, u32[]{:S(2)}) copy-start(f32[64,8]{0,1:T(8,128)} %param.17) | copy-start | bytes 6148
  21.7 7.0 %copy-start.5 = (f32[64,64]{1,0:T(8,128)S(1)}, f32[64,64]{1,0:T(8,128)}, u32[]{:S(2)}) copy-start(f32[64,64]{1,0:T(8,128)} %param.11) | copy-start | bytes 49156
  21.7 7.0 %copy-start.7 = (f32[5,5]{1,0:T(8,128)S(1)}, f32[5,5]{1,0:T(8,128)}, u32[]{:S(2)}) copy-start(f32[5,5]{1,0:T(8,128)} %param.15) | copy-start | bytes 304
  21.7 7.0 %copy-start.8 = (f32[8,24]{1,0:T(8,128)S(1)}, f32[8,24]{1,0:T(8,128)}, u32[]{:S(2)}) copy-start(f32[8,24]{1,0:T(8,128)} %param.14) | copy-start | bytes 2308
  21.7 7.0 %copy-start.9 = (f32[8,8]{1,0:T(8,128)S(1)}, f32[8,8]{1,0:T(8,128)}, u32[]{:S(2)}) copy-start(f32[8,8]{1,0:T(8,128)} %param.13) | copy-start | bytes 772
  21.8 19.7 %all-to-all-start = ((f32[32,1,2688]{2,1,0:T(1,128)}), f32[32,1,2688]{2,1,0:T(1,128)S(1)}, u32[]{:S(2)}, u32[]{:S(2)}) async-start(f32[32,1,2688]{2,1,0:T(1,128)} %both_modes.1), calls=%async_computation | async-start | bytes 688128 | tf_op jit(solution)/shard_map/all_to_all | solution.py:720
  28.6 0.8 %copy-start.4 = (f32[64,96]{1,0:T(8,128)S(1)}, f32[64,96]{1,0:T(8,128)}, u32[]{:S(2)}) copy-start(f32[64,96]{1,0:T(8,128)} %param.12) | copy-start | bytes 73732
  28.7 0.8 %copy-start.6 = (f32[8,64]{1,0:T(8,128)S(1)}, f32[8,64]{1,0:T(8,128)}, u32[]{:S(2)}) copy-start(f32[8,64]{1,0:T(8,128)} %param.16) | copy-start | bytes 6148
  34.2 0.7 copy-start.1
  41.4 0.9 %copy-start.2 = (bf16[128,640]{1,0:T(8,128)(2,1)S(1)}, bf16[128,640]{1,0:T(8,128)(2,1)}, u32[]{:S(2)}) copy-start(bf16[128,640]{1,0:T(8,128)(2,1)} %copy-done.1) | copy-start | bytes 491524

commit v5 on v4

--- a/solution.py
+++ b/solution.py
@@ -112,41 +112,52 @@
     return basis, of_field, extra
 
 
-def own_modes_kernel(own_ref, links_ref, modes_ref, basis_ref):
-    basis, of_field, extra = layer_modes(own_ref, links_ref[...], lax.axis_index("space"), lax.axis_size("space"), 0)
-    basis_ref[...] = basis
+def own_modes_kernel(own_ref, links_ref, sent_ref, basis_ref, blocks, semaphore):
+    basis, modes_of, extra = layer_modes(own_ref, links_ref[...], lax.axis_index("space"), lax.axis_size("space"), 0)
     for field in range(FIELDS):
-        for index, value in enumerate(of_field(field)):
+        for index, value in enumerate(modes_of(field)):
             column = (field * 2 + index) * 128
-            modes_ref[:, column : column + 128] = value
-    modes_ref[:, STATE:] = jnp.broadcast_to(extra, (UNITS, 128))
-
-
-def both_modes_kernel(own_ref, beside_ref, links_ref, sent_ref, blocks, semaphores):
+            blocks[:, 0, column : column + 128] = value
+    copy = pltpu.make_async_copy(blocks, sent_ref.at[:, :, :STATE], semaphore)
+    copy.start()
+    basis_ref[:LAYER] = basis
+    basis_ref[LAYER:] = jnp.broadcast_to(extra, (8, 128))
+    copy.wait()
+
+
+def beside_modes_kernel(half_ref, basis_ref, beside_ref, links_ref, sent_ref, blocks, semaphores):
+    del half_ref
     place = lax.axis_index("space")
     places = lax.axis_size("space")
     partner = (jnp.where(((place >> 3) & 3) < 2, place - EDGE, place + EDGE) + places) % places
-    for column in range(0, STATE, 128):
-        blocks[:, 0, column : column + 128] = own_ref[:, column : column + 128]
-    first = pltpu.make_async_copy(blocks.at[:, :, :STATE], sent_ref.at[:, :, :STATE], semaphores.at[0])
-    first.start()
-    _, of_field, extra = layer_modes(beside_ref, links_ref[...], partner, places, 4)
+    copies = []
+
+    def send(first, columns):
+        part = pltpu.make_async_copy(
+            blocks.at[:, :, first : first + columns],
+            sent_ref.at[:, :, STATE + first : STATE + first + columns],
+            semaphores.at[len(copies)],
+        )
+        part.start()
+        copies.append(part)
+
+    _, modes_of, extra = layer_modes(beside_ref, links_ref[...], partner, places, 4)
     for field in range(FIELDS):
-        for index, value in enumerate(of_field(field)):
-            column = STATE + (field * 2 + index) * 128
+        for index, value in enumerate(modes_of(field)):
+            column = (field * 2 + index) * 128
             blocks[:, 0, column : column + 128] = value
-    blocks[:, 0, 2 * STATE :] = own_ref[:, STATE:] + jnp.broadcast_to(extra, (UNITS, 128))
-    second = pltpu.make_async_copy(blocks.at[:, :, STATE:], sent_ref.at[:, :, STATE:], semaphores.at[1])
-    second.start()
-    first.wait()
-    second.wait()
+        send(field * 256, 256)
+    blocks[:, 0, STATE:] = jnp.broadcast_to(basis_ref[LAYER : LAYER + 1] + extra, (UNITS, 128))
+    send(STATE, 128)
+    for copy in copies:
+        copy.wait()
 
 
 def from_modes_kernel(modes_ref, basis_ref, out_ref, fields, semaphores):
     copies = []
     unit = iota((LAYER, 128), 0) & (UNITS - 1)
     scale = jnp.where(unit < 30, 2.0 / LAYER, 1.0 / LAYER).astype(F32)
-    back = basis_ref[...] * scale
+    back = basis_ref[:LAYER] * scale
     upper = iota((LAYER, 128), 1) >= LAYER
     halved = iota((UNITS, 128), 1) >= LAYER
     for field in range(FIELDS):
@@ -170,7 +181,9 @@
 NEAR = len(SHIFTS_A) + len(SHIFTS_B)
 BLOCKS = NEAR + len(FAR_A) + len(FAR_B)
 RING = 8
-ENTRIES = 256 + FIELDS * 128
+RESTRICT = 256
+PROLONG = RESTRICT + FIELDS * 128
+ENTRIES = PROLONG + 128
 PACKED = ((0, 64, 64), (64, 64, 96), (128, 8, 8), (136, 8, 24), (144, FIELDS, FIELDS), (152, 8, 64), (160, 64, 8))
 
 
@@ -203,8 +216,6 @@
     level_ref,
     chain_high_ref,
     chain_low_ref,
-    prolong_high_ref,
-    prolong_low_ref,
     near_high_ref,
     near_low_ref,
     far_ref,
@@ -213,7 +224,6 @@
         packed_ref[first : first + rows, :columns] for first, rows, columns in PACKED
     )
     fine_ref = level_ref.at[:256]
-    restrict_all_ref = level_ref.at[256:ENTRIES]
     place = lax.axis_index("space")
     kx, ky, kx_other, ky_other, paired = wave_numbers(place & (UNITS - 1))
     single = paired == 0
@@ -313,11 +323,9 @@
     restricting = jnp.where(down, restricting, 0.0)
     prolonging = jnp.where(up, prolonging, 0.0)
     for field in range(FIELDS):
-        part = slice(field * 128, (field + 1) * 128)
-        put_packed(restrict_all_ref, part, jnp.where((wide >> 4) == field, restricting, 0.0))
-        value = jnp.where((tall >> 4) == field, prolonging, 0.0)
-        put(prolong_high_ref, prolong_low_ref, slice(0, 128), part, value)
-        prolong_high_ref[128:, part] = value.astype(BF16)
+        rows = slice(RESTRICT + field * 128, RESTRICT + (field + 1) * 128)
+        put_packed(level_ref, rows, jnp.where((wide >> 4) == field, restricting, 0.0))
+    put_packed(level_ref, slice(PROLONG, ENTRIES), prolonging)
 
     response = jnp.where(tall < 16, prolonging, 0.0)
     fine_below = (wide & 3) == 3
@@ -396,8 +404,6 @@
     level_ref,
     chain_high_ref,
     chain_low_ref,
-    prolong_high_ref,
-    prolong_low_ref,
     near_high_ref,
     near_low_ref,
     far_ref,
@@ -412,7 +418,6 @@
     ends_rate,
 ):
     fine_ref = level_ref.at[:256]
-    restrict_all_ref = level_ref.at[256:ENTRIES]
     mixing_ref[...] = (
         level_ref[ENTRIES : ENTRIES + 32, :128].astype(F32)
         + level_ref[ENTRIES : ENTRIES + 32, 128:].astype(F32)
@@ -426,6 +431,7 @@
     fine_below = (lane & 3) == 3
     coarse_below = (lane & 1) == 1
     halved = lane >= 64
+    of_field = iota((128, 128), 1) >> 4
 
     def packed_dot(value, packed):
         high, low = split(value)
@@ -452,7 +458,7 @@
         return packed_dot(jnp.concatenate(pieces, axis=0), fine_ref[...])
 
     def restrict(state):
-        return packed_dot(jnp.concatenate(fields_of(state), axis=1), restrict_all_ref[...])
+        return packed_dot(jnp.concatenate(fields_of(state), axis=1), level_ref[RESTRICT:PROLONG])
 
     def stages(states):
         wide = [
@@ -541,10 +547,8 @@
             if table[name][order] != 0.0:
                 term = table[name][order] * value
                 total = term if total is None else total + term
-        high, low = split(total)
-        wide = bdot(jnp.concatenate([high, low], axis=1), prolong_high_ref[...])
-        wide = wide + bdot(high, prolong_low_ref[...])
-        wide = jnp.concatenate([wide[:, f * 128 : (f + 1) * 128] for f in range(FIELDS)], axis=0)
+        apart = [jnp.where(of_field[: len(total)] == field, total, 0.0) for field in range(FIELDS)]
+        wide = packed_dot(jnp.concatenate(apart, axis=0), level_ref[PROLONG:ENTRIES])
         weight = jnp.where(mine > 0, table["later"][order], table["first"][order]).astype(F32)
         return wide + weight * initial_around
 
@@ -619,8 +623,6 @@
         (ENTRIES + 64, 256),
         (512, 256),
         (512, 256),
-        (256, FIELDS * 128),
-        (128, FIELDS * 128),
         (NEAR * 128, 256),
         (NEAR * 128, 256),
         (BLOCKS * 128, 256),
@@ -691,29 +693,26 @@
     state = initial.reshape(FIELDS * LAYER, -1)
     state_beside = lax.ppermute(state, ("tm", "space"), route)
     links_beside = lax.ppermute(neighbours, ("tm", "space"), route)
-    modes, basis = pl.pallas_call(
+    block_shape = jax.ShapeDtypeStruct((UNITS, 1, 2 * STATE + 128), F32)
+    half, basis = pl.pallas_call(
         own_modes_kernel,
-        out_shape=(
-            jax.ShapeDtypeStruct((UNITS, STATE + 128), F32),
-            jax.ShapeDtypeStruct((LAYER, 128), F32),
-        ),
+        out_shape=(block_shape, jax.ShapeDtypeStruct((LAYER + 8, 128), F32)),
         in_specs=[IN_VMEM] * 2,
-        out_specs=(IN_VMEM, IN_VMEM),
+        out_specs=(pl.BlockSpec(memory_space=pl.ANY), IN_VMEM),
+        scratch_shapes=[pltpu.VMEM((UNITS, 1, STATE), F32), pltpu.SemaphoreType.DMA],
         compiler_params=params,
         name="own_modes",
     )(state, neighbours)
     sent = pl.pallas_call(
-        both_modes_kernel,
-        out_shape=jax.ShapeDtypeStruct((UNITS, 1, 2 * STATE + 128), F32),
-        in_specs=[IN_VMEM] * 3,
+        beside_modes_kernel,
+        out_shape=block_shape,
+        in_specs=[pl.BlockSpec(memory_space=pl.ANY)] + [IN_VMEM] * 3,
         out_specs=pl.BlockSpec(memory_space=pl.ANY),
-        scratch_shapes=[
-            pltpu.VMEM((UNITS, 1, 2 * STATE + 128), F32),
-            pltpu.SemaphoreType.DMA((2,)),
-        ],
+        input_output_aliases={0: 0},
+        scratch_shapes=[pltpu.VMEM((UNITS, 1, STATE + 128), F32), pltpu.SemaphoreType.DMA((FIELDS + 1,))],
         compiler_params=params,
-        name="both_modes",
-    )(modes, state_beside, links_beside)
+        name="beside_modes",
+    )(half, basis, state_beside, links_beside)
     windows = [[first + i for i in range(UNITS)] for first in range(0, lax.axis_size("space"), UNITS)]
 
     def exchange(blocks):

time: 67.7 us -> 66.7 us (0.985)
  local copies, waits for them, and re-layouts: 3.92 us -> 2.34 us
  Pallas kernels: 19.9 us -> 20.7 us
    unnamed x23 -> x19, local copies, waits for them, and re-layouts: 3.92 us -> 2.34 us
    ppermute x1, waiting for transfers between devices: 2.55 us -> 1.83 us  [on_device(): links_beside = lax.ppermute(neighbours, ('tm', 'space'), route)]
    pallas_call x2, Pallas kernels: 3.2 us -> 3.91 us  [the longest x1 1.97 us: on_device(): pl.pallas_call(own_modes_kernel, out_shape=(block_shape, jax.ShapeDtypeSt...]
  transfers between devices with their start and end apart: 3 -> 3, of which waited for: 2 -> 2; matrix products, arithmetic and copies ran while one was open for 0% -> 0% of each run, Pallas kernels for 9% -> 10%
where the time goes in v5:
time: 66.7 us; the launch traced here: 66.3 us
  starting transfers between devices  21.2 us (32%)
  Pallas kernels  20.7 us (31%)
  blocking collectives  12.8 us (19%)
  waiting for transfers between devices  8.99 us (13%)
  local copies, waits for them, and re-layouts  2.34 us (4%)
    all_to_all x1, blocking collectives, exchange(): lax.all_to_all(blocks, 'space', 0, 0, axis_index_groups=windows, tiled=True)  12.8 us
    ppermute x1, starting transfers between devices, on_device(): state_beside = lax.ppermute(state, ('tm', 'space'), route)  12.4 us
    pallas_call x1, Pallas kernels, iterate_kernel_call(): pl.pallas_call(functools.partial(iterate_kernel, slices), out_shape=jax.S...  10.7 us
    all_to_all x1, waiting for transfers between devices, exchange(): lax.all_to_all(blocks, 'space', 0, 0, axis_index_groups=windows, tiled=True)  7.16 us
    all_to_all x1, starting transfers between devices, exchange(): lax.all_to_all(blocks, 'space', 0, 0, axis_index_groups=windows, tiled=True)  6.87 us
    pallas_call x1, Pallas kernels, operators_call(): pl.pallas_call(operators_kernel, out_shape=[jax.ShapeDtypeStruct(shape, B...  4.82 us
    unnamed x19, local copies, waits for them, and re-layouts  2.34 us
    pallas_call x1, Pallas kernels, on_device(): pl.pallas_call(own_modes_kernel, out_shape=(block_shape, jax.ShapeDtypeSt...  1.97 us
  transfers between devices with their start and end apart: 3, of which 2 were waited for; matrix products, arithmetic and copies ran while one was open for 0% of the time, Pallas kernels for 10%

profile of v5, /device:TPU:1, one launch (start us, length us, event | category | flops | bytes accessed | tf_op | source)
XLA Modules:
  0.0 66.3 jit_solution(14179701674812030128)
XLA Ops:
  0.0 12.4 %collective-permute-start = (f32[320,128]{1,0:T(8,128)}, f32[320,128]{1,0:T(8,128)S(1)}, u32[]{:S(2)}, u32[]{:S(2)}) collective-permute-start(f32[320,128]{1,0:T(8,128)} %bitcast.1), channel_id=1, source_target_pairs={{112,0},{113,1},{114,2},{115,3},{116,4},{117,5},{118,6},{119,7},{1... | collective-permute-start | bytes 491528 | tf_op jit(solution)/shard_map/ppermute | solution.py:694
  12.4 1.9 %collective-permute-start.1 = (s32[6,128]{1,0:T(8,128)}, s32[6,128]{1,0:T(8,128)S(1)}, u32[]{:S(2)}, u32[]{:S(2)}) collective-permute-start(s32[6,128]{1,0:T(8,128)} %links_ref.1), channel_id=1, source_target_pairs={{112,0},{113,1},{114,2},{115,3},{116,4},{117,5},{118,6},{119,7},{1... | collective-permute-start | bytes 9224 | tf_op jit(solution)/shard_map/ppermute | solution.py:695
  14.3 0.0 copy-start
  14.3 0.9 %copy-done = f32[5,64,128]{2,1,0:T(8,128)S(1)} copy-done((f32[5,64,128]{2,1,0:T(8,128)S(1)}, f32[5,64,128]{2,1,0:T(8,128)}, u32[]{:S(2)}) %copy-start) | copy-done | bytes 163864
  15.2 0.0 copy-start.1
  15.2 0.7 %copy-done.1 = s32[6,128]{1,0:T(8,128)S(1)} copy-done((s32[6,128]{1,0:T(8,128)S(1)}, s32[6,128]{1,0:T(8,128)}, u32[]{:S(2)}) %copy-start.1) | copy-done | bytes 3096
  15.9 2.0 %own_modes.1 = (f32[32,1,2688]{2,1,0:T(1,128)}, f32[72,128]{1,0:T(8,128)S(1)}) custom-call(f32[320,128]{1,0:T(8,128)S(1)} %bitcast.2, s32[6,128]{1,0:T(8,128)S(1)} %copy-done.1), custom_call_target="tpu_custom_call" | custom-call | tf_op jit(solution)/shard_map/own_modes/pallas_call | solution.py:697
  17.9 1.8 %collective-permute-done.1.links_ref = s32[6,128]{1,0:T(8,128)S(1)} collective-permute-done((s32[6,128]{1,0:T(8,128)}, s32[6,128]{1,0:T(8,128)S(1)}, u32[]{:S(2)}, u32[]{:S(2)}) %collective-permute-start.1) | collective-permute-done | bytes 3104 | tf_op jit(solution)/shard_map/ppermute | solution.py:695
  19.7 0.0 collective-permute-done.beside_ref
  19.7 1.9 %beside_modes.1 = f32[32,1,2688]{2,1,0:T(1,128)} custom-call(f32[32,1,2688]{2,1,0:T(1,128)} %get-tuple-element.13.half_ref, f32[72,128]{1,0:T(8,128)S(1)} %get-tuple-element.14.basis_ref, f32[320,128]{1,0:T(8,128)S(1)} %collective-permute-done.beside_ref, s32[6,128]{1,0:T(8,128)S(1)} %collective-permute-done.1.links_ref), custom_call_target="tpu_custom_call", output_to_operand_aliasing={{}: (0, {})} | custom-call | tf_op jit(solution)/shard_map/beside_modes/pallas_call | solution.py:706
  21.7 0.0 copy-start.8
  21.7 0.0 copy-start.3
  21.7 0.0 copy-start.5
  21.7 0.0 copy-start.6
  21.7 0.0 copy-start.7
  21.8 6.9 %all-to-all-start = ((f32[32,1,2688]{2,1,0:T(1,128)}), f32[32,1,2688]{2,1,0:T(1,128)S(1)}, u32[]{:S(2)}, u32[]{:S(2)}) async-start(f32[32,1,2688]{2,1,0:T(1,128)} %beside_modes.1), calls=%async_computation | async-start | bytes 688128 | tf_op jit(solution)/shard_map/all_to_all | solution.py:719
  28.6 0.0 copy-done.8
  28.6 0.0 copy-start.2
  28.7 0.0 copy-start.4
  28.7 0.1 copy.11
  28.7 0.0 copy-done.3
  28.8 0.0 copy-done.5
  28.8 0.0 copy-done.6
  28.8 0.0 copy-done.7
  28.8 0.6 copy-done.2
  29.4 0.0 copy-done.4
  29.4 4.8 %operators.1 = (bf16[1088,256]{1,0:T(8,128)(2,1)S(1)}, bf16[512,256]{1,0:T(8,128)(2,1)S(1)}, bf16[512,256]{1,0:T(8,128)(2,1)S(1)}, bf16[1024,256]{1,0:T(8,128)(2...) custom-call(f32[224,128]{1,0:T(8,128)S(1)} %pad_add_fusion.packed_ref), custom_call_target="tpu_custom_call" | custom-call | flops 100000000 | bytes 3000000 | tf_op jit(solution)/shard_map/operators/pallas_call | solution.py:634
  34.2 7.2 %all-to-all-done.received_ref = f32[32,1,2688]{2,1,0:T(1,128)S(1)} async-done(((f32[32,1,2688]{2,1,0:T(1,128)}), f32[32,1,2688]{2,1,0:T(1,128)S(1)}, u32[]{:S(2)}, u32[]{:S(2)}) %all-to-all-start) | async-done | bytes 344096 | tf_op jit(solution)/shard_map/all_to_all | solution.py:719
  41.4 10.7 %iterate.1 = f32[32,1,1280]{2,1,0:T(1,128)S(1)} custom-call(f32[32,1,2688]{2,1,0:T(1,128)S(1)} %all-to-all-done.received_ref, bf16[1088,256]{1,0:T(8,128)(2,1)S(1)} %get-tuple-element.15.level_ref, bf16[512,256]{1,0:T(8,128)(2,1)S(1)} %get-tuple-element.16.chain_high_ref, bf16[512,256]{1,0:T(8,128)(2,1)S(1)} %get-tuple-element.17.chain_low_ref, ...), custom_call_target="tpu_custom_call" | custom-call | tf_op jit(solution)/shard_map/iterate/pallas_call | solution.py:647
  52.1 12.8 %all_to_all.10.modes_ref = f32[32,1,1280]{2,1,0:T(1,128)S(1)} all-to-all(f32[32,1,1280]{2,1,0:T(1,128)S(1)} %iterate.1), channel_id=1, replica_groups={{0,1,2,3,4,5,6,7,8,9,10,11,12,13,14,15,16,17,18,19,20,21,22,23,24,25,26..., dimensions={0} | all-to-all | bytes 327680 | tf_op jit(solution)/shard_map/all_to_all | solution.py:719
  64.9 1.3 %from_modes.1 = f32[1,5,64,128]{3,2,1,0:T(8,128)} custom-call(f32[32,1,1280]{2,1,0:T(1,128)S(1)} %all_to_all.10.modes_ref, f32[72,128]{1,0:T(8,128)S(1)} %get-tuple-element.14.basis_ref), custom_call_target="tpu_custom_call" | custom-call | tf_op jit(solution)/shard_map/from_modes/pallas_call | solution.py:727
  (1 shorter events, 0.0 us)
Async XLA Ops:
  0.0 19.7 %collective-permute-start = (f32[320,128]{1,0:T(8,128)}, f32[320,128]{1,0:T(8,128)S(1)}, u32[]{:S(2)}, u32[]{:S(2)}) collective-permute-start(f32[320,128]{1,0:T(8,128)} %bitcast.1), channel_id=1, source_target_pairs={{112,0},{113,1},{114,2},{115,3},{116,4},{117,5},{118,6},{119,7},{1... | collective-permute-start | bytes 491528 | tf_op jit(solution)/shard_map/ppermute | solution.py:694
  12.4 7.3 %collective-permute-start.1 = (s32[6,128]{1,0:T(8,128)}, s32[6,128]{1,0:T(8,128)S(1)}, u32[]{:S(2)}, u32[]{:S(2)}) collective-permute-start(s32[6,128]{1,0:T(8,128)} %links_ref.1), channel_id=1, source_target_pairs={{112,0},{113,1},{114,2},{115,3},{116,4},{117,5},{118,6},{119,7},{1... | collective-permute-start | bytes 9224 | tf_op jit(solution)/shard_map/ppermute | solution.py:695
  14.3 0.9 %copy-start = (f32[5,64,128]{2,1,0:T(8,128)S(1)}, f32[5,64,128]{2,1,0:T(8,128)}, u32[]{:S(2)}) copy-start(f32[5,64,128]{2,1,0:T(8,128)} %param.9) | copy-start | bytes 491524
  15.2 0.7 %copy-start.1 = (s32[6,128]{1,0:T(8,128)S(1)}, s32[6,128]{1,0:T(8,128)}, u32[]{:S(2)}) copy-start(s32[6,128]{1,0:T(8,128)} %links_ref.1) | copy-start | bytes 9220
  21.7 6.9 %copy-start.8 = (f32[64,8]{0,1:T(8,128)S(1)}, f32[64,8]{0,1:T(8,128)}, u32[]{:S(2)}) copy-start(f32[64,8]{0,1:T(8,128)} %param.17) | copy-start | bytes 6148
  21.7 7.0 %copy-start.3 = (f32[64,64]{1,0:T(8,128)S(1)}, f32[64,64]{1,0:T(8,128)}, u32[]{:S(2)}) copy-start(f32[64,64]{1,0:T(8,128)} %param.11) | copy-start | bytes 49156
  21.7 7.0 %copy-start.5 = (f32[5,5]{1,0:T(8,128)S(1)}, f32[5,5]{1,0:T(8,128)}, u32[]{:S(2)}) copy-start(f32[5,5]{1,0:T(8,128)} %param.15) | copy-start | bytes 304
  21.7 7.0 %copy-start.6 = (f32[8,24]{1,0:T(8,128)S(1)}, f32[8,24]{1,0:T(8,128)}, u32[]{:S(2)}) copy-start(f32[8,24]{1,0:T(8,128)} %param.14) | copy-start | bytes 2308
  21.7 7.0 %copy-start.7 = (f32[8,8]{1,0:T(8,128)S(1)}, f32[8,8]{1,0:T(8,128)}, u32[]{:S(2)}) copy-start(f32[8,8]{1,0:T(8,128)} %param.13) | copy-start | bytes 772
  21.8 19.7 %all-to-all-start = ((f32[32,1,2688]{2,1,0:T(1,128)}), f32[32,1,2688]{2,1,0:T(1,128)S(1)}, u32[]{:S(2)}, u32[]{:S(2)}) async-start(f32[32,1,2688]{2,1,0:T(1,128)} %beside_modes.1), calls=%async_computation | async-start | bytes 688128 | tf_op jit(solution)/shard_map/all_to_all | solution.py:719
  28.6 0.8 %copy-start.2 = (f32[64,96]{1,0:T(8,128)S(1)}, f32[64,96]{1,0:T(8,128)}, u32[]{:S(2)}) copy-start(f32[64,96]{1,0:T(8,128)} %param.12) | copy-start | bytes 73732
  28.7 0.8 %copy-start.4 = (f32[8,64]{1,0:T(8,128)S(1)}, f32[8,64]{1,0:T(8,128)}, u32[]{:S(2)}) copy-start(f32[8,64]{1,0:T(8,128)} %param.16) | copy-start | bytes 6148

commit v6 on v5

--- a/solution.py
+++ b/solution.py
@@ -36,6 +36,11 @@
 
 def nt3(a, b):
     dims = (((1,), (1,)), ((), ()))
+    return lax.dot_general(a, b, dims, precision=lax.Precision.HIGH, preferred_element_type=F32)
+
+
+def nn3(a, b):
+    dims = (((1,), (0,)), ((), ()))
     return lax.dot_general(a, b, dims, precision=lax.Precision.HIGH, preferred_element_type=F32)
 
 
@@ -166,7 +171,7 @@
         odd = modes_ref[:, 0, column + 128 : column + 256]
         real = jnp.where(halved, pltpu.roll(odd, 64, 1), even)
         imaginary = jnp.where(halved, odd, pltpu.roll(even, 64, 1))
-        whole = nn(jnp.transpose(jnp.concatenate([real, imaginary], axis=0)), back)
+        whole = nn3(jnp.transpose(jnp.concatenate([real, imaginary], axis=0)), back)
         fields[field] = jnp.where(upper, whole[LAYER:], whole[:LAYER])
         copies.append(pltpu.make_async_copy(fields.at[field], out_ref.at[0, field], semaphores.at[field]))
         copies[-1].start()
@@ -564,6 +569,9 @@
             integral = (last + 4.0 * (ready[1] + mid_rate_start) + next_last) * (1.0 / 3.0)
             later_defect = integral - old_rate
             states += [tail, later_rate + later_defect]
+        if step < 2:
+            power = psi(power)
+            power_coarse.append(restrict(power))
         found = stages(states)
         if ready is not None:
             (tail_rate, tail_twice), (once, half_twice) = found[-2:]
@@ -590,9 +598,6 @@
             }
             state = added(4)
             state = psi(state) + added(3)
-        if step < 2:
-            power = psi(power)
-            power_coarse.append(restrict(power))
         if step == 1:
             end_start = power_coarse[0] + 2.0 * power_coarse[1] + power_coarse[2]
             mid_rate_start = power_coarse[1] + power_coarse[2]

time: 66.7 us -> 66.6 us (level)
  no operation moved by 1% of the time
where the time goes in v6:
time: 66.6 us; the launch traced here: 66.1 us
  starting transfers between devices  21.2 us (32%)
  Pallas kernels  20.5 us (31%)
  blocking collectives  12.8 us (19%)
  waiting for transfers between devices  8.99 us (13%)
  local copies, waits for them, and re-layouts  2.34 us (4%)
    all_to_all x1, blocking collectives, exchange(): lax.all_to_all(blocks, 'space', 0, 0, axis_index_groups=windows, tiled=True)  12.8 us
    ppermute x1, starting transfers between devices, on_device(): state_beside = lax.ppermute(state, ('tm', 'space'), route)  12.4 us
    pallas_call x1, Pallas kernels, iterate_kernel_call(): pl.pallas_call(functools.partial(iterate_kernel, slices), out_shape=jax.S...  10.6 us
    all_to_all x1, waiting for transfers between devices, exchange(): lax.all_to_all(blocks, 'space', 0, 0, axis_index_groups=windows, tiled=True)  7.16 us
    all_to_all x1, starting transfers between devices, exchange(): lax.all_to_all(blocks, 'space', 0, 0, axis_index_groups=windows, tiled=True)  6.87 us
    pallas_call x1, Pallas kernels, operators_call(): pl.pallas_call(operators_kernel, out_shape=[jax.ShapeDtypeStruct(shape, B...  4.82 us
    unnamed x19, local copies, waits for them, and re-layouts  2.34 us
    pallas_call x1, Pallas kernels, on_device(): pl.pallas_call(own_modes_kernel, out_shape=(block_shape, jax.ShapeDtypeSt...  1.97 us
  transfers between devices with their start and end apart: 3, of which 2 were waited for; matrix products, arithmetic and copies ran while one was open for 0% of the time, Pallas kernels for 10%

profile of v6, /device:TPU:1, one launch (start us, length us, event | category | flops | bytes accessed | tf_op | source)
XLA Modules:
  0.0 66.1 jit_solution(8677179458457945891)
XLA Ops:
  0.0 12.4 %collective-permute-start = (f32[320,128]{1,0:T(8,128)}, f32[320,128]{1,0:T(8,128)S(1)}, u32[]{:S(2)}, u32[]{:S(2)}) collective-permute-start(f32[320,128]{1,0:T(8,128)} %bitcast.1), channel_id=1, source_target_pairs={{112,0},{113,1},{114,2},{115,3},{116,4},{117,5},{118,6},{119,7},{1... | collective-permute-start | bytes 491528 | tf_op jit(solution)/shard_map/ppermute | solution.py:699
  12.4 1.9 %collective-permute-start.1 = (s32[6,128]{1,0:T(8,128)}, s32[6,128]{1,0:T(8,128)S(1)}, u32[]{:S(2)}, u32[]{:S(2)}) collective-permute-start(s32[6,128]{1,0:T(8,128)} %links_ref.1), channel_id=1, source_target_pairs={{112,0},{113,1},{114,2},{115,3},{116,4},{117,5},{118,6},{119,7},{1... | collective-permute-start | bytes 9224 | tf_op jit(solution)/shard_map/ppermute | solution.py:700
  14.3 0.0 copy-start
  14.3 0.9 %copy-done = f32[5,64,128]{2,1,0:T(8,128)S(1)} copy-done((f32[5,64,128]{2,1,0:T(8,128)S(1)}, f32[5,64,128]{2,1,0:T(8,128)}, u32[]{:S(2)}) %copy-start) | copy-done | bytes 163864
  15.2 0.0 copy-start.1
  15.2 0.7 %copy-done.1 = s32[6,128]{1,0:T(8,128)S(1)} copy-done((s32[6,128]{1,0:T(8,128)S(1)}, s32[6,128]{1,0:T(8,128)}, u32[]{:S(2)}) %copy-start.1) | copy-done | bytes 3096
  15.9 2.0 %own_modes.1 = (f32[32,1,2688]{2,1,0:T(1,128)}, f32[72,128]{1,0:T(8,128)S(1)}) custom-call(f32[320,128]{1,0:T(8,128)S(1)} %bitcast.2, s32[6,128]{1,0:T(8,128)S(1)} %copy-done.1), custom_call_target="tpu_custom_call" | custom-call | tf_op jit(solution)/shard_map/own_modes/pallas_call | solution.py:702
  17.9 1.8 %collective-permute-done.1.links_ref = s32[6,128]{1,0:T(8,128)S(1)} collective-permute-done((s32[6,128]{1,0:T(8,128)}, s32[6,128]{1,0:T(8,128)S(1)}, u32[]{:S(2)}, u32[]{:S(2)}) %collective-permute-start.1) | collective-permute-done | bytes 3104 | tf_op jit(solution)/shard_map/ppermute | solution.py:700
  19.7 0.0 collective-permute-done.beside_ref
  19.7 1.9 %beside_modes.1 = f32[32,1,2688]{2,1,0:T(1,128)} custom-call(f32[32,1,2688]{2,1,0:T(1,128)} %get-tuple-element.13.half_ref, f32[72,128]{1,0:T(8,128)S(1)} %get-tuple-element.14.basis_ref, f32[320,128]{1,0:T(8,128)S(1)} %collective-permute-done.beside_ref, s32[6,128]{1,0:T(8,128)S(1)} %collective-permute-done.1.links_ref), custom_call_target="tpu_custom_call", output_to_operand_aliasing={{}: (0, {})} | custom-call | tf_op jit(solution)/shard_map/beside_modes/pallas_call | solution.py:711
  21.7 0.0 copy-start.8
  21.7 0.0 copy-start.3
  21.7 0.0 copy-start.5
  21.7 0.0 copy-start.6
  21.7 0.0 copy-start.7
  21.8 6.9 %all-to-all-start = ((f32[32,1,2688]{2,1,0:T(1,128)}), f32[32,1,2688]{2,1,0:T(1,128)S(1)}, u32[]{:S(2)}, u32[]{:S(2)}) async-start(f32[32,1,2688]{2,1,0:T(1,128)} %beside_modes.1), calls=%async_computation | async-start | bytes 688128 | tf_op jit(solution)/shard_map/all_to_all | solution.py:724
  28.6 0.0 copy-done.8
  28.6 0.0 copy-start.2
  28.7 0.0 copy-start.4
  28.7 0.1 copy.11
  28.7 0.0 copy-done.3
  28.8 0.0 copy-done.5
  28.8 0.0 copy-done.6
  28.8 0.0 copy-done.7
  28.8 0.6 copy-done.2
  29.4 0.0 copy-done.4
  29.4 4.8 %operators.1 = (bf16[1088,256]{1,0:T(8,128)(2,1)S(1)}, bf16[512,256]{1,0:T(8,128)(2,1)S(1)}, bf16[512,256]{1,0:T(8,128)(2,1)S(1)}, bf16[1024,256]{1,0:T(8,128)(2...) custom-call(f32[224,128]{1,0:T(8,128)S(1)} %pad_add_fusion.packed_ref), custom_call_target="tpu_custom_call" | custom-call | flops 100000000 | bytes 3000000 | tf_op jit(solution)/shard_map/operators/pallas_call | solution.py:639
  34.2 7.2 %all-to-all-done.received_ref = f32[32,1,2688]{2,1,0:T(1,128)S(1)} async-done(((f32[32,1,2688]{2,1,0:T(1,128)}), f32[32,1,2688]{2,1,0:T(1,128)S(1)}, u32[]{:S(2)}, u32[]{:S(2)}) %all-to-all-start) | async-done | bytes 344096 | tf_op jit(solution)/shard_map/all_to_all | solution.py:724
  41.4 10.6 %iterate.1 = f32[32,1,1280]{2,1,0:T(1,128)S(1)} custom-call(f32[32,1,2688]{2,1,0:T(1,128)S(1)} %all-to-all-done.received_ref, bf16[1088,256]{1,0:T(8,128)(2,1)S(1)} %get-tuple-element.15.level_ref, bf16[512,256]{1,0:T(8,128)(2,1)S(1)} %get-tuple-element.16.chain_high_ref, bf16[512,256]{1,0:T(8,128)(2,1)S(1)} %get-tuple-element.17.chain_low_ref, ...), custom_call_target="tpu_custom_call" | custom-call | tf_op jit(solution)/shard_map/iterate/pallas_call | solution.py:652
  52.1 12.8 %all_to_all.10.modes_ref = f32[32,1,1280]{2,1,0:T(1,128)S(1)} all-to-all(f32[32,1,1280]{2,1,0:T(1,128)S(1)} %iterate.1), channel_id=1, replica_groups={{0,1,2,3,4,5,6,7,8,9,10,11,12,13,14,15,16,17,18,19,20,21,22,23,24,25,26..., dimensions={0} | all-to-all | bytes 327680 | tf_op jit(solution)/shard_map/all_to_all | solution.py:724
  64.8 1.2 %from_modes.1 = f32[1,5,64,128]{3,2,1,0:T(8,128)} custom-call(f32[32,1,1280]{2,1,0:T(1,128)S(1)} %all_to_all.10.modes_ref, f32[72,128]{1,0:T(8,128)S(1)} %get-tuple-element.14.basis_ref), custom_call_target="tpu_custom_call" | custom-call | tf_op jit(solution)/shard_map/from_modes/pallas_call | solution.py:732
  (1 shorter events, 0.0 us)
Async XLA Ops:
  0.0 19.7 %collective-permute-start = (f32[320,128]{1,0:T(8,128)}, f32[320,128]{1,0:T(8,128)S(1)}, u32[]{:S(2)}, u32[]{:S(2)}) collective-permute-start(f32[320,128]{1,0:T(8,128)} %bitcast.1), channel_id=1, source_target_pairs={{112,0},{113,1},{114,2},{115,3},{116,4},{117,5},{118,6},{119,7},{1... | collective-permute-start | bytes 491528 | tf_op jit(solution)/shard_map/ppermute | solution.py:699
  12.4 7.3 %collective-permute-start.1 = (s32[6,128]{1,0:T(8,128)}, s32[6,128]{1,0:T(8,128)S(1)}, u32[]{:S(2)}, u32[]{:S(2)}) collective-permute-start(s32[6,128]{1,0:T(8,128)} %links_ref.1), channel_id=1, source_target_pairs={{112,0},{113,1},{114,2},{115,3},{116,4},{117,5},{118,6},{119,7},{1... | collective-permute-start | bytes 9224 | tf_op jit(solution)/shard_map/ppermute | solution.py:700
  14.3 0.9 %copy-start = (f32[5,64,128]{2,1,0:T(8,128)S(1)}, f32[5,64,128]{2,1,0:T(8,128)}, u32[]{:S(2)}) copy-start(f32[5,64,128]{2,1,0:T(8,128)} %param.9) | copy-start | bytes 491524
  15.2 0.7 %copy-start.1 = (s32[6,128]{1,0:T(8,128)S(1)}, s32[6,128]{1,0:T(8,128)}, u32[]{:S(2)}) copy-start(s32[6,128]{1,0:T(8,128)} %links_ref.1) | copy-start | bytes 9220
  21.7 6.9 %copy-start.8 = (f32[64,8]{0,1:T(8,128)S(1)}, f32[64,8]{0,1:T(8,128)}, u32[]{:S(2)}) copy-start(f32[64,8]{0,1:T(8,128)} %param.17) | copy-start | bytes 6148
  21.7 7.0 %copy-start.3 = (f32[64,64]{1,0:T(8,128)S(1)}, f32[64,64]{1,0:T(8,128)}, u32[]{:S(2)}) copy-start(f32[64,64]{1,0:T(8,128)} %param.11) | copy-start | bytes 49156
  21.7 7.0 %copy-start.5 = (f32[5,5]{1,0:T(8,128)S(1)}, f32[5,5]{1,0:T(8,128)}, u32[]{:S(2)}) copy-start(f32[5,5]{1,0:T(8,128)} %param.15) | copy-start | bytes 304
  21.7 7.0 %copy-start.6 = (f32[8,24]{1,0:T(8,128)S(1)}, f32[8,24]{1,0:T(8,128)}, u32[]{:S(2)}) copy-start(f32[8,24]{1,0:T(8,128)} %param.14) | copy-start | bytes 2308
  21.7 7.0 %copy-start.7 = (f32[8,8]{1,0:T(8,128)S(1)}, f32[8,8]{1,0:T(8,128)}, u32[]{:S(2)}) copy-start(f32[8,8]{1,0:T(8,128)} %param.13) | copy-start | bytes 772
  21.8 19.7 %all-to-all-start = ((f32[32,1,2688]{2,1,0:T(1,128)}), f32[32,1,2688]{2,1,0:T(1,128)S(1)}, u32[]{:S(2)}, u32[]{:S(2)}) async-start(f32[32,1,2688]{2,1,0:T(1,128)} %beside_modes.1), calls=%async_computation | async-start | bytes 688128 | tf_op jit(solution)/shard_map/all_to_all | solution.py:724
  28.6 0.8 %copy-start.2 = (f32[64,96]{1,0:T(8,128)S(1)}, f32[64,96]{1,0:T(8,128)}, u32[]{:S(2)}) copy-start(f32[64,96]{1,0:T(8,128)} %param.12) | copy-start | bytes 73732
  28.7 0.8 %copy-start.4 = (f32[8,64]{1,0:T(8,128)S(1)}, f32[8,64]{1,0:T(8,128)}, u32[]{:S(2)}) copy-start(f32[8,64]{1,0:T(8,128)} %param.16) | copy-start | bytes 6148
